TPU v7x, 512 devices: a whole 4x4x16 slice. The times are simulated.
512 devices in a mesh: row: 16 (over y, z_hi, core), col: 32 (over z_lo, x).
Axes of the slice: x: 4, y: 4, z: 16 (z_hi: 2, z_lo: 8; z = z_hi * 8 + z_lo), core: 2. Of those that a mesh axis runs over, the one named last changes fastest.
Arguments:
- acts: bfloat16 [1024, 12288], P('col', 'row'), may hold values from -6 to 6
- weight: bfloat16 [12288, 24576], P('row', 'col'), may hold values from -0.0546875 to 0.0546875
- cotangent: bfloat16 [1024, 24576], P('row', 'col'), may hold values from -6 to 6
Outputs:
- output: bfloat16 [1024, 24576], P('row', 'col')
- acts_grad: bfloat16 [1024, 12288], P('col', 'row')
- weight_grad: bfloat16 [12288, 24576], P('row', 'col')
All inputs are finite; a program needn't handle non-finite values.
Results may differ from a plain program's by a relative error of at most 0.0049.
Values may be sent and summed in bfloat16 or wider, within the bound.
No kernel may reach another device: no remote copies, remote signals or barrier semaphores. Data moves between devices by JAX's collectives and lax.ppermute only.
A program may use at most 64 MiB of HBM per device.

v0:
```python
import math

import jax
import jax.numpy as jnp
from jax import lax
from jax.sharding import PartitionSpec as P


def gelu_value(pre):
    return 0.5 * pre * (1.0 + lax.erf(pre / math.sqrt(2.0)))


def gelu_slope(pre):
    return 0.5 * (1.0 + lax.erf(pre / math.sqrt(2.0))) + pre * jnp.exp(
        -0.5 * pre * pre
    ) / math.sqrt(2.0 * math.pi)


def shards(acts, weight, cotangent):
    acts_full = lax.all_gather(acts, "col", axis=0, tiled=True)
    block = acts_full
    pre = lax.psum_scatter(
        jnp.dot(block, weight, preferred_element_type=jnp.float32),
        "row",
        scatter_dimension=0,
        tiled=True,
    )
    output = gelu_value(pre).astype(jnp.bfloat16)
    grad_tile = (cotangent.astype(jnp.float32) * gelu_slope(pre)).astype(jnp.bfloat16)
    grad_full = lax.all_gather(grad_tile, "row", axis=0, tiled=True)
    block = grad_full
    acts_grad = lax.psum_scatter(
        lax.dot_general(
            block, weight, (((1,), (1,)), ((), ())), preferred_element_type=jnp.float32
        ),
        "col",
        scatter_dimension=0,
        tiled=True,
    ).astype(jnp.bfloat16)
    token_count = grad_full.shape[0]
    weight_sum = lax.dot_general(
        acts_full, grad_full, (((0,), (0,)), ((), ())), preferred_element_type=jnp.float32
    )
    weight_grad = (weight_sum * token_count ** (-0.5)).astype(jnp.bfloat16)
    return (output, acts_grad, weight_grad)


def solution(mesh):
    in_specs = (P("col", "row"), P("row", "col"), P("row", "col"))
    out_specs = (P("row", "col"), P("col", "row"), P("row", "col"))
    return jax.shard_map(shards, mesh=mesh, in_specs=in_specs, out_specs=out_specs, check_vma=False)
```

profile of v0, /device:TPU:16, one launch (start us, length us, event | category | flops | bytes accessed | tf_op | source)
XLA Modules:
  0.0 707.3 jit_solution(14044830862657095291)
XLA Ops:
  7.2 0.0 copy-start
  7.2 0.0 all-gather.3.cloned.1.call-start
  7.2 0.7 all-gather.3.cloned.1.call-update
  7.9 0.0 reduce-scatter.3.cloned.1.call-start
  8.0 229.6 %all-gather.3.cloned.1.call-done = bf16[1024,768]{1,0:T(8,128)(2,1)} async-done(((bf16[32,768]{1,0:T(8,128)(2,1)}), bf16[1024,768]{1,0:T(8,128)(2,1)}) %all-gather.3.cloned.1.call-update) | async-done | bytes 1572880 | tf_op jit(solution)/shard_map/all_gather | solution.py:20
  237.5 0.0 copy-done
  237.6 4.4 fusion.7
  242.0 0.0 copy-start.1
  242.0 0.0 reduce-scatter.3.cloned.1.call-update
  242.0 0.0 all-gather.5.cloned.1.call-start
  242.1 134.9 %reduce-scatter.3.cloned.1.call-done = f32[64,768]{1,0:T(8,128)} async-done(((f32[1024,768]{1,0:T(8,128)}), f32[64,768]{1,0:T(8,128)}) %reduce-scatter.3.cloned.1.call-update) | async-done | bytes 196624 | tf_op jit(solution)/shard_map/reduce_scatter | solution.py:22
  376.9 0.0 copy-done.1
  376.9 1.7 fusion.6
  378.6 0.0 all-gather.5.cloned.1.call-update
  378.7 0.0 reduce-scatter.5.cloned.1.call-start
  378.7 77.9 %all-gather.5.cloned.1.call-done = bf16[1024,768]{1,0:T(8,128)(2,1)} async-done(((bf16[64,768]{1,0:T(8,128)(2,1)}), bf16[1024,768]{1,0:T(8,128)(2,1)}) %all-gather.5.cloned.1.call-update) | async-done | bytes 1572880 | tf_op jit(solution)/shard_map/all_gather | solution.py:30
  456.6 4.5 fusion.8
  461.0 0.0 reduce-scatter.5.cloned.1.call-update
  461.0 3.3 fusion
  464.4 1.5 copy.6
  465.8 233.4 %reduce-scatter.5.cloned.1.call-done = f32[32,768]{1,0:T(8,128)} async-done(((f32[1024,768]{1,0:T(8,128)}), f32[32,768]{1,0:T(8,128)}) %reduce-scatter.5.cloned.1.call-update) | async-done | bytes 98320 | tf_op jit(solution)/shard_map/reduce_scatter | solution.py:32
  699.2 1.5 convert_element_type.21
Async XLA Ops:
  7.2 230.4 %copy-start = (bf16[768,768]{1,0:T(8,128)(2,1)S(1)}, bf16[768,768]{1,0:T(8,128)(2,1)}, u32[]{:S(2)}) copy-start(bf16[768,768]{1,0:T(8,128)(2,1)} %param.4) | copy-start | bytes 3538948
  7.2 230.4 %all-gather.3.cloned.1.call-start = ((), (), s32[]{:S(2)}) async-start(), calls=%async_computation.2 | async-start | bytes 1622016 | tf_op jit(solution)/shard_map/all_gather | solution.py:20
  7.9 369.0 %reduce-scatter.3.cloned.1.call-start = ((), (), s32[]{:S(2)}) async-start(), calls=%async_computation.3 | async-start | bytes 3342336 | tf_op jit(solution)/shard_map/reduce_scatter | solution.py:22
  242.0 134.9 %copy-start.1 = (bf16[64,768]{1,0:T(8,128)(2,1)S(1)}, bf16[64,768]{1,0:T(8,128)(2,1)}, u32[]{:S(2)}) copy-start(bf16[64,768]{1,0:T(8,128)(2,1)} %param.5) | copy-start | bytes 294916
  242.0 214.6 %all-gather.5.cloned.1.call-start = ((), (), s32[]{:S(2)}) async-start(), calls=%async_computation.4 | async-start | bytes 1671168 | tf_op jit(solution)/shard_map/all_gather | solution.py:30
  378.7 320.5 %reduce-scatter.5.cloned.1.call-start = ((), (), s32[]{:S(2)}) async-start(), calls=%async_computation.5 | async-start | bytes 3244032 | tf_op jit(solution)/shard_map/reduce_scatter | solution.py:32
Sparse Core Ops, SparseCore 0:
  10.1 227.4 all-gather.2
  242.4 134.4 reduce-scatter.2
  380.8 75.7 all-gather.4
  461.2 237.9 reduce-scatter.4
where the time goes:
time: 707 us
  waiting for transfers between devices  676 us (96%)
  between operations  13.8 us (2%)
  matrix products  12.2 us (2%)
    reduce_scatter x1, waiting for transfers between devices, shards(): lax.psum_scatter(lax.dot_general(block, weight, (((1,), (1,)), ((), ())),...  233 us
    all_gather x1, waiting for transfers between devices, shards(): acts_full = lax.all_gather(acts, 'col', axis=0, tiled=True)  230 us
    reduce_scatter x1, waiting for transfers between devices, shards(): lax.psum_scatter(jnp.dot(block, weight, preferred_element_type=jnp.float3...  135 us
    all_gather x1, waiting for transfers between devices, shards(): grad_full = lax.all_gather(grad_tile, 'row', axis=0, tiled=True)  77.9 us
  transfers between devices with their start and end apart: 4, of which 4 were waited for; matrix products, arithmetic and copies ran while one was open for 1% of the time, Pallas kernels for 0%

commit v1 on v0

v1 whole, which is shorter than its diff:
```python
import functools
import math

import jax
import jax.numpy as jnp
from jax import lax
from jax.experimental import pallas as pl
from jax.experimental.pallas import tpu as pltpu
from jax.sharding import PartitionSpec as P

ROWS, COLS = 16, 32
F32, BF16 = jnp.float32, jnp.bfloat16


def gelu_value(pre):
    return 0.5 * pre * (1.0 + lax.erf(pre / math.sqrt(2.0)))


def gelu_slope(pre):
    return 0.5 * (1.0 + lax.erf(pre / math.sqrt(2.0))) + pre * jnp.exp(
        -0.5 * pre * pre
    ) / math.sqrt(2.0 * math.pi)


def swap(value, axis, mask):
    size = ROWS if axis == "row" else COLS
    return lax.ppermute(value, axis, [(i, i ^ mask) for i in range(size)])


def row_place(block, me_row):
    rel = (block >> 1) ^ me_row
    y, zh, c = rel >> 2, (rel >> 1) & 1, rel & 1
    return ((c * 4 + y) * 2 + zh) * 2 + (block & 1)


def up_kernel(me, own, x1, x2, x3, w, send, keep, acts):
    me_row, me_col = me[0], me[1]
    part = own.shape[0] // 8
    for kx, piece in enumerate((own, x1, x2, x3)):
        for k in range(4):
            for j in range(2):
                block = me_col ^ (kx + 4 * k + 16 * j)
                to = pl.multiple_of(row_place(block, me_row) * part, part)
                acts[pl.ds(to, part), :] = piece[pl.ds((k * 2 + j) * part, part), :]
    half = acts.shape[0] // 2
    step = half // 2
    for i in range(2):
        rows = pl.ds(i * step, step)
        send[rows, :] = jnp.dot(
            acts[pl.ds(half + i * step, step), :], w[...], preferred_element_type=F32
        ).astype(BF16)
    for i in range(2):
        rows = pl.ds(i * step, step)
        keep[rows, :] = jnp.dot(acts[rows, :], w[...], preferred_element_type=F32)


def down_kernel(me, g0, g1, w, own, x1, x2, x3, held):
    me_row, me_col = me[0], me[1]
    part = own.shape[0] // 8
    for c, piece in enumerate((g0, g1)):
        for m in range(4):
            for h in range(2):
                rel = m * 4 + h * 2 + c
                for lo in range(2):
                    block = ((rel ^ me_row) * 2 + lo) ^ me_col
                    x, k, j = block & 3, (block >> 2) & 3, block >> 4
                    to = pl.multiple_of(((x * 4 + k) * 2 + j) * part, part)
                    held[pl.ds(to, part), :] = piece[
                        pl.ds(((m * 2 + h) * 2 + lo) * part, part), :
                    ]
    size = own.shape[0]
    for kx, out in ((2, x2), (1, x1), (3, x3), (0, own)):
        value = lax.dot_general(
            held[pl.ds(kx * size, size), :],
            w[...],
            (((1,), (1,)), ((), ())),
            preferred_element_type=F32,
        )
        out[...] = value.astype(out.dtype)


def call(kernel, outs, scratch, flops, *args):
    vmem = pl.BlockSpec(memory_space=pltpu.VMEM)
    return pl.pallas_call(
        kernel,
        out_shape=outs,
        in_specs=[pl.BlockSpec(memory_space=pltpu.SMEM)] + [vmem] * (len(args) - 1),
        out_specs=[vmem] * len(outs),
        scratch_shapes=scratch,
        compiler_params=pltpu.CompilerParams(vmem_limit_bytes=32 * 1024 * 1024),
        cost_estimate=pl.CostEstimate(
            flops=flops, bytes_accessed=6 * 1024 * 1024, transcendentals=0
        ),
    )(*args)


def shards(acts, weight, cotangent):
    me = jnp.stack([lax.axis_index("row"), lax.axis_index("col")]).astype(jnp.int32)
    part, depth = acts.shape
    width = weight.shape[1]
    tokens = part * COLS

    pair = jnp.concatenate([acts, swap(acts, "col", 16)])
    line = jnp.concatenate([pair] + [swap(pair, "col", 4 * k) for k in (1, 2, 3)])
    x2 = swap(line, "col", 2)
    x1 = swap(line, "col", 1)
    x3 = swap(line, "col", 3)

    flops = 2 * tokens * depth * width
    send, keep, acts_full = call(
        up_kernel,
        [
            jax.ShapeDtypeStruct((tokens // 2, width), BF16),
            jax.ShapeDtypeStruct((tokens // 2, width), F32),
            jax.ShapeDtypeStruct((tokens, depth), BF16),
        ],
        [],
        flops,
        me, line, x1, x2, x3, weight,
    )

    mine = keep + swap(send, "row", 1).astype(F32)
    size = tokens // 8
    sent = [mine[m * size : (m + 1) * size].astype(BF16) for m in (1, 2, 3)]
    got = [swap(s, "row", 4 * m) for s, m in zip(sent, (1, 2, 3))]
    mine = mine[:size] + got[0].astype(F32) + got[1].astype(F32) + got[2].astype(F32)
    size = tokens // 16
    pre = mine[:size] + swap(mine[size:].astype(BF16), "row", 2).astype(F32)

    output = gelu_value(pre).astype(BF16)
    grad = (cotangent.astype(F32) * gelu_slope(pre)).astype(BF16)

    pair = jnp.concatenate([grad, swap(grad, "row", 2)])
    g0 = jnp.concatenate([pair] + [swap(pair, "row", 4 * m) for m in (1, 2, 3)])
    g1 = swap(g0, "row", 1)

    size = tokens // 4
    mine, x1, x2, x3 = call(
        down_kernel,
        [jax.ShapeDtypeStruct((size, depth), F32)]
        + [jax.ShapeDtypeStruct((size, depth), BF16)] * 3,
        [pltpu.VMEM((tokens, width), BF16)],
        flops,
        me, g0, g1, weight,
    )

    x2 = swap(x2, "col", 2)
    x1 = swap(x1, "col", 1)
    x3 = swap(x3, "col", 3)
    mine = mine + x1.astype(F32) + x2.astype(F32) + x3.astype(F32)
    size = tokens // 16
    sent = [mine[k * size : (k + 1) * size].astype(BF16) for k in (1, 2, 3)]
    got = [swap(s, "col", 4 * k) for s, k in zip(sent, (1, 2, 3))]
    mine = mine[:size] + got[0].astype(F32) + got[1].astype(F32) + got[2].astype(F32)
    size = tokens // 32
    acts_grad = (
        mine[:size] + swap(mine[size:].astype(BF16), "col", 16).astype(F32)
    ).astype(BF16)

    grad_full = jnp.concatenate([g0, g1])
    weight_sum = lax.dot_general(
        acts_full, grad_full, (((0,), (0,)), ((), ())), preferred_element_type=F32
    )
    weight_grad = (weight_sum * tokens ** (-0.5)).astype(BF16)
    return (output, acts_grad, weight_grad)


def solution(mesh):
    in_specs = (P("col", "row"), P("row", "col"), P("row", "col"))
    out_specs = (P("row", "col"), P("col", "row"), P("row", "col"))
    return jax.shard_map(shards, mesh=mesh, in_specs=in_specs, out_specs=out_specs, check_vma=False)
```

time: 707 us -> 195 us (0.28)
  the two profiles are of different devices: /device:TPU:16 before, /device:TPU:1 now
where the time goes in v1:
time: 195 us; the launch traced here: 194 us
  starting transfers between devices  112 us (57%)
  waiting for transfers between devices  70.3 us (36%)
  Pallas kernels  4.08 us (2%)
  matrix products  2.47 us (1%)
  local copies, waits for them, and re-layouts  2.38 us (1%)
  other arithmetic  2.08 us (1%)
    ppermute x24, starting transfers between devices, swap(): return lax.ppermute(value, axis, [(i, i ^ mask) for i in range(size)])  112 us
    ppermute x24, waiting for transfers between devices, swap(): return lax.ppermute(value, axis, [(i, i ^ mask) for i in range(size)])  70.3 us
    pallas_call x2, Pallas kernels, call(): pl.pallas_call(kernel, out_shape=outs, in_specs=[pl.BlockSpec(memory_spac...  4.08 us
  transfers between devices with their start and end apart: 24, of which 16 were waited for; matrix products, arithmetic and copies ran while one was open for 2% of the time, Pallas kernels for 0%

profile of v1, /device:TPU:1, one launch (start us, length us, event | category | flops | bytes accessed | tf_op | source)
XLA Modules:
  0.0 194.2 jit_solution(4687200425728394044)
XLA Ops:
  0.6 9.6 %collective-permute-start = (bf16[32,768]{1,0:T(8,128)(2,1)}, bf16[32,768]{1,0:T(8,128)(2,1)S(1)}, u32[]{:S(2)}, u32[]{:S(2)}) collective-permute-start(bf16[32,768]{1,0:T(8,128)(2,1)} %param.3), channel_id=1, source_target_pairs={{0,16},{1,17},{2,18},{3,19},{4,20},{5,21},{6,22},{7,23},{8,24},{9,... | collective-permute-start | bytes 147464 | tf_op jit(solution)/shard_map/ppermute | solution.py:27
  12.0 3.5 %collective-permute-start.1 = (bf16[64,768]{1,0:T(8,128)(2,1)S(1)}, bf16[64,768]{1,0:T(8,128)(2,1)S(1)}, u32[]{:S(2)}, u32[]{:S(2)}) collective-permute-start(bf16[64,768]{1,0:T(8,128)(2,1)S(1)} %get-tuple-element.37), channel_id=1, source_target_pairs={{0,4},{1,5},{2,6},{3,7},{4,0},{5,1},{6,2},{7,3},{8,12},{9,13},{10,... | collective-permute-start | bytes 294920 | tf_op jit(solution)/shard_map/ppermute | solution.py:27
  15.5 6.3 %collective-permute-start.3 = (bf16[64,768]{1,0:T(8,128)(2,1)S(1)}, bf16[64,768]{1,0:T(8,128)(2,1)S(1)}, u32[]{:S(2)}, u32[]{:S(2)}) collective-permute-start(bf16[64,768]{1,0:T(8,128)(2,1)S(1)} %get-tuple-element.37), channel_id=1, source_target_pairs={{0,12},{1,13},{2,14},{3,15},{4,8},{5,9},{6,10},{7,11},{8,4},{9,5},... | collective-permute-start | bytes 294920 | tf_op jit(solution)/shard_map/ppermute | solution.py:27
  21.9 2.2 %collective-permute-start.2 = (bf16[64,768]{1,0:T(8,128)(2,1)S(1)}, bf16[64,768]{1,0:T(8,128)(2,1)S(1)}, u32[]{:S(2)}, u32[]{:S(2)}) collective-permute-start(bf16[64,768]{1,0:T(8,128)(2,1)S(1)} %get-tuple-element.37), channel_id=1, source_target_pairs={{0,8},{1,9},{2,10},{3,11},{4,12},{5,13},{6,14},{7,15},{8,0},{9,1},... | collective-permute-start | bytes 294920 | tf_op jit(solution)/shard_map/ppermute | solution.py:27
  24.1 8.2 %collective-permute-done.2 = bf16[64,768]{1,0:T(8,128)(2,1)S(1)} collective-permute-done((bf16[64,768]{1,0:T(8,128)(2,1)S(1)}, bf16[64,768]{1,0:T(8,128)(2,1)S(1)}, u32[]{:S(2)}, u32[]{:S(2)}) %collective-permute-start.2) | collective-permute-done | bytes 98336 | tf_op jit(solution)/shard_map/ppermute | solution.py:27
  32.4 3.5 %collective-permute-start.6 = (bf16[256,768]{1,0:T(8,128)(2,1)S(1)}, bf16[256,768]{1,0:T(8,128)(2,1)S(1)}, u32[]{:S(2)}, u32[]{:S(2)}) collective-permute-start(bf16[256,768]{1,0:T(8,128)(2,1)S(1)} %constant_dynamic-update-slice_fusion.2.own), channel_id=1, source_target_pairs={{0,3},{1,2},{2,1},{3,0},{4,7},{5,6},{6,5},{7,4},{8,11},{9,10},{10,... | collective-permute-start | bytes 1179656 | tf_op jit(solution)/shard_map/ppermute | solution.py:27
  35.8 2.4 %collective-permute-start.5 = (bf16[256,768]{1,0:T(8,128)(2,1)S(1)}, bf16[256,768]{1,0:T(8,128)(2,1)S(1)}, u32[]{:S(2)}, u32[]{:S(2)}) collective-permute-start(bf16[256,768]{1,0:T(8,128)(2,1)S(1)} %constant_dynamic-update-slice_fusion.2.own), channel_id=1, source_target_pairs={{0,2},{1,3},{2,0},{3,1},{4,6},{5,7},{6,4},{7,5},{8,10},{9,11},{10,... | collective-permute-start | bytes 1179656 | tf_op jit(solution)/shard_map/ppermute | solution.py:27
  38.3 3.1 %collective-permute-start.4 = (bf16[256,768]{1,0:T(8,128)(2,1)S(1)}, bf16[256,768]{1,0:T(8,128)(2,1)S(1)}, u32[]{:S(2)}, u32[]{:S(2)}) collective-permute-start(bf16[256,768]{1,0:T(8,128)(2,1)S(1)} %constant_dynamic-update-slice_fusion.2.own), channel_id=1, source_target_pairs={{0,1},{1,0},{2,3},{3,2},{4,5},{5,4},{6,7},{7,6},{8,9},{9,8},{10,11... | collective-permute-start | bytes 1179656 | tf_op jit(solution)/shard_map/ppermute | solution.py:27
  41.4 12.0 %collective-permute-done.6.x3 = bf16[256,768]{1,0:T(8,128)(2,1)S(1)} collective-permute-done((bf16[256,768]{1,0:T(8,128)(2,1)S(1)}, bf16[256,768]{1,0:T(8,128)(2,1)S(1)}, u32[]{:S(2)}, u32[]{:S(2)}) %collective-permute-start.6) | collective-permute-done | bytes 393248 | tf_op jit(solution)/shard_map/ppermute | solution.py:27
  53.5 2.3 %collective-permute-done.4.x1 = bf16[256,768]{1,0:T(8,128)(2,1)S(1)} collective-permute-done((bf16[256,768]{1,0:T(8,128)(2,1)S(1)}, bf16[256,768]{1,0:T(8,128)(2,1)S(1)}, u32[]{:S(2)}, u32[]{:S(2)}) %collective-permute-start.4) | collective-permute-done | bytes 393248 | tf_op jit(solution)/shard_map/ppermute | solution.py:27
  59.1 4.1 %collective-permute-start.7 = (bf16[512,768]{1,0:T(8,128)(2,1)S(1)}, bf16[512,768]{1,0:T(8,128)(2,1)S(1)}, u32[]{:S(2)}, u32[]{:S(2)}) collective-permute-start(bf16[512,768]{1,0:T(8,128)(2,1)S(1)} %get-tuple-element.11), channel_id=1, source_target_pairs={{0,32},{32,0},{64,96},{96,64},{128,160},{160,128},{192,224},{224,1... | collective-permute-start | bytes 2359304 | tf_op jit(solution)/shard_map/ppermute | solution.py:27
  65.4 2.3 %collective-permute-start.8 = (bf16[128,768]{1,0:T(8,128)(2,1)S(1)}, bf16[128,768]{1,0:T(8,128)(2,1)S(1)}, u32[]{:S(2)}, u32[]{:S(2)}) collective-permute-start(bf16[128,768]{1,0:T(8,128)(2,1)S(1)} %get-tuple-element.23), channel_id=1, source_target_pairs={{0,128},{32,160},{64,192},{96,224},{128,0},{160,32},{192,64},{224,... | collective-permute-start | bytes 589832 | tf_op jit(solution)/shard_map/ppermute | solution.py:27
  67.7 3.8 %collective-permute-start.10 = (bf16[128,768]{1,0:T(8,128)(2,1)S(1)}, bf16[128,768]{1,0:T(8,128)(2,1)S(1)}, u32[]{:S(2)}, u32[]{:S(2)}) collective-permute-start(bf16[128,768]{1,0:T(8,128)(2,1)S(1)} %get-tuple-element.24), channel_id=1, source_target_pairs={{0,384},{32,416},{64,448},{96,480},{128,256},{160,288},{192,320},{... | collective-permute-start | bytes 589832 | tf_op jit(solution)/shard_map/ppermute | solution.py:27
  71.5 2.9 %collective-permute-start.9 = (bf16[128,768]{1,0:T(8,128)(2,1)S(1)}, bf16[128,768]{1,0:T(8,128)(2,1)S(1)}, u32[]{:S(2)}, u32[]{:S(2)}) collective-permute-start(bf16[128,768]{1,0:T(8,128)(2,1)S(1)} %get-tuple-element.25), channel_id=1, source_target_pairs={{0,256},{32,288},{64,320},{96,352},{128,384},{160,416},{192,448},{... | collective-permute-start | bytes 589832 | tf_op jit(solution)/shard_map/ppermute | solution.py:27
  76.6 3.9 %collective-permute-done.9 = bf16[128,768]{1,0:T(8,128)(2,1)S(1)} collective-permute-done((bf16[128,768]{1,0:T(8,128)(2,1)S(1)}, bf16[128,768]{1,0:T(8,128)(2,1)S(1)}, u32[]{:S(2)}, u32[]{:S(2)}) %collective-permute-start.9) | collective-permute-done | bytes 196640 | tf_op jit(solution)/shard_map/ppermute | solution.py:27
  80.6 9.8 %collective-permute-start.11 = (bf16[64,768]{1,0:T(8,128)(2,1)S(1)}, bf16[64,768]{1,0:T(8,128)(2,1)S(1)}, u32[]{:S(2)}, u32[]{:S(2)}) collective-permute-start(bf16[64,768]{1,0:T(8,128)(2,1)S(1)} %slice.94), channel_id=1, source_target_pairs={{0,64},{32,96},{64,0},{96,32},{128,192},{160,224},{192,128},{224,1... | collective-permute-start | bytes 294920 | tf_op jit(solution)/shard_map/ppermute | solution.py:27
  90.4 6.1 %collective-permute-done.11 = bf16[64,768]{1,0:T(8,128)(2,1)S(1)} collective-permute-done((bf16[64,768]{1,0:T(8,128)(2,1)S(1)}, bf16[64,768]{1,0:T(8,128)(2,1)S(1)}, u32[]{:S(2)}, u32[]{:S(2)}) %collective-permute-start.11) | collective-permute-done | bytes 98336 | tf_op jit(solution)/shard_map/ppermute | solution.py:27
  96.6 13.0 %collective-permute-start.12 = (bf16[64,768]{1,0:T(8,128)(2,1)S(1)}, bf16[64,768]{1,0:T(8,128)(2,1)S(1)}, u32[]{:S(2)}, u32[]{:S(2)}) collective-permute-start(bf16[64,768]{1,0:T(8,128)(2,1)S(1)} %get-tuple-element.18), channel_id=1, source_target_pairs={{0,64},{32,96},{64,0},{96,32},{128,192},{160,224},{192,128},{224,1... | collective-permute-start | bytes 294920 | tf_op jit(solution)/shard_map/ppermute | solution.py:27
  109.6 2.8 %collective-permute-done.12 = bf16[64,768]{1,0:T(8,128)(2,1)S(1)} collective-permute-done((bf16[64,768]{1,0:T(8,128)(2,1)S(1)}, bf16[64,768]{1,0:T(8,128)(2,1)S(1)}, u32[]{:S(2)}, u32[]{:S(2)}) %collective-permute-start.12) | collective-permute-done | bytes 98336 | tf_op jit(solution)/shard_map/ppermute | solution.py:27
  112.4 2.2 %collective-permute-start.13 = (bf16[128,768]{1,0:T(8,128)(2,1)S(1)}, bf16[128,768]{1,0:T(8,128)(2,1)S(1)}, u32[]{:S(2)}, u32[]{:S(2)}) collective-permute-start(bf16[128,768]{1,0:T(8,128)(2,1)S(1)} %pad_maximum_fusion), channel_id=1, source_target_pairs={{0,128},{32,160},{64,192},{96,224},{128,0},{160,32},{192,64},{224,... | collective-permute-start | bytes 589832 | tf_op jit(solution)/shard_map/ppermute | solution.py:27
  116.5 4.9 %collective-permute-start.14 = (bf16[128,768]{1,0:T(8,128)(2,1)S(1)}, bf16[128,768]{1,0:T(8,128)(2,1)S(1)}, u32[]{:S(2)}, u32[]{:S(2)}) collective-permute-start(bf16[128,768]{1,0:T(8,128)(2,1)S(1)} %pad_maximum_fusion), channel_id=1, source_target_pairs={{0,256},{32,288},{64,320},{96,352},{128,384},{160,416},{192,448},{... | collective-permute-start | bytes 589832 | tf_op jit(solution)/shard_map/ppermute | solution.py:27
  121.5 4.6 %collective-permute-done.14 = bf16[128,768]{1,0:T(8,128)(2,1)S(1)} collective-permute-done((bf16[128,768]{1,0:T(8,128)(2,1)S(1)}, bf16[128,768]{1,0:T(8,128)(2,1)S(1)}, u32[]{:S(2)}, u32[]{:S(2)}) %collective-permute-start.14) | collective-permute-done | bytes 196640 | tf_op jit(solution)/shard_map/ppermute | solution.py:27
  126.1 6.8 %collective-permute-start.16 = (bf16[512,768]{1,0:T(8,128)(2,1)S(1)}, bf16[512,768]{1,0:T(8,128)(2,1)S(1)}, u32[]{:S(2)}, u32[]{:S(2)}) collective-permute-start(bf16[512,768]{1,0:T(8,128)(2,1)S(1)} %get-tuple-element.30.g0), channel_id=1, source_target_pairs={{0,32},{32,0},{64,96},{96,64},{128,160},{160,128},{192,224},{224,1... | collective-permute-start | bytes 2359304 | tf_op jit(solution)/shard_map/ppermute | solution.py:27
  136.9 3.1 %collective-permute-start.17 = (bf16[256,768]{1,0:T(8,128)(2,1)S(1)}, bf16[256,768]{1,0:T(8,128)(2,1)S(1)}, u32[]{:S(2)}, u32[]{:S(2)}) collective-permute-start(bf16[256,768]{1,0:T(8,128)(2,1)S(1)} %get-tuple-element.13), channel_id=1, source_target_pairs={{0,1},{1,0},{2,3},{3,2},{4,5},{5,4},{6,7},{7,6},{8,9},{9,8},{10,11... | collective-permute-start | bytes 1179656 | tf_op jit(solution)/shard_map/ppermute | solution.py:27
  140.0 4.4 %collective-permute-start.18 = (bf16[256,768]{1,0:T(8,128)(2,1)S(1)}, bf16[256,768]{1,0:T(8,128)(2,1)S(1)}, u32[]{:S(2)}, u32[]{:S(2)}) collective-permute-start(bf16[256,768]{1,0:T(8,128)(2,1)S(1)} %get-tuple-element.14), channel_id=1, source_target_pairs={{0,2},{1,3},{2,0},{3,1},{4,6},{5,7},{6,4},{7,5},{8,10},{9,11},{10,... | collective-permute-start | bytes 1179656 | tf_op jit(solution)/shard_map/ppermute | solution.py:27
  149.1 10.7 %collective-permute-done.18 = bf16[256,768]{1,0:T(8,128)(2,1)S(1)} collective-permute-done((bf16[256,768]{1,0:T(8,128)(2,1)S(1)}, bf16[256,768]{1,0:T(8,128)(2,1)S(1)}, u32[]{:S(2)}, u32[]{:S(2)}) %collective-permute-start.18) | collective-permute-done | bytes 393248 | tf_op jit(solution)/shard_map/ppermute | solution.py:27
  159.8 6.0 %collective-permute-done.19 = bf16[256,768]{1,0:T(8,128)(2,1)S(1)} collective-permute-done((bf16[256,768]{1,0:T(8,128)(2,1)S(1)}, bf16[256,768]{1,0:T(8,128)(2,1)S(1)}, u32[]{:S(2)}, u32[]{:S(2)}) %collective-permute-start.19) | collective-permute-done | bytes 393248 | tf_op jit(solution)/shard_map/ppermute | solution.py:27
  167.9 7.7 %collective-permute-start.22 = (bf16[64,768]{1,0:T(8,128)(2,1)S(1)}, bf16[64,768]{1,0:T(8,128)(2,1)S(1)}, u32[]{:S(2)}, u32[]{:S(2)}) collective-permute-start(bf16[64,768]{1,0:T(8,128)(2,1)S(1)} %get-tuple-element.27), channel_id=1, source_target_pairs={{0,12},{1,13},{2,14},{3,15},{4,8},{5,9},{6,10},{7,11},{8,4},{9,5},... | collective-permute-start | bytes 294920 | tf_op jit(solution)/shard_map/ppermute | solution.py:27
  175.6 2.2 %collective-permute-start.21 = (bf16[64,768]{1,0:T(8,128)(2,1)S(1)}, bf16[64,768]{1,0:T(8,128)(2,1)S(1)}, u32[]{:S(2)}, u32[]{:S(2)}) collective-permute-start(bf16[64,768]{1,0:T(8,128)(2,1)S(1)} %get-tuple-element.28), channel_id=1, source_target_pairs={{0,8},{1,9},{2,10},{3,11},{4,12},{5,13},{6,14},{7,15},{8,0},{9,1},... | collective-permute-start | bytes 294920 | tf_op jit(solution)/shard_map/ppermute | solution.py:27
  178.9 4.1 %collective-permute-done.21 = bf16[64,768]{1,0:T(8,128)(2,1)S(1)} collective-permute-done((bf16[64,768]{1,0:T(8,128)(2,1)S(1)}, bf16[64,768]{1,0:T(8,128)(2,1)S(1)}, u32[]{:S(2)}, u32[]{:S(2)}) %collective-permute-start.21) | collective-permute-done | bytes 98336 | tf_op jit(solution)/shard_map/ppermute | solution.py:27
  183.0 8.1 %collective-permute-start.23 = (bf16[32,768]{1,0:T(8,128)(2,1)S(1)}, bf16[32,768]{1,0:T(8,128)(2,1)S(1)}, u32[]{:S(2)}, u32[]{:S(2)}) collective-permute-start(bf16[32,768]{1,0:T(8,128)(2,1)S(1)} %slice.95), channel_id=1, source_target_pairs={{0,16},{1,17},{2,18},{3,19},{4,20},{5,21},{6,22},{7,23},{8,24},{9,... | collective-permute-start | bytes 147464 | tf_op jit(solution)/shard_map/ppermute | solution.py:27
  191.1 2.5 %multiply_convert_fusion = bf16[768,768]{1,0:T(8,128)(2,1)} fusion(bf16[1024,768]{1,0:T(8,128)(2,1)S(1)} %get-tuple-element.16, bf16[1024,768]{1,0:T(8,128)(2,1)S(1)} %constant_dynamic-update-slice_fusion.12), kind=kOutput, calls=%fused_computation | convolution fusion | flops 1209139200 | bytes 4325376 | tf_op jit(solution)/shard_map/dot_general | solution.py:161
  (49 shorter events, 24.3 us)
Async XLA Ops:
  0.6 11.3 %collective-permute-start = (bf16[32,768]{1,0:T(8,128)(2,1)}, bf16[32,768]{1,0:T(8,128)(2,1)S(1)}, u32[]{:S(2)}, u32[]{:S(2)}) collective-permute-start(bf16[32,768]{1,0:T(8,128)(2,1)} %param.3), channel_id=1, source_target_pairs={{0,16},{1,17},{2,18},{3,19},{4,20},{5,21},{6,22},{7,23},{8,24},{9,... | collective-permute-start | bytes 147464 | tf_op jit(solution)/shard_map/ppermute | solution.py:27
  12.0 12.1 %collective-permute-start.1 = (bf16[64,768]{1,0:T(8,128)(2,1)S(1)}, bf16[64,768]{1,0:T(8,128)(2,1)S(1)}, u32[]{:S(2)}, u32[]{:S(2)}) collective-permute-start(bf16[64,768]{1,0:T(8,128)(2,1)S(1)} %get-tuple-element.37), channel_id=1, source_target_pairs={{0,4},{1,5},{2,6},{3,7},{4,0},{5,1},{6,2},{7,3},{8,12},{9,13},{10,... | collective-permute-start | bytes 294920 | tf_op jit(solution)/shard_map/ppermute | solution.py:27
  15.5 16.8 %collective-permute-start.3 = (bf16[64,768]{1,0:T(8,128)(2,1)S(1)}, bf16[64,768]{1,0:T(8,128)(2,1)S(1)}, u32[]{:S(2)}, u32[]{:S(2)}) collective-permute-start(bf16[64,768]{1,0:T(8,128)(2,1)S(1)} %get-tuple-element.37), channel_id=1, source_target_pairs={{0,12},{1,13},{2,14},{3,15},{4,8},{5,9},{6,10},{7,11},{8,4},{9,5},... | collective-permute-start | bytes 294920 | tf_op jit(solution)/shard_map/ppermute | solution.py:27
  21.9 10.4 %collective-permute-start.2 = (bf16[64,768]{1,0:T(8,128)(2,1)S(1)}, bf16[64,768]{1,0:T(8,128)(2,1)S(1)}, u32[]{:S(2)}, u32[]{:S(2)}) collective-permute-start(bf16[64,768]{1,0:T(8,128)(2,1)S(1)} %get-tuple-element.37), channel_id=1, source_target_pairs={{0,8},{1,9},{2,10},{3,11},{4,12},{5,13},{6,14},{7,15},{8,0},{9,1},... | collective-permute-start | bytes 294920 | tf_op jit(solution)/shard_map/ppermute | solution.py:27
  32.4 21.1 %collective-permute-start.6 = (bf16[256,768]{1,0:T(8,128)(2,1)S(1)}, bf16[256,768]{1,0:T(8,128)(2,1)S(1)}, u32[]{:S(2)}, u32[]{:S(2)}) collective-permute-start(bf16[256,768]{1,0:T(8,128)(2,1)S(1)} %constant_dynamic-update-slice_fusion.2.own), channel_id=1, source_target_pairs={{0,3},{1,2},{2,1},{3,0},{4,7},{5,6},{6,5},{7,4},{8,11},{9,10},{10,... | collective-permute-start | bytes 1179656 | tf_op jit(solution)/shard_map/ppermute | solution.py:27
  35.8 17.6 %collective-permute-start.5 = (bf16[256,768]{1,0:T(8,128)(2,1)S(1)}, bf16[256,768]{1,0:T(8,128)(2,1)S(1)}, u32[]{:S(2)}, u32[]{:S(2)}) collective-permute-start(bf16[256,768]{1,0:T(8,128)(2,1)S(1)} %constant_dynamic-update-slice_fusion.2.own), channel_id=1, source_target_pairs={{0,2},{1,3},{2,0},{3,1},{4,6},{5,7},{6,4},{7,5},{8,10},{9,11},{10,... | collective-permute-start | bytes 1179656 | tf_op jit(solution)/shard_map/ppermute | solution.py:27
  38.3 17.5 %collective-permute-start.4 = (bf16[256,768]{1,0:T(8,128)(2,1)S(1)}, bf16[256,768]{1,0:T(8,128)(2,1)S(1)}, u32[]{:S(2)}, u32[]{:S(2)}) collective-permute-start(bf16[256,768]{1,0:T(8,128)(2,1)S(1)} %constant_dynamic-update-slice_fusion.2.own), channel_id=1, source_target_pairs={{0,1},{1,0},{2,3},{3,2},{4,5},{5,4},{6,7},{7,6},{8,9},{9,8},{10,11... | collective-permute-start | bytes 1179656 | tf_op jit(solution)/shard_map/ppermute | solution.py:27
  55.8 1.3 copy-start
  59.1 6.0 %collective-permute-start.7 = (bf16[512,768]{1,0:T(8,128)(2,1)S(1)}, bf16[512,768]{1,0:T(8,128)(2,1)S(1)}, u32[]{:S(2)}, u32[]{:S(2)}) collective-permute-start(bf16[512,768]{1,0:T(8,128)(2,1)S(1)} %get-tuple-element.11), channel_id=1, source_target_pairs={{0,32},{32,0},{64,96},{96,64},{128,160},{160,128},{192,224},{224,1... | collective-permute-start | bytes 2359304 | tf_op jit(solution)/shard_map/ppermute | solution.py:27
  65.3 31.1 %copy-start.2 = (bf16[64,768]{1,0:T(8,128)(2,1)S(1)}, bf16[64,768]{1,0:T(8,128)(2,1)}, u32[]{:S(2)}) copy-start(bf16[64,768]{1,0:T(8,128)(2,1)} %param.5) | copy-start | bytes 294916
  65.4 9.0 %collective-permute-start.8 = (bf16[128,768]{1,0:T(8,128)(2,1)S(1)}, bf16[128,768]{1,0:T(8,128)(2,1)S(1)}, u32[]{:S(2)}, u32[]{:S(2)}) collective-permute-start(bf16[128,768]{1,0:T(8,128)(2,1)S(1)} %get-tuple-element.23), channel_id=1, source_target_pairs={{0,128},{32,160},{64,192},{96,224},{128,0},{160,32},{192,64},{224,... | collective-permute-start | bytes 589832 | tf_op jit(solution)/shard_map/ppermute | solution.py:27
  67.7 8.9 %collective-permute-start.10 = (bf16[128,768]{1,0:T(8,128)(2,1)S(1)}, bf16[128,768]{1,0:T(8,128)(2,1)S(1)}, u32[]{:S(2)}, u32[]{:S(2)}) collective-permute-start(bf16[128,768]{1,0:T(8,128)(2,1)S(1)} %get-tuple-element.24), channel_id=1, source_target_pairs={{0,384},{32,416},{64,448},{96,480},{128,256},{160,288},{192,320},{... | collective-permute-start | bytes 589832 | tf_op jit(solution)/shard_map/ppermute | solution.py:27
  71.5 9.0 %collective-permute-start.9 = (bf16[128,768]{1,0:T(8,128)(2,1)S(1)}, bf16[128,768]{1,0:T(8,128)(2,1)S(1)}, u32[]{:S(2)}, u32[]{:S(2)}) collective-permute-start(bf16[128,768]{1,0:T(8,128)(2,1)S(1)} %get-tuple-element.25), channel_id=1, source_target_pairs={{0,256},{32,288},{64,320},{96,352},{128,384},{160,416},{192,448},{... | collective-permute-start | bytes 589832 | tf_op jit(solution)/shard_map/ppermute | solution.py:27
  80.6 54.3 %copy-start.1 = (bf16[768,768]{1,0:T(8,128)(2,1)S(1)}, bf16[768,768]{1,0:T(8,128)(2,1)}, u32[]{:S(2)}) copy-start(bf16[768,768]{1,0:T(8,128)(2,1)} %w.3) | copy-start | bytes 3538948
  80.6 15.9 %collective-permute-start.11 = (bf16[64,768]{1,0:T(8,128)(2,1)S(1)}, bf16[64,768]{1,0:T(8,128)(2,1)S(1)}, u32[]{:S(2)}, u32[]{:S(2)}) collective-permute-start(bf16[64,768]{1,0:T(8,128)(2,1)S(1)} %slice.94), channel_id=1, source_target_pairs={{0,64},{32,96},{64,0},{96,32},{128,192},{160,224},{192,128},{224,1... | collective-permute-start | bytes 294920 | tf_op jit(solution)/shard_map/ppermute | solution.py:27
  96.6 15.8 %collective-permute-start.12 = (bf16[64,768]{1,0:T(8,128)(2,1)S(1)}, bf16[64,768]{1,0:T(8,128)(2,1)S(1)}, u32[]{:S(2)}, u32[]{:S(2)}) collective-permute-start(bf16[64,768]{1,0:T(8,128)(2,1)S(1)} %get-tuple-element.18), channel_id=1, source_target_pairs={{0,64},{32,96},{64,0},{96,32},{128,192},{160,224},{192,128},{224,1... | collective-permute-start | bytes 294920 | tf_op jit(solution)/shard_map/ppermute | solution.py:27
  112.4 9.0 %collective-permute-start.13 = (bf16[128,768]{1,0:T(8,128)(2,1)S(1)}, bf16[128,768]{1,0:T(8,128)(2,1)S(1)}, u32[]{:S(2)}, u32[]{:S(2)}) collective-permute-start(bf16[128,768]{1,0:T(8,128)(2,1)S(1)} %pad_maximum_fusion), channel_id=1, source_target_pairs={{0,128},{32,160},{64,192},{96,224},{128,0},{160,32},{192,64},{224,... | collective-permute-start | bytes 589832 | tf_op jit(solution)/shard_map/ppermute | solution.py:27
  114.6 11.5 %collective-permute-start.15 = (bf16[128,768]{1,0:T(8,128)(2,1)S(1)}, bf16[128,768]{1,0:T(8,128)(2,1)S(1)}, u32[]{:S(2)}, u32[]{:S(2)}) collective-permute-start(bf16[128,768]{1,0:T(8,128)(2,1)S(1)} %pad_maximum_fusion), channel_id=1, source_target_pairs={{0,384},{32,416},{64,448},{96,480},{128,256},{160,288},{192,320},{... | collective-permute-start | bytes 589832 | tf_op jit(solution)/shard_map/ppermute | solution.py:27
  116.5 9.5 %collective-permute-start.14 = (bf16[128,768]{1,0:T(8,128)(2,1)S(1)}, bf16[128,768]{1,0:T(8,128)(2,1)S(1)}, u32[]{:S(2)}, u32[]{:S(2)}) collective-permute-start(bf16[128,768]{1,0:T(8,128)(2,1)S(1)} %pad_maximum_fusion), channel_id=1, source_target_pairs={{0,256},{32,288},{64,320},{96,352},{128,384},{160,416},{192,448},{... | collective-permute-start | bytes 589832 | tf_op jit(solution)/shard_map/ppermute | solution.py:27
  126.1 8.7 %collective-permute-start.16 = (bf16[512,768]{1,0:T(8,128)(2,1)S(1)}, bf16[512,768]{1,0:T(8,128)(2,1)S(1)}, u32[]{:S(2)}, u32[]{:S(2)}) collective-permute-start(bf16[512,768]{1,0:T(8,128)(2,1)S(1)} %get-tuple-element.30.g0), channel_id=1, source_target_pairs={{0,32},{32,0},{64,96},{96,64},{128,160},{160,128},{192,224},{224,1... | collective-permute-start | bytes 2359304 | tf_op jit(solution)/shard_map/ppermute | solution.py:27
  136.9 12.2 %collective-permute-start.17 = (bf16[256,768]{1,0:T(8,128)(2,1)S(1)}, bf16[256,768]{1,0:T(8,128)(2,1)S(1)}, u32[]{:S(2)}, u32[]{:S(2)}) collective-permute-start(bf16[256,768]{1,0:T(8,128)(2,1)S(1)} %get-tuple-element.13), channel_id=1, source_target_pairs={{0,1},{1,0},{2,3},{3,2},{4,5},{5,4},{6,7},{7,6},{8,9},{9,8},{10,11... | collective-permute-start | bytes 1179656 | tf_op jit(solution)/shard_map/ppermute | solution.py:27
  140.0 19.8 %collective-permute-start.18 = (bf16[256,768]{1,0:T(8,128)(2,1)S(1)}, bf16[256,768]{1,0:T(8,128)(2,1)S(1)}, u32[]{:S(2)}, u32[]{:S(2)}) collective-permute-start(bf16[256,768]{1,0:T(8,128)(2,1)S(1)} %get-tuple-element.14), channel_id=1, source_target_pairs={{0,2},{1,3},{2,0},{3,1},{4,6},{5,7},{6,4},{7,5},{8,10},{9,11},{10,... | collective-permute-start | bytes 1179656 | tf_op jit(solution)/shard_map/ppermute | solution.py:27
  144.4 21.4 %collective-permute-start.19 = (bf16[256,768]{1,0:T(8,128)(2,1)S(1)}, bf16[256,768]{1,0:T(8,128)(2,1)S(1)}, u32[]{:S(2)}, u32[]{:S(2)}) collective-permute-start(bf16[256,768]{1,0:T(8,128)(2,1)S(1)} %get-tuple-element.15), channel_id=1, source_target_pairs={{0,3},{1,2},{2,1},{3,0},{4,7},{5,6},{6,5},{7,4},{8,11},{9,10},{10,... | collective-permute-start | bytes 1179656 | tf_op jit(solution)/shard_map/ppermute | solution.py:27
  166.0 11.9 %collective-permute-start.20 = (bf16[64,768]{1,0:T(8,128)(2,1)S(1)}, bf16[64,768]{1,0:T(8,128)(2,1)S(1)}, u32[]{:S(2)}, u32[]{:S(2)}) collective-permute-start(bf16[64,768]{1,0:T(8,128)(2,1)S(1)} %get-tuple-element.26), channel_id=1, source_target_pairs={{0,4},{1,5},{2,6},{3,7},{4,0},{5,1},{6,2},{7,3},{8,12},{9,13},{10,... | collective-permute-start | bytes 294920 | tf_op jit(solution)/shard_map/ppermute | solution.py:27
  167.9 11.0 %collective-permute-start.22 = (bf16[64,768]{1,0:T(8,128)(2,1)S(1)}, bf16[64,768]{1,0:T(8,128)(2,1)S(1)}, u32[]{:S(2)}, u32[]{:S(2)}) collective-permute-start(bf16[64,768]{1,0:T(8,128)(2,1)S(1)} %get-tuple-element.27), channel_id=1, source_target_pairs={{0,12},{1,13},{2,14},{3,15},{4,8},{5,9},{6,10},{7,11},{8,4},{9,5},... | collective-permute-start | bytes 294920 | tf_op jit(solution)/shard_map/ppermute | solution.py:27
  175.6 7.4 %collective-permute-start.21 = (bf16[64,768]{1,0:T(8,128)(2,1)S(1)}, bf16[64,768]{1,0:T(8,128)(2,1)S(1)}, u32[]{:S(2)}, u32[]{:S(2)}) collective-permute-start(bf16[64,768]{1,0:T(8,128)(2,1)S(1)} %get-tuple-element.28), channel_id=1, source_target_pairs={{0,8},{1,9},{2,10},{3,11},{4,12},{5,13},{6,14},{7,15},{8,0},{9,1},... | collective-permute-start | bytes 294920 | tf_op jit(solution)/shard_map/ppermute | solution.py:27
  183.0 10.5 %collective-permute-start.23 = (bf16[32,768]{1,0:T(8,128)(2,1)S(1)}, bf16[32,768]{1,0:T(8,128)(2,1)S(1)}, u32[]{:S(2)}, u32[]{:S(2)}) collective-permute-start(bf16[32,768]{1,0:T(8,128)(2,1)S(1)} %slice.95), channel_id=1, source_target_pairs={{0,16},{1,17},{2,18},{3,19},{4,20},{5,21},{6,22},{7,23},{8,24},{9,... | collective-permute-start | bytes 147464 | tf_op jit(solution)/shard_map/ppermute | solution.py:27

commit v2 on v1

v2 whole, which is shorter than its diff:
```python
import functools
import math

import jax
import jax.numpy as jnp
from jax import lax
from jax.experimental import pallas as pl
from jax.experimental.pallas import tpu as pltpu
from jax.sharding import PartitionSpec as P

ROWS, COLS = 16, 32
CHUNKS = 1
F32, BF16 = jnp.float32, jnp.bfloat16
Y_GROUPS = [[y * 4 + low for y in range(4)] for low in range(4)]
X_GROUPS = [[z * 4 + x for x in range(4)] for z in range(8)]


def gelu_value(pre):
    return 0.5 * pre * (1.0 + lax.erf(pre / math.sqrt(2.0)))


def gelu_slope(pre):
    return 0.5 * (1.0 + lax.erf(pre / math.sqrt(2.0))) + pre * jnp.exp(
        -0.5 * pre * pre
    ) / math.sqrt(2.0 * math.pi)


def swap(value, axis, mask):
    size = ROWS if axis == "row" else COLS
    return lax.ppermute(value, axis, [(i, i ^ mask) for i in range(size)])


def spread(value, axis, groups):
    return lax.all_to_all(
        value, axis, split_axis=0, concat_axis=0, axis_index_groups=groups, tiled=True
    )


def row_place(block, me_row):
    owner = block >> 1
    return (((owner ^ me_row) & 1) * 8 + (owner >> 1)) * 2 + (block & 1)


def up_kernel(me, own, x1, x2, x3, w, _, send, keep, acts):
    me_row, me_col = me[0], me[1]
    part = own.shape[0] // 8
    for kx, piece in enumerate((own, x1, x2, x3)):
        for k in range(4):
            for j in range(2):
                block = me_col ^ (kx + 4 * k + 16 * j)
                to = pl.multiple_of(row_place(block, me_row) * part, part)
                acts[pl.ds(to, part), :] = piece[pl.ds((k * 2 + j) * part, part), :]
    half = acts.shape[0] // 2
    step = min(half, 256)
    for i in range(half // step):
        rows = pl.ds(i * step, step)
        send[rows, :] = jnp.dot(
            acts[pl.ds(half + i * step, step), :], w[...], preferred_element_type=F32
        ).astype(BF16)
    for i in range(half // step):
        rows = pl.ds(i * step, step)
        keep[rows, :] = jnp.dot(acts[rows, :], w[...], preferred_element_type=F32)


def down_kernel(me, g0, g1, w, out, held):
    me_row, me_col = me[0], me[1]
    part = g0.shape[0] // 16
    for c, piece in enumerate((g0, g1)):
        for yz in range(8):
            for lo in range(2):
                owner = yz * 2 + ((me_row & 1) ^ c)
                block = owner * 2 + lo
                rel = block ^ me_col
                x, k, j = block & 3, (rel >> 2) & 3, rel >> 4
                to = pl.multiple_of(((x * 4 + k) * 2 + j) * part, part)
                held[pl.ds(to, part), :] = piece[pl.ds((yz * 2 + lo) * part, part), :]
    step = 256
    for i in range(out.shape[0] // step):
        rows = pl.ds(i * step, step)
        out[rows, :] = lax.dot_general(
            held[rows, :], w[...], (((1,), (1,)), ((), ())), preferred_element_type=F32
        ).astype(BF16)


def call(kernel, outs, scratch, flops, *args):
    vmem = pl.BlockSpec(memory_space=pltpu.VMEM)
    return pl.pallas_call(
        kernel,
        out_shape=outs,
        in_specs=[pl.BlockSpec(memory_space=pltpu.SMEM)] + [vmem] * (len(args) - 1),
        out_specs=[vmem] * len(outs),
        scratch_shapes=scratch,
        compiler_params=pltpu.CompilerParams(vmem_limit_bytes=32 * 1024 * 1024),
        cost_estimate=pl.CostEstimate(
            flops=flops, bytes_accessed=6 * 1024 * 1024, transcendentals=0
        ),
    )(*args)


def total(parts):
    parts = [p.astype(F32) for p in parts]
    return functools.reduce(lambda a, b: a + b, parts)


def shards(acts, weight, cotangent):
    row, col = lax.axis_index("row"), lax.axis_index("col")
    me = jnp.stack([row, col]).astype(jnp.int32)
    high = ((row >> 1) & 1) == 1
    part, depth = acts.shape
    width = weight.shape[1]
    tokens = part * COLS

    pair = jnp.concatenate([acts, swap(acts, "col", 16)])
    line = jnp.concatenate([pair] + [swap(pair, "col", 4 * k) for k in (1, 2, 3)])
    x3 = swap(line, "col", 3)
    x2 = swap(line, "col", 2)
    x1 = swap(line, "col", 1)
    other = swap(cotangent, "row", 2)

    flops = 2 * tokens * depth * width
    send, keep, acts_full = call(
        up_kernel,
        [
            jax.ShapeDtypeStruct((tokens // 2, width), BF16),
            jax.ShapeDtypeStruct((tokens // 2, width), F32),
            jax.ShapeDtypeStruct((tokens, depth), BF16),
        ],
        [],
        flops,
        me, line, x1, x2, x3, weight, other,
    )

    mine = (keep + swap(send, "row", 1).astype(F32)).astype(BF16)
    size = tokens // 8
    got = spread(mine, "row", Y_GROUPS)
    mine = total([got[y * size : (y + 1) * size] for y in range(4)])
    pre = mine + swap(mine.astype(BF16), "row", 2).astype(F32)

    size = tokens // 16
    both = jnp.concatenate(
        [jnp.where(high, other, cotangent), jnp.where(high, cotangent, other)]
    )
    output = gelu_value(jnp.where(high, pre[size:], pre[:size])).astype(BF16)
    grad = (both.astype(F32) * gelu_slope(pre)).astype(BF16)

    g0 = lax.all_gather(grad, "row", axis=0, tiled=True, axis_index_groups=Y_GROUPS)
    g1 = swap(g0, "row", 1)

    (partial,) = call(
        down_kernel,
        [jax.ShapeDtypeStruct((tokens, depth), BF16)],
        [pltpu.VMEM((tokens, width), BF16)],
        flops,
        me, g0, g1, weight,
    )

    size = tokens // 4
    got = spread(partial, "col", X_GROUPS)
    mine = total([got[x * size : (x + 1) * size] for x in range(4)])
    size = tokens // 16
    sent = [mine[k * size : (k + 1) * size].astype(BF16) for k in (1, 2, 3)]
    got = [swap(s, "col", 4 * k) for s, k in zip(sent, (1, 2, 3))]
    mine = total([mine[:size]] + got)
    size = tokens // 32
    acts_grad = total([mine[:size], swap(mine[size:].astype(BF16), "col", 16)]).astype(BF16)

    grad_full = jnp.concatenate([g0, g1])
    weight_sum = lax.dot_general(
        acts_full, grad_full, (((0,), (0,)), ((), ())), preferred_element_type=F32
    )
    weight_grad = (weight_sum * tokens ** (-0.5)).astype(BF16)
    return (output, acts_grad, weight_grad)


def solution(mesh):
    in_specs = (P("col", "row"), P("row", "col"), P("row", "col"))
    out_specs = (P("row", "col"), P("col", "row"), P("row", "col"))
    return jax.shard_map(shards, mesh=mesh, in_specs=in_specs, out_specs=out_specs, check_vma=False)
```

time: 195 us -> 184 us (0.944); the launches traced: 194 us -> 180 us
  blocking collectives: 0 us -> 34 us
  waiting for transfers between devices: 70.3 us -> 37.4 us
  starting transfers between devices: 112 us -> 96.4 us
    ppermute x24 -> x15, waiting for transfers between devices: 70.3 us -> 25.7 us  [swap(): return lax.ppermute(value, axis, [(i, i ^ mask) for i in range(size)])]
    all_to_all x0 -> x1, blocking collectives: none -> 23.3 us  [spread(): lax.all_to_all(value, axis, split_axis=0, concat_axis=0, axis_index_group...]
    ppermute x24 -> x15, starting transfers between devices: 112 us -> 92.1 us  [swap(): return lax.ppermute(value, axis, [(i, i ^ mask) for i in range(size)])]
    all_to_all x0 -> x1, waiting for transfers between devices: none -> 11.7 us  [spread(): lax.all_to_all(value, axis, split_axis=0, concat_axis=0, axis_index_group...]
    all_gather x0 -> x1, blocking collectives: none -> 10.7 us  [shards(): lax.all_gather(grad, 'row', axis=0, tiled=True, axis_index_groups=Y_GROUPS)]
    all_to_all x0 -> x1, starting transfers between devices: none -> 4.31 us  [spread(): lax.all_to_all(value, axis, split_axis=0, concat_axis=0, axis_index_group...]
  transfers between devices with their start and end apart: 24 -> 16, of which waited for: 16 -> 10; matrix products, arithmetic and copies ran while one was open for 2% -> 2% of each run, Pallas kernels for 0% -> 0%
where the time goes in v2:
time: 184 us; the launch traced here: 180 us
  starting transfers between devices  96.4 us (52%)
  waiting for transfers between devices  37.4 us (20%)
  blocking collectives  34 us (18%)
  Pallas kernels  4.05 us (2%)
  other arithmetic  3.13 us (2%)
  matrix products  2.47 us (1%)
  local copies, waits for them, and re-layouts  2.16 us (1%)
    ppermute x15, starting transfers between devices, swap(): return lax.ppermute(value, axis, [(i, i ^ mask) for i in range(size)])  92.1 us
    ppermute x15, waiting for transfers between devices, swap(): return lax.ppermute(value, axis, [(i, i ^ mask) for i in range(size)])  25.7 us
    all_to_all x1, blocking collectives, spread(): lax.all_to_all(value, axis, split_axis=0, concat_axis=0, axis_index_group...  23.3 us
    all_to_all x1, waiting for transfers between devices, spread(): lax.all_to_all(value, axis, split_axis=0, concat_axis=0, axis_index_group...  11.7 us
    all_gather x1, blocking collectives, shards(): lax.all_gather(grad, 'row', axis=0, tiled=True, axis_index_groups=Y_GROUPS)  10.7 us
    all_to_all x1, starting transfers between devices, spread(): lax.all_to_all(value, axis, split_axis=0, concat_axis=0, axis_index_group...  4.31 us
    pallas_call x2, Pallas kernels, call(): pl.pallas_call(kernel, out_shape=outs, in_specs=[pl.BlockSpec(memory_spac...  4.05 us
  transfers between devices with their start and end apart: 16, of which 10 were waited for; matrix products, arithmetic and copies ran while one was open for 2% of the time, Pallas kernels for 0%

profile of v2, /device:TPU:1, one launch (start us, length us, event | category | flops | bytes accessed | tf_op | source)
XLA Modules:
  0.0 180.4 jit_solution(4337074426275950377)
XLA Ops:
  0.6 9.6 %collective-permute-start = (bf16[32,768]{1,0:T(8,128)(2,1)}, bf16[32,768]{1,0:T(8,128)(2,1)S(1)}, u32[]{:S(2)}, u32[]{:S(2)}) collective-permute-start(bf16[32,768]{1,0:T(8,128)(2,1)} %param.3), channel_id=1, source_target_pairs={{0,16},{1,17},{2,18},{3,19},{4,20},{5,21},{6,22},{7,23},{8,24},{9,... | collective-permute-start | bytes 147464 | tf_op jit(solution)/shard_map/ppermute | solution.py:30
  12.0 3.5 %collective-permute-start.1 = (bf16[64,768]{1,0:T(8,128)(2,1)S(1)}, bf16[64,768]{1,0:T(8,128)(2,1)S(1)}, u32[]{:S(2)}, u32[]{:S(2)}) collective-permute-start(bf16[64,768]{1,0:T(8,128)(2,1)S(1)} %get-tuple-element.18), channel_id=1, source_target_pairs={{0,4},{1,5},{2,6},{3,7},{4,0},{5,1},{6,2},{7,3},{8,12},{9,13},{10,... | collective-permute-start | bytes 294920 | tf_op jit(solution)/shard_map/ppermute | solution.py:30
  15.5 6.6 %collective-permute-start.2 = (bf16[64,768]{1,0:T(8,128)(2,1)S(1)}, bf16[64,768]{1,0:T(8,128)(2,1)S(1)}, u32[]{:S(2)}, u32[]{:S(2)}) collective-permute-start(bf16[64,768]{1,0:T(8,128)(2,1)S(1)} %get-tuple-element.18), channel_id=1, source_target_pairs={{0,8},{1,9},{2,10},{3,11},{4,12},{5,13},{6,14},{7,15},{8,0},{9,1},... | collective-permute-start | bytes 294920 | tf_op jit(solution)/shard_map/ppermute | solution.py:30
  22.1 1.9 %collective-permute-start.3 = (bf16[64,768]{1,0:T(8,128)(2,1)S(1)}, bf16[64,768]{1,0:T(8,128)(2,1)S(1)}, u32[]{:S(2)}, u32[]{:S(2)}) collective-permute-start(bf16[64,768]{1,0:T(8,128)(2,1)S(1)} %get-tuple-element.18), channel_id=1, source_target_pairs={{0,12},{1,13},{2,14},{3,15},{4,8},{5,9},{6,10},{7,11},{8,4},{9,5},... | collective-permute-start | bytes 294920 | tf_op jit(solution)/shard_map/ppermute | solution.py:30
  24.1 1.0 collective-permute-done.2
  25.1 4.4 %collective-permute-done.3 = bf16[64,768]{1,0:T(8,128)(2,1)S(1)} collective-permute-done((bf16[64,768]{1,0:T(8,128)(2,1)S(1)}, bf16[64,768]{1,0:T(8,128)(2,1)S(1)}, u32[]{:S(2)}, u32[]{:S(2)}) %collective-permute-start.3) | collective-permute-done | bytes 98336 | tf_op jit(solution)/shard_map/ppermute | solution.py:30
  29.5 3.1 %collective-permute-start.4 = (bf16[256,768]{1,0:T(8,128)(2,1)S(1)}, bf16[256,768]{1,0:T(8,128)(2,1)S(1)}, u32[]{:S(2)}, u32[]{:S(2)}) collective-permute-start(bf16[256,768]{1,0:T(8,128)(2,1)S(1)} %constant_dynamic-update-slice_fusion.2.own), channel_id=1, source_target_pairs={{0,1},{1,0},{2,3},{3,2},{4,5},{5,4},{6,7},{7,6},{8,9},{9,8},{10,11... | collective-permute-start | bytes 1179656 | tf_op jit(solution)/shard_map/ppermute | solution.py:30
  32.6 4.4 %collective-permute-start.5 = (bf16[256,768]{1,0:T(8,128)(2,1)S(1)}, bf16[256,768]{1,0:T(8,128)(2,1)S(1)}, u32[]{:S(2)}, u32[]{:S(2)}) collective-permute-start(bf16[256,768]{1,0:T(8,128)(2,1)S(1)} %constant_dynamic-update-slice_fusion.2.own), channel_id=1, source_target_pairs={{0,2},{1,3},{2,0},{3,1},{4,6},{5,7},{6,4},{7,5},{8,10},{9,11},{10,... | collective-permute-start | bytes 1179656 | tf_op jit(solution)/shard_map/ppermute | solution.py:30
  36.9 2.1 %collective-permute-start.6 = (bf16[256,768]{1,0:T(8,128)(2,1)S(1)}, bf16[256,768]{1,0:T(8,128)(2,1)S(1)}, u32[]{:S(2)}, u32[]{:S(2)}) collective-permute-start(bf16[256,768]{1,0:T(8,128)(2,1)S(1)} %constant_dynamic-update-slice_fusion.2.own), channel_id=1, source_target_pairs={{0,3},{1,2},{2,1},{3,0},{4,7},{5,6},{6,5},{7,4},{8,11},{9,10},{10,... | collective-permute-start | bytes 1179656 | tf_op jit(solution)/shard_map/ppermute | solution.py:30
  39.1 9.7 %collective-permute-start.7 = (bf16[64,768]{1,0:T(8,128)(2,1)}, bf16[64,768]{1,0:T(8,128)(2,1)S(1)}, u32[]{:S(2)}, u32[]{:S(2)}) collective-permute-start(bf16[64,768]{1,0:T(8,128)(2,1)} %param.5), channel_id=1, source_target_pairs={{0,64},{32,96},{64,0},{96,32},{128,192},{160,224},{192,128},{224,1... | collective-permute-start | bytes 294920 | tf_op jit(solution)/shard_map/ppermute | solution.py:30
  48.9 4.6 %collective-permute-done.7._ = bf16[64,768]{1,0:T(8,128)(2,1)S(1)} collective-permute-done((bf16[64,768]{1,0:T(8,128)(2,1)}, bf16[64,768]{1,0:T(8,128)(2,1)S(1)}, u32[]{:S(2)}, u32[]{:S(2)}) %collective-permute-start.7) | collective-permute-done | bytes 98336 | tf_op jit(solution)/shard_map/ppermute | solution.py:30
  53.4 3.9 %collective-permute-done.6.x3 = bf16[256,768]{1,0:T(8,128)(2,1)S(1)} collective-permute-done((bf16[256,768]{1,0:T(8,128)(2,1)S(1)}, bf16[256,768]{1,0:T(8,128)(2,1)S(1)}, u32[]{:S(2)}, u32[]{:S(2)}) %collective-permute-start.6) | collective-permute-done | bytes 393248 | tf_op jit(solution)/shard_map/ppermute | solution.py:30
  57.3 1.3 copy-done
  58.6 2.0 %shard_map.58 = (bf16[512,768]{1,0:T(8,128)(2,1)S(1)}, f32[512,768]{1,0:T(8,128)S(1)}, bf16[1024,768]{1,0:T(8,128)(2,1)S(1)}) custom-call(s32[2]{0:T(128)S(1)} %pad_add_fusion.me, bf16[256,768]{1,0:T(8,128)(2,1)S(1)} %constant_dynamic-update-slice_fusion.2.own, bf16[256,768]{1,0:T(8,128)(2,1)S(1)} %collective-permute-done.4.x1, ...), custom_call_target="tpu_custom_call" | custom-call | flops 1207959552 | bytes 6291456 | tf_op jit(solution)/shard_map/pallas_call | solution.py:87
  60.6 4.1 %collective-permute-start.8 = (bf16[512,768]{1,0:T(8,128)(2,1)S(1)}, bf16[512,768]{1,0:T(8,128)(2,1)S(1)}, u32[]{:S(2)}, u32[]{:S(2)}) collective-permute-start(bf16[512,768]{1,0:T(8,128)(2,1)S(1)} %get-tuple-element.7), channel_id=1, source_target_pairs={{0,32},{32,0},{64,96},{96,64},{128,160},{160,128},{192,224},{224,1... | collective-permute-start | bytes 2359304 | tf_op jit(solution)/shard_map/ppermute | solution.py:30
  64.7 1.9 %collective-permute-done.8 = bf16[512,768]{1,0:T(8,128)(2,1)S(1)} collective-permute-done((bf16[512,768]{1,0:T(8,128)(2,1)S(1)}, bf16[512,768]{1,0:T(8,128)(2,1)S(1)}, u32[]{:S(2)}, u32[]{:S(2)}) %collective-permute-start.8) | collective-permute-done | bytes 786464 | tf_op jit(solution)/shard_map/ppermute | solution.py:30
  66.6 1.1 add_convert_fusion
  67.7 4.3 %all-to-all-start = ((bf16[4,128,768]{2,1,0:T(8,128)(2,1)}), bf16[4,128,768]{2,1,0:T(8,128)(2,1)S(1)}, u32[]{:S(2)}, u32[]{:S(2)}) async-start(bf16[4,128,768]{2,1,0:T(8,128)(2,1)} %bitcast.2), calls=%async_computation | async-start | bytes 1572864 | tf_op jit(solution)/shard_map/all_to_all | solution.py:34
  72.0 11.7 %all-to-all-done = bf16[4,128,768]{2,1,0:T(8,128)(2,1)S(1)} async-done(((bf16[4,128,768]{2,1,0:T(8,128)(2,1)}), bf16[4,128,768]{2,1,0:T(8,128)(2,1)S(1)}, u32[]{:S(2)}, u32[]{:S(2)}) %all-to-all-start) | async-done | bytes 786464 | tf_op jit(solution)/shard_map/all_to_all | solution.py:34
  83.8 11.8 %collective-permute-start.9 = (bf16[128,768]{1,0:T(8,128)(2,1)S(1)}, bf16[128,768]{1,0:T(8,128)(2,1)S(1)}, u32[]{:S(2)}, u32[]{:S(2)}) collective-permute-start(bf16[128,768]{1,0:T(8,128)(2,1)S(1)} %bitcast_convert_fusion), channel_id=1, source_target_pairs={{0,64},{32,96},{64,0},{96,32},{128,192},{160,224},{192,128},{224,1... | collective-permute-start | bytes 589832 | tf_op jit(solution)/shard_map/ppermute | solution.py:30
  95.7 3.7 %collective-permute-done.9 = bf16[128,768]{1,0:T(8,128)(2,1)S(1)} collective-permute-done((bf16[128,768]{1,0:T(8,128)(2,1)S(1)}, bf16[128,768]{1,0:T(8,128)(2,1)S(1)}, u32[]{:S(2)}, u32[]{:S(2)}) %collective-permute-start.9) | collective-permute-done | bytes 196640 | tf_op jit(solution)/shard_map/ppermute | solution.py:30
  99.7 10.7 %all_gather.3.g0 = bf16[512,768]{1,0:T(8,128)(2,1)S(1)} all-gather(bf16[128,768]{1,0:T(8,128)(2,1)S(1)} %get-tuple-element.11), channel_id=1, replica_groups={{0,128,256,384},{32,160,288,416},{64,192,320,448},{96,224,352,480},{1,1..., dimensions={0}, use_global_device_ids=true | all-gather | bytes 983040 | tf_op jit(solution)/shard_map/all_gather | solution.py:146
  110.4 12.7 %collective-permute-start.10 = (bf16[512,768]{1,0:T(8,128)(2,1)S(1)}, bf16[512,768]{1,0:T(8,128)(2,1)S(1)}, u32[]{:S(2)}, u32[]{:S(2)}) collective-permute-start(bf16[512,768]{1,0:T(8,128)(2,1)S(1)} %all_gather.3.g0), channel_id=1, source_target_pairs={{0,32},{32,0},{64,96},{96,64},{128,160},{160,128},{192,224},{224,1... | collective-permute-start | bytes 2359304 | tf_op jit(solution)/shard_map/ppermute | solution.py:30
  123.2 1.9 %collective-permute-done.10.g1 = bf16[512,768]{1,0:T(8,128)(2,1)S(1)} collective-permute-done((bf16[512,768]{1,0:T(8,128)(2,1)S(1)}, bf16[512,768]{1,0:T(8,128)(2,1)S(1)}, u32[]{:S(2)}, u32[]{:S(2)}) %collective-permute-start.10) | collective-permute-done | bytes 786464 | tf_op jit(solution)/shard_map/ppermute | solution.py:30
  125.0 2.0 %shard_map.59 = bf16[1024,768]{1,0:T(8,128)(2,1)S(1)} custom-call(s32[2]{0:T(128)S(1)} %pad_add_fusion.me, bf16[512,768]{1,0:T(8,128)(2,1)S(1)} %all_gather.3.g0, bf16[512,768]{1,0:T(8,128)(2,1)S(1)} %collective-permute-done.10.g1, bf16[768,768]{1,0:T(8,128)(2,1)S(1)} %copy-done.1), custom_call_target="tpu_custom_call" | custom-call | flops 1207959552 | bytes 6291456 | tf_op jit(solution)/shard_map/pallas_call | solution.py:87
  127.1 23.3 %all_to_all.18 = bf16[4,256,768]{2,1,0:T(8,128)(2,1)S(1)} all-to-all(bf16[4,256,768]{2,1,0:T(8,128)(2,1)S(1)} %bitcast.23), channel_id=1, replica_groups={{0,1,2,3},{4,5,6,7},{8,9,10,11},{12,13,14,15},{16,17,18,19},{20,21,22,2..., dimensions={0} | all-to-all | bytes 3145728 | tf_op jit(solution)/shard_map/all_to_all | solution.py:34
  150.6 2.5 %collective-permute-start.11 = (bf16[64,768]{1,0:T(8,128)(2,1)S(1)}, bf16[64,768]{1,0:T(8,128)(2,1)S(1)}, u32[]{:S(2)}, u32[]{:S(2)}) collective-permute-start(bf16[64,768]{1,0:T(8,128)(2,1)S(1)} %get-tuple-element.13), channel_id=1, source_target_pairs={{0,4},{1,5},{2,6},{3,7},{4,0},{5,1},{6,2},{7,3},{8,12},{9,13},{10,... | collective-permute-start | bytes 294920 | tf_op jit(solution)/shard_map/ppermute | solution.py:30
  153.1 8.3 %collective-permute-start.12 = (bf16[64,768]{1,0:T(8,128)(2,1)S(1)}, bf16[64,768]{1,0:T(8,128)(2,1)S(1)}, u32[]{:S(2)}, u32[]{:S(2)}) collective-permute-start(bf16[64,768]{1,0:T(8,128)(2,1)S(1)} %get-tuple-element.15), channel_id=1, source_target_pairs={{0,8},{1,9},{2,10},{3,11},{4,12},{5,13},{6,14},{7,15},{8,0},{9,1},... | collective-permute-start | bytes 294920 | tf_op jit(solution)/shard_map/ppermute | solution.py:30
  161.5 3.1 %collective-permute-start.13 = (bf16[64,768]{1,0:T(8,128)(2,1)S(1)}, bf16[64,768]{1,0:T(8,128)(2,1)S(1)}, u32[]{:S(2)}, u32[]{:S(2)}) collective-permute-start(bf16[64,768]{1,0:T(8,128)(2,1)S(1)} %get-tuple-element.14), channel_id=1, source_target_pairs={{0,12},{1,13},{2,14},{3,15},{4,8},{5,9},{6,10},{7,11},{8,4},{9,5},... | collective-permute-start | bytes 294920 | tf_op jit(solution)/shard_map/ppermute | solution.py:30
  165.3 3.5 %collective-permute-done.13 = bf16[64,768]{1,0:T(8,128)(2,1)S(1)} collective-permute-done((bf16[64,768]{1,0:T(8,128)(2,1)S(1)}, bf16[64,768]{1,0:T(8,128)(2,1)S(1)}, u32[]{:S(2)}, u32[]{:S(2)}) %collective-permute-start.13) | collective-permute-done | bytes 98336 | tf_op jit(solution)/shard_map/ppermute | solution.py:30
  168.8 8.6 %collective-permute-start.14 = (bf16[32,768]{1,0:T(8,128)(2,1)S(1)}, bf16[32,768]{1,0:T(8,128)(2,1)S(1)}, u32[]{:S(2)}, u32[]{:S(2)}) collective-permute-start(bf16[32,768]{1,0:T(8,128)(2,1)S(1)} %slice.152), channel_id=1, source_target_pairs={{0,16},{1,17},{2,18},{3,19},{4,20},{5,21},{6,22},{7,23},{8,24},{9,... | collective-permute-start | bytes 147464 | tf_op jit(solution)/shard_map/ppermute | solution.py:30
  177.3 2.5 %multiply_convert_fusion = bf16[768,768]{1,0:T(8,128)(2,1)} fusion(bf16[1024,768]{1,0:T(8,128)(2,1)S(1)} %get-tuple-element.8, bf16[512,768]{1,0:T(8,128)(2,1)S(1)} %collective-permute-done.10.g1, bf16[512,768]{1,0:T(8,128)(2,1)S(1)} %all_gather.3.g0), kind=kOutput, calls=%fused_computation | convolution fusion | flops 1212284928 | bytes 4325376 | tf_op jit(solution)/shard_map/dot_general | solution.py:168
  (27 shorter events, 3.8 us)
Async XLA Ops:
  0.6 11.3 %collective-permute-start = (bf16[32,768]{1,0:T(8,128)(2,1)}, bf16[32,768]{1,0:T(8,128)(2,1)S(1)}, u32[]{:S(2)}, u32[]{:S(2)}) collective-permute-start(bf16[32,768]{1,0:T(8,128)(2,1)} %param.3), channel_id=1, source_target_pairs={{0,16},{1,17},{2,18},{3,19},{4,20},{5,21},{6,22},{7,23},{8,24},{9,... | collective-permute-start | bytes 147464 | tf_op jit(solution)/shard_map/ppermute | solution.py:30
  12.0 12.1 %collective-permute-start.1 = (bf16[64,768]{1,0:T(8,128)(2,1)S(1)}, bf16[64,768]{1,0:T(8,128)(2,1)S(1)}, u32[]{:S(2)}, u32[]{:S(2)}) collective-permute-start(bf16[64,768]{1,0:T(8,128)(2,1)S(1)} %get-tuple-element.18), channel_id=1, source_target_pairs={{0,4},{1,5},{2,6},{3,7},{4,0},{5,1},{6,2},{7,3},{8,12},{9,13},{10,... | collective-permute-start | bytes 294920 | tf_op jit(solution)/shard_map/ppermute | solution.py:30
  15.5 9.6 %collective-permute-start.2 = (bf16[64,768]{1,0:T(8,128)(2,1)S(1)}, bf16[64,768]{1,0:T(8,128)(2,1)S(1)}, u32[]{:S(2)}, u32[]{:S(2)}) collective-permute-start(bf16[64,768]{1,0:T(8,128)(2,1)S(1)} %get-tuple-element.18), channel_id=1, source_target_pairs={{0,8},{1,9},{2,10},{3,11},{4,12},{5,13},{6,14},{7,15},{8,0},{9,1},... | collective-permute-start | bytes 294920 | tf_op jit(solution)/shard_map/ppermute | solution.py:30
  22.1 7.3 %collective-permute-start.3 = (bf16[64,768]{1,0:T(8,128)(2,1)S(1)}, bf16[64,768]{1,0:T(8,128)(2,1)S(1)}, u32[]{:S(2)}, u32[]{:S(2)}) collective-permute-start(bf16[64,768]{1,0:T(8,128)(2,1)S(1)} %get-tuple-element.18), channel_id=1, source_target_pairs={{0,12},{1,13},{2,14},{3,15},{4,8},{5,9},{6,10},{7,11},{8,4},{9,5},... | collective-permute-start | bytes 294920 | tf_op jit(solution)/shard_map/ppermute | solution.py:30
  29.5 24.0 %collective-permute-start.4 = (bf16[256,768]{1,0:T(8,128)(2,1)S(1)}, bf16[256,768]{1,0:T(8,128)(2,1)S(1)}, u32[]{:S(2)}, u32[]{:S(2)}) collective-permute-start(bf16[256,768]{1,0:T(8,128)(2,1)S(1)} %constant_dynamic-update-slice_fusion.2.own), channel_id=1, source_target_pairs={{0,1},{1,0},{2,3},{3,2},{4,5},{5,4},{6,7},{7,6},{8,9},{9,8},{10,11... | collective-permute-start | bytes 1179656 | tf_op jit(solution)/shard_map/ppermute | solution.py:30
  32.6 20.9 %collective-permute-start.5 = (bf16[256,768]{1,0:T(8,128)(2,1)S(1)}, bf16[256,768]{1,0:T(8,128)(2,1)S(1)}, u32[]{:S(2)}, u32[]{:S(2)}) collective-permute-start(bf16[256,768]{1,0:T(8,128)(2,1)S(1)} %constant_dynamic-update-slice_fusion.2.own), channel_id=1, source_target_pairs={{0,2},{1,3},{2,0},{3,1},{4,6},{5,7},{6,4},{7,5},{8,10},{9,11},{10,... | collective-permute-start | bytes 1179656 | tf_op jit(solution)/shard_map/ppermute | solution.py:30
  36.9 20.4 %collective-permute-start.6 = (bf16[256,768]{1,0:T(8,128)(2,1)S(1)}, bf16[256,768]{1,0:T(8,128)(2,1)S(1)}, u32[]{:S(2)}, u32[]{:S(2)}) collective-permute-start(bf16[256,768]{1,0:T(8,128)(2,1)S(1)} %constant_dynamic-update-slice_fusion.2.own), channel_id=1, source_target_pairs={{0,3},{1,2},{2,1},{3,0},{4,7},{5,6},{6,5},{7,4},{8,11},{9,10},{10,... | collective-permute-start | bytes 1179656 | tf_op jit(solution)/shard_map/ppermute | solution.py:30
  39.1 14.4 %collective-permute-start.7 = (bf16[64,768]{1,0:T(8,128)(2,1)}, bf16[64,768]{1,0:T(8,128)(2,1)S(1)}, u32[]{:S(2)}, u32[]{:S(2)}) collective-permute-start(bf16[64,768]{1,0:T(8,128)(2,1)} %param.5), channel_id=1, source_target_pairs={{0,64},{32,96},{64,0},{96,32},{128,192},{160,224},{192,128},{224,1... | collective-permute-start | bytes 294920 | tf_op jit(solution)/shard_map/ppermute | solution.py:30
  57.3 1.3 copy-start
  60.6 6.0 %collective-permute-start.8 = (bf16[512,768]{1,0:T(8,128)(2,1)S(1)}, bf16[512,768]{1,0:T(8,128)(2,1)S(1)}, u32[]{:S(2)}, u32[]{:S(2)}) collective-permute-start(bf16[512,768]{1,0:T(8,128)(2,1)S(1)} %get-tuple-element.7), channel_id=1, source_target_pairs={{0,32},{32,0},{64,96},{96,64},{128,160},{160,128},{192,224},{224,1... | collective-permute-start | bytes 2359304 | tf_op jit(solution)/shard_map/ppermute | solution.py:30
  67.7 28.0 %copy-start.2 = (bf16[64,768]{1,0:T(8,128)(2,1)S(1)}, bf16[64,768]{1,0:T(8,128)(2,1)}, u32[]{:S(2)}) copy-start(bf16[64,768]{1,0:T(8,128)(2,1)} %param.5) | copy-start | bytes 294916
  67.7 16.0 %all-to-all-start = ((bf16[4,128,768]{2,1,0:T(8,128)(2,1)}), bf16[4,128,768]{2,1,0:T(8,128)(2,1)S(1)}, u32[]{:S(2)}, u32[]{:S(2)}) async-start(bf16[4,128,768]{2,1,0:T(8,128)(2,1)} %bitcast.2), calls=%async_computation | async-start | bytes 1572864 | tf_op jit(solution)/shard_map/all_to_all | solution.py:34
  83.8 41.2 %copy-start.1 = (bf16[768,768]{1,0:T(8,128)(2,1)S(1)}, bf16[768,768]{1,0:T(8,128)(2,1)}, u32[]{:S(2)}) copy-start(bf16[768,768]{1,0:T(8,128)(2,1)} %w.3) | copy-start | bytes 3538948
  83.8 15.6 %collective-permute-start.9 = (bf16[128,768]{1,0:T(8,128)(2,1)S(1)}, bf16[128,768]{1,0:T(8,128)(2,1)S(1)}, u32[]{:S(2)}, u32[]{:S(2)}) collective-permute-start(bf16[128,768]{1,0:T(8,128)(2,1)S(1)} %bitcast_convert_fusion), channel_id=1, source_target_pairs={{0,64},{32,96},{64,0},{96,32},{128,192},{160,224},{192,128},{224,1... | collective-permute-start | bytes 589832 | tf_op jit(solution)/shard_map/ppermute | solution.py:30
  110.4 14.6 %collective-permute-start.10 = (bf16[512,768]{1,0:T(8,128)(2,1)S(1)}, bf16[512,768]{1,0:T(8,128)(2,1)S(1)}, u32[]{:S(2)}, u32[]{:S(2)}) collective-permute-start(bf16[512,768]{1,0:T(8,128)(2,1)S(1)} %all_gather.3.g0), channel_id=1, source_target_pairs={{0,32},{32,0},{64,96},{96,64},{128,160},{160,128},{192,224},{224,1... | collective-permute-start | bytes 2359304 | tf_op jit(solution)/shard_map/ppermute | solution.py:30
  150.6 14.7 %collective-permute-start.11 = (bf16[64,768]{1,0:T(8,128)(2,1)S(1)}, bf16[64,768]{1,0:T(8,128)(2,1)S(1)}, u32[]{:S(2)}, u32[]{:S(2)}) collective-permute-start(bf16[64,768]{1,0:T(8,128)(2,1)S(1)} %get-tuple-element.13), channel_id=1, source_target_pairs={{0,4},{1,5},{2,6},{3,7},{4,0},{5,1},{6,2},{7,3},{8,12},{9,13},{10,... | collective-permute-start | bytes 294920 | tf_op jit(solution)/shard_map/ppermute | solution.py:30
  153.1 12.1 %collective-permute-start.12 = (bf16[64,768]{1,0:T(8,128)(2,1)S(1)}, bf16[64,768]{1,0:T(8,128)(2,1)S(1)}, u32[]{:S(2)}, u32[]{:S(2)}) collective-permute-start(bf16[64,768]{1,0:T(8,128)(2,1)S(1)} %get-tuple-element.15), channel_id=1, source_target_pairs={{0,8},{1,9},{2,10},{3,11},{4,12},{5,13},{6,14},{7,15},{8,0},{9,1},... | collective-permute-start | bytes 294920 | tf_op jit(solution)/shard_map/ppermute | solution.py:30
  161.5 7.3 %collective-permute-start.13 = (bf16[64,768]{1,0:T(8,128)(2,1)S(1)}, bf16[64,768]{1,0:T(8,128)(2,1)S(1)}, u32[]{:S(2)}, u32[]{:S(2)}) collective-permute-start(bf16[64,768]{1,0:T(8,128)(2,1)S(1)} %get-tuple-element.14), channel_id=1, source_target_pairs={{0,12},{1,13},{2,14},{3,15},{4,8},{5,9},{6,10},{7,11},{8,4},{9,5},... | collective-permute-start | bytes 294920 | tf_op jit(solution)/shard_map/ppermute | solution.py:30
  168.8 11.0 %collective-permute-start.14 = (bf16[32,768]{1,0:T(8,128)(2,1)S(1)}, bf16[32,768]{1,0:T(8,128)(2,1)S(1)}, u32[]{:S(2)}, u32[]{:S(2)}) collective-permute-start(bf16[32,768]{1,0:T(8,128)(2,1)S(1)} %slice.152), channel_id=1, source_target_pairs={{0,16},{1,17},{2,18},{3,19},{4,20},{5,21},{6,22},{7,23},{8,24},{9,... | collective-permute-start | bytes 147464 | tf_op jit(solution)/shard_map/ppermute | solution.py:30

commit v3 on v0

v3 whole, which is shorter than its diff:
```python
import functools
import math

import jax
import jax.numpy as jnp
from jax import lax
from jax.experimental import pallas as pl
from jax.experimental.pallas import tpu as pltpu
from jax.sharding import PartitionSpec as P

ROWS, COLS = 16, 32
F32, BF16 = jnp.float32, jnp.bfloat16
Y_GROUPS = [[y * 4 + low for y in range(4)] for low in range(4)]
Z_GROUPS = [[(h * 4 + z) * 4 + x for z in range(4)] for h in range(2) for x in range(4)]


def gelu_value(pre):
    return 0.5 * pre * (1.0 + lax.erf(pre / math.sqrt(2.0)))


def gelu_slope(pre):
    return 0.5 * (1.0 + lax.erf(pre / math.sqrt(2.0))) + pre * jnp.exp(
        -0.5 * pre * pre
    ) / math.sqrt(2.0 * math.pi)


def swap(value, axis, mask):
    size = ROWS if axis == "row" else COLS
    return lax.ppermute(value, axis, [(i, i ^ mask) for i in range(size)])


def spread(value, axis, groups):
    return lax.all_to_all(
        value, axis, split_axis=0, concat_axis=0, axis_index_groups=groups, tiled=True
    )


def total(parts):
    parts = [p.astype(F32) for p in parts]
    return functools.reduce(lambda a, b: a + b, parts)


def line_place(z, me_col):
    return (z & 3) * 2 + ((z >> 2) ^ (me_col >> 4))


def own_first(me):
    return ((me[0] ^ (me[1] >> 1)) & 1) == 0


def products(me, piece, weights, held, out):
    part = held.shape[0] // 8
    for z in range(8):
        src = pl.multiple_of(line_place(z, me[1]) * part, part)
        held[pl.ds(z * part, part), :] = piece[pl.ds(src, part), :]
    for block, w in enumerate(weights):
        value = jnp.dot(held[...], w[...], preferred_element_type=F32)
        for z in range(8):
            out[pl.ds((z * 2 + block) * part, part), :] = value[z * part : (z + 1) * part]


def early_kernel(me, piece, w0, w1, out, held):
    products(me, piece, (w0, w1), held, out)


def send_kernel(me, early, piece, _, w0, w1, late, send, held):
    products(me, piece, (w0, w1), held, late)

    @pl.when(own_first(me))
    def _():
        send[...] = late[...].astype(BF16)

    @pl.when(jnp.logical_not(own_first(me)))
    def _():
        send[...] = early[...].astype(BF16)


def keep_kernel(me, early, late, got, out):
    @pl.when(own_first(me))
    def _():
        out[...] = (early[...] + got[...].astype(F32)).astype(BF16)

    @pl.when(jnp.logical_not(own_first(me)))
    def _():
        out[...] = (late[...] + got[...].astype(F32)).astype(BF16)


def order_kernel(me, line, across, out):
    half = line.shape[0]
    part = half // 8
    swapped = (me[0] ^ (me[1] >> 1)) & 1
    for s, piece in enumerate((line, across)):
        for z in range(8):
            src = pl.multiple_of(line_place(z, me[1]) * part, part)
            to = pl.multiple_of((s ^ swapped) * half + z * part, part)
            out[pl.ds(to, part), :] = piece[pl.ds(src, part), :]


def back(me, grad, weights, held):
    size = held.shape[1]
    part = size // 8
    for z in range(8):
        to = pl.multiple_of(line_place(z, me[1]) * part, part)
        for block in range(2):
            held[block, pl.ds(to, part), :] = grad[pl.ds((z * 2 + block) * part, part), :]
    values = [
        lax.dot_general(
            held[block], w[...], (((1,), (1,)), ((), ())), preferred_element_type=F32
        )
        for block, w in enumerate(weights)
    ]
    return values[0] + values[1]


def first_kernel(me, grad, _, w0, w1, out, held):
    out[...] = back(me, grad, (w0, w1), held)


def second_kernel(me, first, grad, w0, w1, keep, send, held):
    value = back(me, grad, (w0, w1), held)

    @pl.when(own_first(me))
    def _():
        keep[...] = first[...]
        send[...] = value.astype(BF16)

    @pl.when(jnp.logical_not(own_first(me)))
    def _():
        keep[...] = value
        send[...] = first[...].astype(BF16)


def call(kernel, outs, scratch, flops, *args):
    vmem = pl.BlockSpec(memory_space=pltpu.VMEM)
    return pl.pallas_call(
        kernel,
        out_shape=outs,
        in_specs=[pl.BlockSpec(memory_space=pltpu.SMEM)] + [vmem] * (len(args) - 1),
        out_specs=[vmem] * len(outs),
        scratch_shapes=scratch,
        compiler_params=pltpu.CompilerParams(vmem_limit_bytes=32 * 1024 * 1024),
        cost_estimate=pl.CostEstimate(
            flops=flops, bytes_accessed=3 * 1024 * 1024, transcendentals=0
        ),
    )(*args)


def shape(rows, columns, dtype):
    return jax.ShapeDtypeStruct((rows, columns), dtype)


def shards(acts, weight, cotangent):
    row, col = lax.axis_index("row"), lax.axis_index("col")
    me = jnp.stack([row, col]).astype(jnp.int32)
    upper = ((row >> 1) & 1) == 1
    odd = (col & 1) == 1
    part, depth = acts.shape
    width = weight.shape[1]
    tokens = part * COLS
    flops = tokens * depth * width

    pair = jnp.concatenate([acts, swap(acts, "col", 16)])
    partner = swap(weight, "col", 1)
    line = lax.all_gather(pair, "col", axis=0, tiled=True, axis_index_groups=Z_GROUPS)
    across = swap(line, "col", 2)

    other = swap(cotangent, "row", 2)
    low = jnp.stack([jnp.where(upper, x, y) for x, y in ((other, cotangent), (cotangent, other))])
    low, high = low[:, :part], low[:, part:]
    both = [jnp.where(odd, high, low), swap(jnp.where(odd, low, high), "col", 1)]
    both = jnp.stack(both, axis=1).reshape(4 * part, width)

    size = tokens // 2
    held = [pltpu.VMEM((tokens // 4, depth), BF16)]
    (early,) = call(
        early_kernel, [shape(size, width, F32)], held, flops, me, line, weight, partner
    )
    late, send = call(
        send_kernel,
        [shape(size, width, F32), shape(size, width, BF16)],
        held, flops, me, early, across, other, weight, partner,
    )

    (mine,) = call(
        keep_kernel,
        [shape(size, width, BF16)],
        [], size * width, me, early, late, swap(send, "row", 1),
    )
    size = tokens // 8
    got = spread(mine, "row", Y_GROUPS)
    mine = total([got[y * size : (y + 1) * size] for y in range(4)])
    pre = mine + swap(mine.astype(BF16), "row", 2).astype(F32)

    size = tokens // 16
    value = gelu_value(jnp.where(upper, pre[size:], pre[:size])).astype(BF16)
    grad = (both.astype(F32) * gelu_slope(pre)).astype(BF16)
    mine, got = value[:part], swap(value[part:], "col", 1)
    output = jnp.concatenate([jnp.where(odd, got, mine), jnp.where(odd, mine, got)])

    g0 = lax.all_gather(grad, "row", axis=0, tiled=True, axis_index_groups=Y_GROUPS)
    g1 = swap(g0, "row", 1)

    size = tokens // 2
    (near,) = call(order_kernel, [shape(size, depth, BF16)], [], 0, me, line, across)
    far = swap(near, "col", 1)

    size = tokens // 4
    held = [pltpu.VMEM((2, size, width), BF16)]
    (first,) = call(
        first_kernel,
        [shape(size, depth, F32)],
        held, flops, me, g0, far, weight, partner,
    )
    keep, send = call(
        second_kernel,
        [shape(size, depth, F32), shape(size, depth, BF16)],
        held, flops, me, first, g1, weight, partner,
    )

    mine = total([keep, swap(send, "col", 2)]).astype(BF16)
    size = tokens // 16
    got = spread(mine, "col", Z_GROUPS)
    mine = total([got[k * size : (k + 1) * size] for k in range(4)])
    acts_grad = total([mine[:part], swap(mine[part:].astype(BF16), "col", 16)]).astype(BF16)

    split = [g.reshape(8, 2, part, width) for g in (g0, g1)]
    own = [s[:, 0].reshape(-1, width) for s in split]
    others = jnp.concatenate([s[:, 1].reshape(-1, width) for s in split])
    weight_sum = lax.dot_general(
        jnp.concatenate([near, far]),
        jnp.concatenate(own + [swap(others, "col", 1)]),
        (((0,), (0,)), ((), ())),
        preferred_element_type=F32,
    )
    weight_grad = (weight_sum * tokens ** (-0.5)).astype(BF16)
    return (output, acts_grad, weight_grad)


def solution(mesh):
    in_specs = (P("col", "row"), P("row", "col"), P("row", "col"))
    out_specs = (P("row", "col"), P("col", "row"), P("row", "col"))
    return jax.shard_map(shards, mesh=mesh, in_specs=in_specs, out_specs=out_specs, check_vma=False)
```

time: 707 us -> 178 us (0.25)
  the two profiles are of different devices: /device:TPU:16 before, /device:TPU:1 now
where the time goes in v3:
time: 178 us; the launch traced here: 175 us
  starting transfers between devices  92.1 us (52%)
  waiting for transfers between devices  33.9 us (19%)
  blocking collectives  28 us (16%)
  Pallas kernels  7.65 us (4%)
  other arithmetic  6.79 us (4%)
  matrix products  3.69 us (2%)
  local copies, waits for them, and re-layouts  2.21 us (1%)
    ppermute x13, starting transfers between devices, swap(): return lax.ppermute(value, axis, [(i, i ^ mask) for i in range(size)])  74.6 us
    ppermute x13, waiting for transfers between devices, swap(): return lax.ppermute(value, axis, [(i, i ^ mask) for i in range(size)])  21.4 us
    all_to_all x2, starting transfers between devices, spread(): lax.all_to_all(value, axis, split_axis=0, concat_axis=0, axis_index_group...  17.5 us
    all_gather x1, blocking collectives, shards(): lax.all_gather(pair, 'col', axis=0, tiled=True, axis_index_groups=Z_GROUPS)  15.8 us
    all_to_all x2, waiting for transfers between devices, spread(): lax.all_to_all(value, axis, split_axis=0, concat_axis=0, axis_index_group...  12.5 us
    all_gather x1, blocking collectives, shards(): lax.all_gather(grad, 'row', axis=0, tiled=True, axis_index_groups=Y_GROUPS)  12.2 us
    pallas_call x6, Pallas kernels, call(): pl.pallas_call(kernel, out_shape=outs, in_specs=[pl.BlockSpec(memory_spac...  7.65 us
    dot_general x1, matrix products, shards(): lax.dot_general(jnp.concatenate([near, far]), jnp.concatenate(own + [swap...  3.69 us
  transfers between devices with their start and end apart: 15, of which 9 were waited for; matrix products, arithmetic and copies ran while one was open for 6% of the time, Pallas kernels for 2%

profile of v3, /device:TPU:1, one launch (start us, length us, event | category | flops | bytes accessed | tf_op | source)
XLA Modules:
  0.0 175.3 jit_solution(14531198278863146930)
XLA Ops:
  0.6 4.0 %collective-permute-start.1 = (bf16[768,768]{1,0:T(8,128)(2,1)}, bf16[768,768]{1,0:T(8,128)(2,1)S(1)}, u32[]{:S(2)}, u32[]{:S(2)}) collective-permute-start(bf16[768,768]{1,0:T(8,128)(2,1)} %w0.7), channel_id=1, source_target_pairs={{0,1},{1,0},{2,3},{3,2},{4,5},{5,4},{6,7},{7,6},{8,9},{9,8},{10,11... | collective-permute-start | bytes 3538952 | tf_op jit(solution)/shard_map/ppermute | solution.py:29
  4.6 8.8 %collective-permute-start = (bf16[32,768]{1,0:T(8,128)(2,1)}, bf16[32,768]{1,0:T(8,128)(2,1)S(1)}, u32[]{:S(2)}, u32[]{:S(2)}) collective-permute-start(bf16[32,768]{1,0:T(8,128)(2,1)} %param.3), channel_id=1, source_target_pairs={{0,16},{1,17},{2,18},{3,19},{4,20},{5,21},{6,22},{7,23},{8,24},{9,... | collective-permute-start | bytes 147464 | tf_op jit(solution)/shard_map/ppermute | solution.py:29
  13.4 1.7 collective-permute-done
  15.9 15.8 %all_gather.6.piece.line = bf16[256,768]{1,0:T(8,128)(2,1)S(1)} all-gather(bf16[64,768]{1,0:T(8,128)(2,1)S(1)} %pad_maximum_fusion.2), channel_id=1, replica_groups={{0,4,8,12},{1,5,9,13},{2,6,10,14},{3,7,11,15},{16,20,24,28},{17,21,25,2..., dimensions={0}, use_global_device_ids=true | all-gather | bytes 491520 | tf_op jit(solution)/shard_map/all_gather | solution.py:164
  31.7 4.4 %collective-permute-start.2 = (bf16[256,768]{1,0:T(8,128)(2,1)S(1)}, bf16[256,768]{1,0:T(8,128)(2,1)S(1)}, u32[]{:S(2)}, u32[]{:S(2)}) collective-permute-start(bf16[256,768]{1,0:T(8,128)(2,1)S(1)} %all_gather.6.piece.line), channel_id=1, source_target_pairs={{0,2},{1,3},{2,0},{3,1},{4,6},{5,7},{6,4},{7,5},{8,10},{9,11},{10,... | collective-permute-start | bytes 1179656 | tf_op jit(solution)/shard_map/ppermute | solution.py:29
  36.1 10.8 %collective-permute-start.3 = (bf16[64,768]{1,0:T(8,128)(2,1)}, bf16[64,768]{1,0:T(8,128)(2,1)S(1)}, u32[]{:S(2)}, u32[]{:S(2)}) collective-permute-start(bf16[64,768]{1,0:T(8,128)(2,1)} %param.5), channel_id=1, source_target_pairs={{0,64},{32,96},{64,0},{96,32},{128,192},{160,224},{192,128},{224,1... | collective-permute-start | bytes 294920 | tf_op jit(solution)/shard_map/ppermute | solution.py:29
  47.0 1.3 copy-done
  48.3 1.3 shard_map.58.early
  50.5 1.4 shard_map.59
  51.9 8.2 %collective-permute-start.4 = (bf16[512,768]{1,0:T(8,128)(2,1)S(1)}, bf16[512,768]{1,0:T(8,128)(2,1)S(1)}, u32[]{:S(2)}, u32[]{:S(2)}) collective-permute-start(bf16[512,768]{1,0:T(8,128)(2,1)S(1)} %get-tuple-element.8), channel_id=1, source_target_pairs={{0,32},{32,0},{64,96},{96,64},{128,160},{160,128},{192,224},{224,1... | collective-permute-start | bytes 2359304 | tf_op jit(solution)/shard_map/ppermute | solution.py:29
  60.1 1.9 %collective-permute-done.4.got = bf16[512,768]{1,0:T(8,128)(2,1)S(1)} collective-permute-done((bf16[512,768]{1,0:T(8,128)(2,1)S(1)}, bf16[512,768]{1,0:T(8,128)(2,1)S(1)}, u32[]{:S(2)}, u32[]{:S(2)}) %collective-permute-start.4) | collective-permute-done | bytes 786464 | tf_op jit(solution)/shard_map/ppermute | solution.py:29
  61.9 1.6 shard_map.60
  63.5 4.3 %all-to-all-start = ((bf16[4,128,768]{2,1,0:T(8,128)(2,1)}), bf16[4,128,768]{2,1,0:T(8,128)(2,1)}, u32[]{:S(2)}, u32[]{:S(2)}) async-start(bf16[4,128,768]{2,1,0:T(8,128)(2,1)} %bitcast.2), calls=%async_computation | async-start | bytes 1572864 | tf_op jit(solution)/shard_map/all_to_all | solution.py:33
  68.0 1.9 %collective-permute-start.7 = (bf16[2,32,768]{2,1,0:T(8,128)(2,1)S(1)}, bf16[2,32,768]{2,1,0:T(8,128)(2,1)S(1)}, u32[]{:S(2)}, u32[]{:S(2)}) collective-permute-start(bf16[2,32,768]{2,1,0:T(8,128)(2,1)S(1)} %get-tuple-element.18), channel_id=1, source_target_pairs={{0,1},{1,0},{2,3},{3,2},{4,5},{5,4},{6,7},{7,6},{8,9},{9,8},{10,11... | collective-permute-start | bytes 294920 | tf_op jit(solution)/shard_map/ppermute | solution.py:29
  69.9 9.8 %all-to-all-done = bf16[4,128,768]{2,1,0:T(8,128)(2,1)} async-done(((bf16[4,128,768]{2,1,0:T(8,128)(2,1)}), bf16[4,128,768]{2,1,0:T(8,128)(2,1)}, u32[]{:S(2)}, u32[]{:S(2)}) %all-to-all-start) | async-done | bytes 786464 | tf_op jit(solution)/shard_map/all_to_all | solution.py:33
  79.7 1.3 bitcast_convert_fusion
  81.0 12.6 %collective-permute-start.5 = (bf16[128,768]{1,0:T(8,128)(2,1)S(1)}, bf16[128,768]{1,0:T(8,128)(2,1)S(1)}, u32[]{:S(2)}, u32[]{:S(2)}) collective-permute-start(bf16[128,768]{1,0:T(8,128)(2,1)S(1)} %bitcast_convert_fusion), channel_id=1, source_target_pairs={{0,64},{32,96},{64,0},{96,32},{128,192},{160,224},{192,128},{224,1... | collective-permute-start | bytes 589832 | tf_op jit(solution)/shard_map/ppermute | solution.py:29
  94.3 1.9 %collective-permute-start.8 = (bf16[512,768]{1,0:T(8,128)(2,1)S(1)}, bf16[512,768]{1,0:T(8,128)(2,1)S(1)}, u32[]{:S(2)}, u32[]{:S(2)}) collective-permute-start(bf16[512,768]{1,0:T(8,128)(2,1)S(1)} %shard_map.61), channel_id=1, source_target_pairs={{0,1},{1,0},{2,3},{3,2},{4,5},{5,4},{6,7},{7,6},{8,9},{9,8},{10,11... | collective-permute-start | bytes 2359304 | tf_op jit(solution)/shard_map/ppermute | solution.py:29
  97.3 2.2 %fusion.13 = (bf16[128,768]{1,0:T(8,128)(2,1)S(1)}, f32[128,768]{1,0:T(8,128)}) fusion(f32[2,2,32,768]{3,2,1,0:T(8,128)S(1)} %copy.6, bf16[128,768]{1,0:T(8,128)(2,1)S(1)} %collective-permute-done.5, bf16[4,128,768]{2,1,0:T(8,128)(2,1)} %all-to-all-done), kind=kLoop, calls=%fused_computation.17 | loop fusion | flops 1867776 | bytes 1966080 | tf_op jit(solution)/shard_map/convert_element_type | solution.py:196
  99.5 12.2 %all_gather.7.grad = bf16[512,768]{1,0:T(8,128)(2,1)S(1)} all-gather(bf16[128,768]{1,0:T(8,128)(2,1)S(1)} %get-tuple-element.11), channel_id=1, replica_groups={{0,128,256,384},{32,160,288,416},{64,192,320,448},{96,224,352,480},{1,1..., dimensions={0}, use_global_device_ids=true | all-gather | bytes 983040 | tf_op jit(solution)/shard_map/all_gather | solution.py:200
  111.7 5.7 %collective-permute-start.9 = (bf16[512,768]{1,0:T(8,128)(2,1)S(1)}, bf16[512,768]{1,0:T(8,128)(2,1)S(1)}, u32[]{:S(2)}, u32[]{:S(2)}) collective-permute-start(bf16[512,768]{1,0:T(8,128)(2,1)S(1)} %all_gather.7.grad), channel_id=1, source_target_pairs={{0,32},{32,0},{64,96},{96,64},{128,160},{160,128},{192,224},{224,1... | collective-permute-start | bytes 2359304 | tf_op jit(solution)/shard_map/ppermute | solution.py:29
  117.5 1.3 shard_map.62.first
  119.3 1.4 shard_map.63
  120.8 2.8 %collective-permute-start.10 = (bf16[256,768]{1,0:T(8,128)(2,1)S(1)}, bf16[256,768]{1,0:T(8,128)(2,1)S(1)}, u32[]{:S(2)}, u32[]{:S(2)}) collective-permute-start(bf16[256,768]{1,0:T(8,128)(2,1)S(1)} %get-tuple-element.10), channel_id=1, source_target_pairs={{0,2},{1,3},{2,0},{3,1},{4,6},{5,7},{6,4},{7,5},{8,10},{9,11},{10,... | collective-permute-start | bytes 1179656 | tf_op jit(solution)/shard_map/ppermute | solution.py:29
  123.6 11.0 %collective-permute-done.10 = bf16[256,768]{1,0:T(8,128)(2,1)S(1)} collective-permute-done((bf16[256,768]{1,0:T(8,128)(2,1)S(1)}, bf16[256,768]{1,0:T(8,128)(2,1)S(1)}, u32[]{:S(2)}, u32[]{:S(2)}) %collective-permute-start.10) | collective-permute-done | bytes 393248 | tf_op jit(solution)/shard_map/ppermute | solution.py:29
  135.4 13.2 %all-to-all-start.1 = ((bf16[4,64,768]{2,1,0:T(8,128)(2,1)}), bf16[4,64,768]{2,1,0:T(8,128)(2,1)S(1)}, u32[]{:S(2)}, u32[]{:S(2)}) async-start(bf16[4,64,768]{2,1,0:T(8,128)(2,1)} %bitcast.9), calls=%async_computation.1 | async-start | bytes 786432 | tf_op jit(solution)/shard_map/all_to_all | solution.py:33
  148.7 1.9 %collective-permute-start.6 = (bf16[32,768]{1,0:T(8,128)(2,1)S(1)}, bf16[32,768]{1,0:T(8,128)(2,1)S(1)}, u32[]{:S(2)}, u32[]{:S(2)}) collective-permute-start(bf16[32,768]{1,0:T(8,128)(2,1)S(1)} %slice.103), channel_id=1, source_target_pairs={{0,1},{1,0},{2,3},{3,2},{4,5},{5,4},{6,7},{7,6},{8,9},{9,8},{10,11... | collective-permute-start | bytes 147464 | tf_op jit(solution)/shard_map/ppermute | solution.py:29
  151.5 3.5 %collective-permute-start.12 = (bf16[512,768]{1,0:T(8,128)(2,1)S(1)}, bf16[512,768]{1,0:T(8,128)(2,1)}, u32[]{:S(2)}, u32[]{:S(2)}) collective-permute-start(bf16[512,768]{1,0:T(8,128)(2,1)S(1)} %pad_maximum_fusion), channel_id=1, source_target_pairs={{0,1},{1,0},{2,3},{3,2},{4,5},{5,4},{6,7},{7,6},{8,9},{9,8},{10,11... | collective-permute-start | bytes 2359304 | tf_op jit(solution)/shard_map/ppermute | solution.py:29
  155.7 2.7 %all-to-all-done.1 = bf16[4,64,768]{2,1,0:T(8,128)(2,1)S(1)} async-done(((bf16[4,64,768]{2,1,0:T(8,128)(2,1)}), bf16[4,64,768]{2,1,0:T(8,128)(2,1)S(1)}, u32[]{:S(2)}, u32[]{:S(2)}) %all-to-all-start.1) | async-done | bytes 393248 | tf_op jit(solution)/shard_map/all_to_all | solution.py:33
  158.5 8.0 %collective-permute-start.11 = (bf16[32,768]{1,0:T(8,128)(2,1)S(1)}, bf16[32,768]{1,0:T(8,128)(2,1)S(1)}, u32[]{:S(2)}, u32[]{:S(2)}) collective-permute-start(bf16[32,768]{1,0:T(8,128)(2,1)S(1)} %fusion.17), channel_id=1, source_target_pairs={{0,16},{1,17},{2,18},{3,19},{4,20},{5,21},{6,22},{7,23},{8,24},{9,... | collective-permute-start | bytes 147464 | tf_op jit(solution)/shard_map/ppermute | solution.py:29
  166.6 4.4 %collective-permute-done.12 = bf16[512,768]{1,0:T(8,128)(2,1)} collective-permute-done((bf16[512,768]{1,0:T(8,128)(2,1)S(1)}, bf16[512,768]{1,0:T(8,128)(2,1)}, u32[]{:S(2)}, u32[]{:S(2)}) %collective-permute-start.12) | collective-permute-done | bytes 786464 | tf_op jit(solution)/shard_map/ppermute | solution.py:29
  171.0 3.7 %multiply_convert_fusion = bf16[768,768]{1,0:T(8,128)(2,1)} fusion(bf16[512,768]{1,0:T(8,128)(2,1)S(1)} %copy-done.5, bf16[512,768]{1,0:T(8,128)(2,1)S(1)} %copy-done.7, bf16[512,768]{1,0:T(8,128)(2,1)} %collective-permute-done.12, bf16[256,768]{1,0:T(8,128)(2,1)} %bitcast.36, bf16[256,768]{1,0:T(8,128)(2,1)S(1)} %bitcast.35), kind=kOutput, calls=%fused_computation | convolution fusion | flops 1217003520 | bytes 4325376 | tf_op jit(solution)/shard_map/dot_general | solution.py:229
  (46 shorter events, 7.2 us)
Async XLA Ops:
  0.6 46.4 %collective-permute-start.1 = (bf16[768,768]{1,0:T(8,128)(2,1)}, bf16[768,768]{1,0:T(8,128)(2,1)S(1)}, u32[]{:S(2)}, u32[]{:S(2)}) collective-permute-start(bf16[768,768]{1,0:T(8,128)(2,1)} %w0.7), channel_id=1, source_target_pairs={{0,1},{1,0},{2,3},{3,2},{4,5},{5,4},{6,7},{7,6},{8,9},{9,8},{10,11... | collective-permute-start | bytes 3538952 | tf_op jit(solution)/shard_map/ppermute | solution.py:29
  4.6 10.5 %collective-permute-start = (bf16[32,768]{1,0:T(8,128)(2,1)}, bf16[32,768]{1,0:T(8,128)(2,1)S(1)}, u32[]{:S(2)}, u32[]{:S(2)}) collective-permute-start(bf16[32,768]{1,0:T(8,128)(2,1)} %param.3), channel_id=1, source_target_pairs={{0,16},{1,17},{2,18},{3,19},{4,20},{5,21},{6,22},{7,23},{8,24},{9,... | collective-permute-start | bytes 147464 | tf_op jit(solution)/shard_map/ppermute | solution.py:29
  31.7 18.8 %collective-permute-start.2 = (bf16[256,768]{1,0:T(8,128)(2,1)S(1)}, bf16[256,768]{1,0:T(8,128)(2,1)S(1)}, u32[]{:S(2)}, u32[]{:S(2)}) collective-permute-start(bf16[256,768]{1,0:T(8,128)(2,1)S(1)} %all_gather.6.piece.line), channel_id=1, source_target_pairs={{0,2},{1,3},{2,0},{3,1},{4,6},{5,7},{6,4},{7,5},{8,10},{9,11},{10,... | collective-permute-start | bytes 1179656 | tf_op jit(solution)/shard_map/ppermute | solution.py:29
  36.1 14.4 %collective-permute-start.3 = (bf16[64,768]{1,0:T(8,128)(2,1)}, bf16[64,768]{1,0:T(8,128)(2,1)S(1)}, u32[]{:S(2)}, u32[]{:S(2)}) collective-permute-start(bf16[64,768]{1,0:T(8,128)(2,1)} %param.5), channel_id=1, source_target_pairs={{0,64},{32,96},{64,0},{96,32},{128,192},{160,224},{192,128},{224,1... | collective-permute-start | bytes 294920 | tf_op jit(solution)/shard_map/ppermute | solution.py:29
  47.0 1.3 copy-start
  48.3 2.2 %copy-start.1 = (bf16[768,768]{1,0:T(8,128)(2,1)S(1)}, bf16[768,768]{1,0:T(8,128)(2,1)}, u32[]{:S(2)}) copy-start(bf16[768,768]{1,0:T(8,128)(2,1)} %w0.7) | copy-start | bytes 3538948
  51.9 10.1 %collective-permute-start.4 = (bf16[512,768]{1,0:T(8,128)(2,1)S(1)}, bf16[512,768]{1,0:T(8,128)(2,1)S(1)}, u32[]{:S(2)}, u32[]{:S(2)}) collective-permute-start(bf16[512,768]{1,0:T(8,128)(2,1)S(1)} %get-tuple-element.8), channel_id=1, source_target_pairs={{0,32},{32,0},{64,96},{96,64},{128,160},{160,128},{192,224},{224,1... | collective-permute-start | bytes 2359304 | tf_op jit(solution)/shard_map/ppermute | solution.py:29
  63.5 4.4 %copy-start.9 = (bf16[64,768]{1,0:T(8,128)(2,1)S(1)}, bf16[64,768]{1,0:T(8,128)(2,1)}, u32[]{:S(2)}) copy-start(bf16[64,768]{1,0:T(8,128)(2,1)} %param.5) | copy-start | bytes 294916
  63.5 16.1 %all-to-all-start = ((bf16[4,128,768]{2,1,0:T(8,128)(2,1)}), bf16[4,128,768]{2,1,0:T(8,128)(2,1)}, u32[]{:S(2)}, u32[]{:S(2)}) async-start(bf16[4,128,768]{2,1,0:T(8,128)(2,1)} %bitcast.2), calls=%async_computation | async-start | bytes 1572864 | tf_op jit(solution)/shard_map/all_to_all | solution.py:33
  68.0 25.7 %collective-permute-start.7 = (bf16[2,32,768]{2,1,0:T(8,128)(2,1)S(1)}, bf16[2,32,768]{2,1,0:T(8,128)(2,1)S(1)}, u32[]{:S(2)}, u32[]{:S(2)}) collective-permute-start(bf16[2,32,768]{2,1,0:T(8,128)(2,1)S(1)} %get-tuple-element.18), channel_id=1, source_target_pairs={{0,1},{1,0},{2,3},{3,2},{4,5},{5,4},{6,7},{7,6},{8,9},{9,8},{10,11... | collective-permute-start | bytes 294920 | tf_op jit(solution)/shard_map/ppermute | solution.py:29
  81.0 16.3 %collective-permute-start.5 = (bf16[128,768]{1,0:T(8,128)(2,1)S(1)}, bf16[128,768]{1,0:T(8,128)(2,1)S(1)}, u32[]{:S(2)}, u32[]{:S(2)}) collective-permute-start(bf16[128,768]{1,0:T(8,128)(2,1)S(1)} %bitcast_convert_fusion), channel_id=1, source_target_pairs={{0,64},{32,96},{64,0},{96,32},{128,192},{160,224},{192,128},{224,1... | collective-permute-start | bytes 589832 | tf_op jit(solution)/shard_map/ppermute | solution.py:29
  94.3 23.1 %copy-start.6 = (bf16[512,768]{1,0:T(8,128)(2,1)}, bf16[512,768]{1,0:T(8,128)(2,1)S(1)}, u32[]{:S(2)}) copy-start(bf16[512,768]{1,0:T(8,128)(2,1)S(1)} %shard_map.61) | copy-start | bytes 2359300
  94.3 23.1 %collective-permute-start.8 = (bf16[512,768]{1,0:T(8,128)(2,1)S(1)}, bf16[512,768]{1,0:T(8,128)(2,1)S(1)}, u32[]{:S(2)}, u32[]{:S(2)}) collective-permute-start(bf16[512,768]{1,0:T(8,128)(2,1)S(1)} %shard_map.61), channel_id=1, source_target_pairs={{0,1},{1,0},{2,3},{3,2},{4,5},{5,4},{6,7},{7,6},{8,9},{9,8},{10,11... | collective-permute-start | bytes 2359304 | tf_op jit(solution)/shard_map/ppermute | solution.py:29
  111.7 7.6 %collective-permute-start.9 = (bf16[512,768]{1,0:T(8,128)(2,1)S(1)}, bf16[512,768]{1,0:T(8,128)(2,1)S(1)}, u32[]{:S(2)}, u32[]{:S(2)}) collective-permute-start(bf16[512,768]{1,0:T(8,128)(2,1)S(1)} %all_gather.7.grad), channel_id=1, source_target_pairs={{0,32},{32,0},{64,96},{96,64},{128,160},{160,128},{192,224},{224,1... | collective-permute-start | bytes 2359304 | tf_op jit(solution)/shard_map/ppermute | solution.py:29
  117.5 1.4 copy-start.4
  119.3 1.4 copy-start.2
  120.8 27.8 %copy-start.8 = (f32[128,768]{1,0:T(8,128)S(1)}, f32[128,768]{1,0:T(8,128)}, u32[]{:S(2)}) copy-start(f32[128,768]{1,0:T(8,128)} %get-tuple-element.12) | copy-start | bytes 1179652
  120.8 13.8 %collective-permute-start.10 = (bf16[256,768]{1,0:T(8,128)(2,1)S(1)}, bf16[256,768]{1,0:T(8,128)(2,1)S(1)}, u32[]{:S(2)}, u32[]{:S(2)}) collective-permute-start(bf16[256,768]{1,0:T(8,128)(2,1)S(1)} %get-tuple-element.10), channel_id=1, source_target_pairs={{0,2},{1,3},{2,0},{3,1},{4,6},{5,7},{6,4},{7,5},{8,10},{9,11},{10,... | collective-permute-start | bytes 1179656 | tf_op jit(solution)/shard_map/ppermute | solution.py:29
  135.4 15.2 %copy-start.3 = (bf16[512,768]{1,0:T(8,128)(2,1)S(1)}, bf16[512,768]{1,0:T(8,128)(2,1)}, u32[]{:S(2)}) copy-start(bf16[512,768]{1,0:T(8,128)(2,1)} %copy-done.2) | copy-start | bytes 2359300
  135.4 23.0 %all-to-all-start.1 = ((bf16[4,64,768]{2,1,0:T(8,128)(2,1)}), bf16[4,64,768]{2,1,0:T(8,128)(2,1)S(1)}, u32[]{:S(2)}, u32[]{:S(2)}) async-start(bf16[4,64,768]{2,1,0:T(8,128)(2,1)} %bitcast.9), calls=%async_computation.1 | async-start | bytes 786432 | tf_op jit(solution)/shard_map/all_to_all | solution.py:33
  148.7 6.4 %collective-permute-start.6 = (bf16[32,768]{1,0:T(8,128)(2,1)S(1)}, bf16[32,768]{1,0:T(8,128)(2,1)S(1)}, u32[]{:S(2)}, u32[]{:S(2)}) collective-permute-start(bf16[32,768]{1,0:T(8,128)(2,1)S(1)} %slice.103), channel_id=1, source_target_pairs={{0,1},{1,0},{2,3},{3,2},{4,5},{5,4},{6,7},{7,6},{8,9},{9,8},{10,11... | collective-permute-start | bytes 147464 | tf_op jit(solution)/shard_map/ppermute | solution.py:29
  151.5 19.5 %copy-start.5 = (bf16[512,768]{1,0:T(8,128)(2,1)S(1)}, bf16[512,768]{1,0:T(8,128)(2,1)}, u32[]{:S(2)}) copy-start(bf16[512,768]{1,0:T(8,128)(2,1)} %copy-done.4) | copy-start | bytes 2359300
  151.5 19.5 %copy-start.7 = (bf16[512,768]{1,0:T(8,128)(2,1)S(1)}, bf16[512,768]{1,0:T(8,128)(2,1)}, u32[]{:S(2)}) copy-start(bf16[512,768]{1,0:T(8,128)(2,1)} %copy-done.6) | copy-start | bytes 2359300
  151.5 19.4 %collective-permute-start.12 = (bf16[512,768]{1,0:T(8,128)(2,1)S(1)}, bf16[512,768]{1,0:T(8,128)(2,1)}, u32[]{:S(2)}, u32[]{:S(2)}) collective-permute-start(bf16[512,768]{1,0:T(8,128)(2,1)S(1)} %pad_maximum_fusion), channel_id=1, source_target_pairs={{0,1},{1,0},{2,3},{3,2},{4,5},{5,4},{6,7},{7,6},{8,9},{9,8},{10,11... | collective-permute-start | bytes 2359304 | tf_op jit(solution)/shard_map/ppermute | solution.py:29
  158.5 16.2 %collective-permute-start.11 = (bf16[32,768]{1,0:T(8,128)(2,1)S(1)}, bf16[32,768]{1,0:T(8,128)(2,1)S(1)}, u32[]{:S(2)}, u32[]{:S(2)}) collective-permute-start(bf16[32,768]{1,0:T(8,128)(2,1)S(1)} %fusion.17), channel_id=1, source_target_pairs={{0,16},{1,17},{2,18},{3,19},{4,20},{5,21},{6,22},{7,23},{8,24},{9,... | collective-permute-start | bytes 147464 | tf_op jit(solution)/shard_map/ppermute | solution.py:29

commit v4 on v3

--- a/solution.py
+++ b/solution.py
@@ -59,7 +59,8 @@
             out[pl.ds((z * 2 + block) * part, part), :] = value[z * part : (z + 1) * part]
 
 
-def early_kernel(me, piece, w0, w1, out, held):
+def early_kernel(me, piece, w0, w1, cotangent, out, passed, held):
+    passed[...] = cotangent[...]
     products(me, piece, (w0, w1), held, out)
 
 
@@ -164,17 +165,20 @@
     line = lax.all_gather(pair, "col", axis=0, tiled=True, axis_index_groups=Z_GROUPS)
     across = swap(line, "col", 2)
 
-    other = swap(cotangent, "row", 2)
-    low = jnp.stack([jnp.where(upper, x, y) for x, y in ((other, cotangent), (cotangent, other))])
-    low, high = low[:, :part], low[:, part:]
-    both = [jnp.where(odd, high, low), swap(jnp.where(odd, low, high), "col", 1)]
-    both = jnp.stack(both, axis=1).reshape(4 * part, width)
-
     size = tokens // 2
     held = [pltpu.VMEM((tokens // 4, depth), BF16)]
-    (early,) = call(
-        early_kernel, [shape(size, width, F32)], held, flops, me, line, weight, partner
-    )
+    early, passed = call(
+        early_kernel,
+        [shape(size, width, F32), shape(2 * part, width, BF16)],
+        held, flops, me, line, weight, partner, cotangent,
+    )
+
+    other = swap(passed, "row", 2)
+    pairs = [jnp.where(upper, a, b) for a, b in ((other, cotangent), (cotangent, other))]
+    mine = [jnp.where(odd, p[part:], p[:part]) for p in pairs]
+    got = swap(jnp.concatenate([jnp.where(odd, p[:part], p[part:]) for p in pairs]), "col", 1)
+    both = jnp.concatenate([mine[0], got[:part], mine[1], got[part:]])
+
     late, send = call(
         send_kernel,
         [shape(size, width, F32), shape(size, width, BF16)],
@@ -224,11 +228,12 @@
     acts_grad = total([mine[:part], swap(mine[part:].astype(BF16), "col", 16)]).astype(BF16)
 
     split = [g.reshape(8, 2, part, width) for g in (g0, g1)]
-    own = [s[:, 0].reshape(-1, width) for s in split]
-    others = jnp.concatenate([s[:, 1].reshape(-1, width) for s in split])
+    own = [g[:, 0].reshape(-1, width) for g in split]
+    others = [swap(split[0][:, 1].reshape(-1, width), "col", 1)]
+    others += [swap(others[0], "row", 1)]
     weight_sum = lax.dot_general(
         jnp.concatenate([near, far]),
-        jnp.concatenate(own + [swap(others, "col", 1)]),
+        jnp.concatenate(own + others),
         (((0,), (0,)), ((), ())),
         preferred_element_type=F32,
     )

time: 178 us -> 183 us (1.028); the launches traced: 175 us -> 182 us
  starting transfers between devices: 92.1 us -> 100 us
  waiting for transfers between devices: 33.9 us -> 31.3 us
    ppermute x13 -> x14, starting transfers between devices: 74.6 us -> 92.5 us  [swap(): return lax.ppermute(value, axis, [(i, i ^ mask) for i in range(size)])]
    all_to_all x2, starting transfers between devices: 17.5 us -> 7.94 us  [spread(): lax.all_to_all(value, axis, split_axis=0, concat_axis=0, axis_index_group...]
    all_to_all x2, waiting for transfers between devices: 12.5 us -> 4.19 us  [spread(): lax.all_to_all(value, axis, split_axis=0, concat_axis=0, axis_index_group...]
    ppermute x13 -> x14, waiting for transfers between devices: 21.4 us -> 27.1 us  [swap(): return lax.ppermute(value, axis, [(i, i ^ mask) for i in range(size)])]
  transfers between devices with their start and end apart: 15 -> 16, of which waited for: 9 -> 8; matrix products, arithmetic and copies ran while one was open for 6% -> 5% of each run, Pallas kernels for 2% -> 3%
where the time goes in v4:
time: 183 us; the launch traced here: 182 us
  starting transfers between devices  100 us (55%)
  waiting for transfers between devices  31.3 us (17%)
  blocking collectives  27.7 us (15%)
  Pallas kernels  9.17 us (5%)
  other arithmetic  6.75 us (4%)
  matrix products  3.83 us (2%)
  local copies, waits for them, and re-layouts  2.29 us (1%)
    ppermute x14, starting transfers between devices, swap(): return lax.ppermute(value, axis, [(i, i ^ mask) for i in range(size)])  92.5 us
    ppermute x14, waiting for transfers between devices, swap(): return lax.ppermute(value, axis, [(i, i ^ mask) for i in range(size)])  27.1 us
    all_gather x1, blocking collectives, shards(): lax.all_gather(pair, 'col', axis=0, tiled=True, axis_index_groups=Z_GROUPS)  15.8 us
    all_gather x1, blocking collectives, shards(): lax.all_gather(grad, 'row', axis=0, tiled=True, axis_index_groups=Y_GROUPS)  12 us
    pallas_call x6, Pallas kernels, call(): pl.pallas_call(kernel, out_shape=outs, in_specs=[pl.BlockSpec(memory_spac...  9.17 us
    all_to_all x2, starting transfers between devices, spread(): lax.all_to_all(value, axis, split_axis=0, concat_axis=0, axis_index_group...  7.94 us
    all_to_all x2, waiting for transfers between devices, spread(): lax.all_to_all(value, axis, split_axis=0, concat_axis=0, axis_index_group...  4.19 us
    dot_general x1, matrix products, shards(): lax.dot_general(jnp.concatenate([near, far]), jnp.concatenate(own + other...  3.83 us
  transfers between devices with their start and end apart: 16, of which 8 were waited for; matrix products, arithmetic and copies ran while one was open for 5% of the time, Pallas kernels for 3%

profile of v4, /device:TPU:1, one launch (start us, length us, event | category | flops | bytes accessed | tf_op | source)
XLA Modules:
  0.0 182.4 jit_solution(16684938576232670663)
XLA Ops:
  0.6 4.0 %collective-permute-start.1 = (bf16[768,768]{1,0:T(8,128)(2,1)}, bf16[768,768]{1,0:T(8,128)(2,1)S(1)}, u32[]{:S(2)}, u32[]{:S(2)}) collective-permute-start(bf16[768,768]{1,0:T(8,128)(2,1)} %w0.7), channel_id=1, source_target_pairs={{0,1},{1,0},{2,3},{3,2},{4,5},{5,4},{6,7},{7,6},{8,9},{9,8},{10,11... | collective-permute-start | bytes 3538952 | tf_op jit(solution)/shard_map/ppermute | solution.py:29
  4.6 8.8 %collective-permute-start = (bf16[32,768]{1,0:T(8,128)(2,1)}, bf16[32,768]{1,0:T(8,128)(2,1)S(1)}, u32[]{:S(2)}, u32[]{:S(2)}) collective-permute-start(bf16[32,768]{1,0:T(8,128)(2,1)} %param.3), channel_id=1, source_target_pairs={{0,16},{1,17},{2,18},{3,19},{4,20},{5,21},{6,22},{7,23},{8,24},{9,... | collective-permute-start | bytes 147464 | tf_op jit(solution)/shard_map/ppermute | solution.py:29
  13.4 1.7 collective-permute-done
  15.9 15.8 %all_gather.6.piece.line = bf16[256,768]{1,0:T(8,128)(2,1)S(1)} all-gather(bf16[64,768]{1,0:T(8,128)(2,1)S(1)} %pad_maximum_fusion), channel_id=1, replica_groups={{0,4,8,12},{1,5,9,13},{2,6,10,14},{3,7,11,15},{16,20,24,28},{17,21,25,2..., dimensions={0}, use_global_device_ids=true | all-gather | bytes 491520 | tf_op jit(solution)/shard_map/all_gather | solution.py:165
  31.7 4.4 %collective-permute-start.2 = (bf16[256,768]{1,0:T(8,128)(2,1)S(1)}, bf16[256,768]{1,0:T(8,128)(2,1)S(1)}, u32[]{:S(2)}, u32[]{:S(2)}) collective-permute-start(bf16[256,768]{1,0:T(8,128)(2,1)S(1)} %all_gather.6.piece.line), channel_id=1, source_target_pairs={{0,2},{1,3},{2,0},{3,1},{4,6},{5,7},{6,4},{7,5},{8,10},{9,11},{10,... | collective-permute-start | bytes 1179656 | tf_op jit(solution)/shard_map/ppermute | solution.py:29
  39.6 10.8 %collective-permute-start.3 = (bf16[64,768]{1,0:T(8,128)(2,1)S(1)}, bf16[64,768]{1,0:T(8,128)(2,1)S(1)}, u32[]{:S(2)}, u32[]{:S(2)}) collective-permute-start(bf16[64,768]{1,0:T(8,128)(2,1)S(1)} %get-tuple-element.10), channel_id=1, source_target_pairs={{0,64},{32,96},{64,0},{96,32},{128,192},{160,224},{192,128},{224,1... | collective-permute-start | bytes 294920 | tf_op jit(solution)/shard_map/ppermute | solution.py:29
  50.5 3.3 %collective-permute-done.3._ = bf16[64,768]{1,0:T(8,128)(2,1)S(1)} collective-permute-done((bf16[64,768]{1,0:T(8,128)(2,1)S(1)}, bf16[64,768]{1,0:T(8,128)(2,1)S(1)}, u32[]{:S(2)}, u32[]{:S(2)}) %collective-permute-start.3) | collective-permute-done | bytes 98336 | tf_op jit(solution)/shard_map/ppermute | solution.py:29
  53.8 1.4 shard_map.59
  55.2 8.3 %collective-permute-start.4 = (bf16[512,768]{1,0:T(8,128)(2,1)S(1)}, bf16[512,768]{1,0:T(8,128)(2,1)S(1)}, u32[]{:S(2)}, u32[]{:S(2)}) collective-permute-start(bf16[512,768]{1,0:T(8,128)(2,1)S(1)} %get-tuple-element.12), channel_id=1, source_target_pairs={{0,32},{32,0},{64,96},{96,64},{128,160},{160,128},{192,224},{224,1... | collective-permute-start | bytes 2359304 | tf_op jit(solution)/shard_map/ppermute | solution.py:29
  63.6 1.9 %collective-permute-done.4.got = bf16[512,768]{1,0:T(8,128)(2,1)S(1)} collective-permute-done((bf16[512,768]{1,0:T(8,128)(2,1)S(1)}, bf16[512,768]{1,0:T(8,128)(2,1)S(1)}, u32[]{:S(2)}, u32[]{:S(2)}) %collective-permute-start.4) | collective-permute-done | bytes 786464 | tf_op jit(solution)/shard_map/ppermute | solution.py:29
  65.4 1.6 shard_map.60
  67.0 4.3 %all-to-all-start = ((bf16[4,128,768]{2,1,0:T(8,128)(2,1)}), bf16[4,128,768]{2,1,0:T(8,128)(2,1)}, u32[]{:S(2)}, u32[]{:S(2)}) async-start(bf16[4,128,768]{2,1,0:T(8,128)(2,1)} %bitcast.2), calls=%async_computation | async-start | bytes 1572864 | tf_op jit(solution)/shard_map/all_to_all | solution.py:33
  71.4 1.5 shard_map.61
  72.9 4.1 %collective-permute-start.8 = (bf16[512,768]{1,0:T(8,128)(2,1)}, bf16[512,768]{1,0:T(8,128)(2,1)}, u32[]{:S(2)}, u32[]{:S(2)}) collective-permute-start(bf16[512,768]{1,0:T(8,128)(2,1)} %shard_map.61), channel_id=1, source_target_pairs={{0,1},{1,0},{2,3},{3,2},{4,5},{5,4},{6,7},{7,6},{8,9},{9,8},{10,11... | collective-permute-start | bytes 2359304 | tf_op jit(solution)/shard_map/ppermute | solution.py:29
  77.0 1.9 %collective-permute-start.7 = (bf16[64,768]{1,0:T(8,128)(2,1)S(1)}, bf16[64,768]{1,0:T(8,128)(2,1)S(1)}, u32[]{:S(2)}, u32[]{:S(2)}) collective-permute-start(bf16[64,768]{1,0:T(8,128)(2,1)S(1)} %pad_maximum_fusion.2), channel_id=1, source_target_pairs={{0,1},{1,0},{2,3},{3,2},{4,5},{5,4},{6,7},{7,6},{8,9},{9,8},{10,11... | collective-permute-start | bytes 294920 | tf_op jit(solution)/shard_map/ppermute | solution.py:29
  79.0 4.2 %all-to-all-done = bf16[4,128,768]{2,1,0:T(8,128)(2,1)} async-done(((bf16[4,128,768]{2,1,0:T(8,128)(2,1)}), bf16[4,128,768]{2,1,0:T(8,128)(2,1)}, u32[]{:S(2)}, u32[]{:S(2)}) %all-to-all-start) | async-done | bytes 786464 | tf_op jit(solution)/shard_map/all_to_all | solution.py:33
  84.5 11.9 %collective-permute-start.5 = (bf16[128,768]{1,0:T(8,128)(2,1)S(1)}, bf16[128,768]{1,0:T(8,128)(2,1)S(1)}, u32[]{:S(2)}, u32[]{:S(2)}) collective-permute-start(bf16[128,768]{1,0:T(8,128)(2,1)S(1)} %bitcast_convert_fusion), channel_id=1, source_target_pairs={{0,64},{32,96},{64,0},{96,32},{128,192},{160,224},{192,128},{224,1... | collective-permute-start | bytes 589832 | tf_op jit(solution)/shard_map/ppermute | solution.py:29
  96.6 3.3 %collective-permute-done.5 = bf16[128,768]{1,0:T(8,128)(2,1)S(1)} collective-permute-done((bf16[128,768]{1,0:T(8,128)(2,1)S(1)}, bf16[128,768]{1,0:T(8,128)(2,1)S(1)}, u32[]{:S(2)}, u32[]{:S(2)}) %collective-permute-start.5) | collective-permute-done | bytes 196640 | tf_op jit(solution)/shard_map/ppermute | solution.py:29
  100.0 2.3 %fusion.15 = (bf16[128,768]{1,0:T(8,128)(2,1)S(1)}, f32[128,768]{1,0:T(8,128)}) fusion(bf16[32,768]{1,0:T(8,128)(2,1)S(1)} %get-tuple-element.26, bf16[32,768]{1,0:T(8,128)(2,1)S(1)} %get-tuple-element.27, bf16[32,768]{1,0:T(8,128)(2,1)S(1)} %get-tuple-element.25, bf16[32,768]{1,0:T(8,128)(2,1)S(1)} %get-tuple-element.30, ...), kind=kLoop, calls=%fused_computation.18 | loop fusion | flops 2654208 | bytes 1769472 | tf_op jit(solution)/shard_map/convert_element_type | solution.py:200
  102.2 12.0 %all_gather.7.grad = bf16[512,768]{1,0:T(8,128)(2,1)S(1)} all-gather(bf16[128,768]{1,0:T(8,128)(2,1)S(1)} %get-tuple-element.15), channel_id=1, replica_groups={{0,128,256,384},{32,160,288,416},{64,192,320,448},{96,224,352,480},{1,1..., dimensions={0}, use_global_device_ids=true | all-gather | bytes 983040 | tf_op jit(solution)/shard_map/all_gather | solution.py:204
  114.2 6.0 %collective-permute-start.9 = (bf16[512,768]{1,0:T(8,128)(2,1)S(1)}, bf16[512,768]{1,0:T(8,128)(2,1)S(1)}, u32[]{:S(2)}, u32[]{:S(2)}) collective-permute-start(bf16[512,768]{1,0:T(8,128)(2,1)S(1)} %all_gather.7.grad), channel_id=1, source_target_pairs={{0,32},{32,0},{64,96},{96,64},{128,160},{160,128},{192,224},{224,1... | collective-permute-start | bytes 2359304 | tf_op jit(solution)/shard_map/ppermute | solution.py:29
  120.2 1.9 %shard_map.62.first = f32[256,768]{1,0:T(8,128)S(1)} custom-call(s32[2]{0:T(128)S(1)} %pad_add_fusion.me, bf16[512,768]{1,0:T(8,128)(2,1)S(1)} %all_gather.7.grad, bf16[512,768]{1,0:T(8,128)(2,1)} %collective-permute-done.8._, bf16[768,768]{1,0:T(8,128)(2,1)S(1)} %copy-done.1, bf16[768,768]{1,0:T(8,128)(2,1)S(1)} %collective-permute-done.1.w1), custom_call_target="tpu_custom_call" | custom-call | flops 603979776 | bytes 3145728 | tf_op jit(solution)/shard_map/pallas_call | solution.py:136
  122.1 1.4 shard_map.63
  123.6 14.7 %collective-permute-start.10 = (bf16[256,768]{1,0:T(8,128)(2,1)S(1)}, bf16[256,768]{1,0:T(8,128)(2,1)S(1)}, u32[]{:S(2)}, u32[]{:S(2)}) collective-permute-start(bf16[256,768]{1,0:T(8,128)(2,1)S(1)} %get-tuple-element.14), channel_id=1, source_target_pairs={{0,2},{1,3},{2,0},{3,1},{4,6},{5,7},{6,4},{7,5},{8,10},{9,11},{10,... | collective-permute-start | bytes 1179656 | tf_op jit(solution)/shard_map/ppermute | solution.py:29
  138.3 9.3 %collective-permute-done.10 = bf16[256,768]{1,0:T(8,128)(2,1)S(1)} collective-permute-done((bf16[256,768]{1,0:T(8,128)(2,1)S(1)}, bf16[256,768]{1,0:T(8,128)(2,1)S(1)}, u32[]{:S(2)}, u32[]{:S(2)}) %collective-permute-start.10) | collective-permute-done | bytes 393248 | tf_op jit(solution)/shard_map/ppermute | solution.py:29
  148.4 3.6 %all-to-all-start.1 = ((bf16[4,64,768]{2,1,0:T(8,128)(2,1)}), bf16[4,64,768]{2,1,0:T(8,128)(2,1)S(1)}, u32[]{:S(2)}, u32[]{:S(2)}) async-start(bf16[4,64,768]{2,1,0:T(8,128)(2,1)} %bitcast.4), calls=%async_computation.1 | async-start | bytes 786432 | tf_op jit(solution)/shard_map/all_to_all | solution.py:33
  152.1 2.2 %collective-permute-start.12 = (bf16[256,768]{1,0:T(8,128)(2,1)S(1)}, bf16[256,768]{1,0:T(8,128)(2,1)S(1)}, u32[]{:S(2)}, u32[]{:S(2)}) collective-permute-start(bf16[256,768]{1,0:T(8,128)(2,1)S(1)} %bitcast.25), channel_id=1, source_target_pairs={{0,1},{1,0},{2,3},{3,2},{4,5},{5,4},{6,7},{7,6},{8,9},{9,8},{10,11... | collective-permute-start | bytes 1179656 | tf_op jit(solution)/shard_map/ppermute | solution.py:29
  154.3 3.1 %collective-permute-start.6 = (bf16[32,768]{1,0:T(8,128)(2,1)S(1)}, bf16[32,768]{1,0:T(8,128)(2,1)S(1)}, u32[]{:S(2)}, u32[]{:S(2)}) collective-permute-start(bf16[32,768]{1,0:T(8,128)(2,1)S(1)} %slice.119), channel_id=1, source_target_pairs={{0,1},{1,0},{2,3},{3,2},{4,5},{5,4},{6,7},{7,6},{8,9},{9,8},{10,11... | collective-permute-start | bytes 147464 | tf_op jit(solution)/shard_map/ppermute | solution.py:29
  157.5 7.3 %collective-permute-done.6 = bf16[32,768]{1,0:T(8,128)(2,1)S(1)} collective-permute-done((bf16[32,768]{1,0:T(8,128)(2,1)S(1)}, bf16[32,768]{1,0:T(8,128)(2,1)S(1)}, u32[]{:S(2)}, u32[]{:S(2)}) %collective-permute-start.6) | collective-permute-done | bytes 49184 | tf_op jit(solution)/shard_map/ppermute | solution.py:29
  165.5 3.7 %collective-permute-start.13 = (bf16[256,768]{1,0:T(8,128)(2,1)S(1)}, bf16[256,768]{1,0:T(8,128)(2,1)S(1)}, u32[]{:S(2)}, u32[]{:S(2)}) collective-permute-start(bf16[256,768]{1,0:T(8,128)(2,1)S(1)} %collective-permute-done.12), channel_id=1, source_target_pairs={{0,32},{32,0},{64,96},{96,64},{128,160},{160,128},{192,224},{224,1... | collective-permute-start | bytes 1179656 | tf_op jit(solution)/shard_map/ppermute | solution.py:29
  169.3 8.7 %collective-permute-start.11 = (bf16[32,768]{1,0:T(8,128)(2,1)S(1)}, bf16[32,768]{1,0:T(8,128)(2,1)S(1)}, u32[]{:S(2)}, u32[]{:S(2)}) collective-permute-start(bf16[32,768]{1,0:T(8,128)(2,1)S(1)} %fusion.18), channel_id=1, source_target_pairs={{0,16},{1,17},{2,18},{3,19},{4,20},{5,21},{6,22},{7,23},{8,24},{9,... | collective-permute-start | bytes 147464 | tf_op jit(solution)/shard_map/ppermute | solution.py:29
  178.0 3.8 %multiply_convert_fusion = bf16[768,768]{1,0:T(8,128)(2,1)} fusion(bf16[512,768]{1,0:T(8,128)(2,1)} %collective-permute-done.8._, bf16[512,768]{1,0:T(8,128)(2,1)} %shard_map.61, bf16[256,768]{1,0:T(8,128)(2,1)S(1)} %collective-permute-done.13, bf16[256,768]{1,0:T(8,128)(2,1)S(1)} %collective-permute-done.12, bf16[256,768]{1,0:T(8,128)(2,1)S(1)} %bitcast.23, ...), kind=kOutput, calls=%fused_computation | convolution fusion | flops 1218576384 | bytes 4325376 | tf_op jit(solution)/shard_map/dot_general | solution.py:234
  (41 shorter events, 8.3 us)
Async XLA Ops:
  0.6 35.5 %collective-permute-start.1 = (bf16[768,768]{1,0:T(8,128)(2,1)}, bf16[768,768]{1,0:T(8,128)(2,1)S(1)}, u32[]{:S(2)}, u32[]{:S(2)}) collective-permute-start(bf16[768,768]{1,0:T(8,128)(2,1)} %w0.7), channel_id=1, source_target_pairs={{0,1},{1,0},{2,3},{3,2},{4,5},{5,4},{6,7},{7,6},{8,9},{9,8},{10,11... | collective-permute-start | bytes 3538952 | tf_op jit(solution)/shard_map/ppermute | solution.py:29
  4.6 10.5 %collective-permute-start = (bf16[32,768]{1,0:T(8,128)(2,1)}, bf16[32,768]{1,0:T(8,128)(2,1)S(1)}, u32[]{:S(2)}, u32[]{:S(2)}) collective-permute-start(bf16[32,768]{1,0:T(8,128)(2,1)} %param.3), channel_id=1, source_target_pairs={{0,16},{1,17},{2,18},{3,19},{4,20},{5,21},{6,22},{7,23},{8,24},{9,... | collective-permute-start | bytes 147464 | tf_op jit(solution)/shard_map/ppermute | solution.py:29
  31.7 18.8 %collective-permute-start.2 = (bf16[256,768]{1,0:T(8,128)(2,1)S(1)}, bf16[256,768]{1,0:T(8,128)(2,1)S(1)}, u32[]{:S(2)}, u32[]{:S(2)}) collective-permute-start(bf16[256,768]{1,0:T(8,128)(2,1)S(1)} %all_gather.6.piece.line), channel_id=1, source_target_pairs={{0,2},{1,3},{2,0},{3,1},{4,6},{5,7},{6,4},{7,5},{8,10},{9,11},{10,... | collective-permute-start | bytes 1179656 | tf_op jit(solution)/shard_map/ppermute | solution.py:29
  36.1 1.3 copy-start
  37.4 0.9 copy-start.4
  38.3 15.5 %copy-start.1 = (bf16[768,768]{1,0:T(8,128)(2,1)S(1)}, bf16[768,768]{1,0:T(8,128)(2,1)}, u32[]{:S(2)}) copy-start(bf16[768,768]{1,0:T(8,128)(2,1)} %w0.7) | copy-start | bytes 3538948
  39.6 14.2 %collective-permute-start.3 = (bf16[64,768]{1,0:T(8,128)(2,1)S(1)}, bf16[64,768]{1,0:T(8,128)(2,1)S(1)}, u32[]{:S(2)}, u32[]{:S(2)}) collective-permute-start(bf16[64,768]{1,0:T(8,128)(2,1)S(1)} %get-tuple-element.10), channel_id=1, source_target_pairs={{0,64},{32,96},{64,0},{96,32},{128,192},{160,224},{192,128},{224,1... | collective-permute-start | bytes 294920 | tf_op jit(solution)/shard_map/ppermute | solution.py:29
  55.2 10.2 %collective-permute-start.4 = (bf16[512,768]{1,0:T(8,128)(2,1)S(1)}, bf16[512,768]{1,0:T(8,128)(2,1)S(1)}, u32[]{:S(2)}, u32[]{:S(2)}) collective-permute-start(bf16[512,768]{1,0:T(8,128)(2,1)S(1)} %get-tuple-element.12), channel_id=1, source_target_pairs={{0,32},{32,0},{64,96},{96,64},{128,160},{160,128},{192,224},{224,1... | collective-permute-start | bytes 2359304 | tf_op jit(solution)/shard_map/ppermute | solution.py:29
  67.0 9.9 %copy-start.5 = (bf16[64,768]{1,0:T(8,128)(2,1)S(1)}, bf16[64,768]{1,0:T(8,128)(2,1)}, u32[]{:S(2)}) copy-start(bf16[64,768]{1,0:T(8,128)(2,1)} %cotangent.1) | copy-start | bytes 294916
  67.0 16.1 %all-to-all-start = ((bf16[4,128,768]{2,1,0:T(8,128)(2,1)}), bf16[4,128,768]{2,1,0:T(8,128)(2,1)}, u32[]{:S(2)}, u32[]{:S(2)}) async-start(bf16[4,128,768]{2,1,0:T(8,128)(2,1)} %bitcast.2), calls=%async_computation | async-start | bytes 1572864 | tf_op jit(solution)/shard_map/all_to_all | solution.py:33
  72.9 47.3 %collective-permute-start.8 = (bf16[512,768]{1,0:T(8,128)(2,1)}, bf16[512,768]{1,0:T(8,128)(2,1)}, u32[]{:S(2)}, u32[]{:S(2)}) collective-permute-start(bf16[512,768]{1,0:T(8,128)(2,1)} %shard_map.61), channel_id=1, source_target_pairs={{0,1},{1,0},{2,3},{3,2},{4,5},{5,4},{6,7},{7,6},{8,9},{9,8},{10,11... | collective-permute-start | bytes 2359304 | tf_op jit(solution)/shard_map/ppermute | solution.py:29
  77.0 19.6 %collective-permute-start.7 = (bf16[64,768]{1,0:T(8,128)(2,1)S(1)}, bf16[64,768]{1,0:T(8,128)(2,1)S(1)}, u32[]{:S(2)}, u32[]{:S(2)}) collective-permute-start(bf16[64,768]{1,0:T(8,128)(2,1)S(1)} %pad_maximum_fusion.2), channel_id=1, source_target_pairs={{0,1},{1,0},{2,3},{3,2},{4,5},{5,4},{6,7},{7,6},{8,9},{9,8},{10,11... | collective-permute-start | bytes 294920 | tf_op jit(solution)/shard_map/ppermute | solution.py:29
  84.5 15.5 %collective-permute-start.5 = (bf16[128,768]{1,0:T(8,128)(2,1)S(1)}, bf16[128,768]{1,0:T(8,128)(2,1)S(1)}, u32[]{:S(2)}, u32[]{:S(2)}) collective-permute-start(bf16[128,768]{1,0:T(8,128)(2,1)S(1)} %bitcast_convert_fusion), channel_id=1, source_target_pairs={{0,64},{32,96},{64,0},{96,32},{128,192},{160,224},{192,128},{224,1... | collective-permute-start | bytes 589832 | tf_op jit(solution)/shard_map/ppermute | solution.py:29
  114.2 8.0 %collective-permute-start.9 = (bf16[512,768]{1,0:T(8,128)(2,1)S(1)}, bf16[512,768]{1,0:T(8,128)(2,1)S(1)}, u32[]{:S(2)}, u32[]{:S(2)}) collective-permute-start(bf16[512,768]{1,0:T(8,128)(2,1)S(1)} %all_gather.7.grad), channel_id=1, source_target_pairs={{0,32},{32,0},{64,96},{96,64},{128,160},{160,128},{192,224},{224,1... | collective-permute-start | bytes 2359304 | tf_op jit(solution)/shard_map/ppermute | solution.py:29
  122.1 1.5 copy-start.2
  123.6 24.0 %collective-permute-start.10 = (bf16[256,768]{1,0:T(8,128)(2,1)S(1)}, bf16[256,768]{1,0:T(8,128)(2,1)S(1)}, u32[]{:S(2)}, u32[]{:S(2)}) collective-permute-start(bf16[256,768]{1,0:T(8,128)(2,1)S(1)} %get-tuple-element.14), channel_id=1, source_target_pairs={{0,2},{1,3},{2,0},{3,1},{4,6},{5,7},{6,4},{7,5},{8,10},{9,11},{10,... | collective-permute-start | bytes 1179656 | tf_op jit(solution)/shard_map/ppermute | solution.py:29
  148.4 5.8 %copy-start.6 = (f32[128,768]{1,0:T(8,128)S(1)}, f32[128,768]{1,0:T(8,128)}, u32[]{:S(2)}) copy-start(f32[128,768]{1,0:T(8,128)} %get-tuple-element.16) | copy-start | bytes 1179652
  148.4 20.7 %copy-start.3 = (bf16[512,768]{1,0:T(8,128)(2,1)S(1)}, bf16[512,768]{1,0:T(8,128)(2,1)}, u32[]{:S(2)}) copy-start(bf16[512,768]{1,0:T(8,128)(2,1)} %copy-done.2) | copy-start | bytes 2359300
  148.4 20.8 %all-to-all-start.1 = ((bf16[4,64,768]{2,1,0:T(8,128)(2,1)}), bf16[4,64,768]{2,1,0:T(8,128)(2,1)S(1)}, u32[]{:S(2)}, u32[]{:S(2)}) async-start(bf16[4,64,768]{2,1,0:T(8,128)(2,1)} %bitcast.4), calls=%async_computation.1 | async-start | bytes 786432 | tf_op jit(solution)/shard_map/all_to_all | solution.py:33
  152.1 13.4 %collective-permute-start.12 = (bf16[256,768]{1,0:T(8,128)(2,1)S(1)}, bf16[256,768]{1,0:T(8,128)(2,1)S(1)}, u32[]{:S(2)}, u32[]{:S(2)}) collective-permute-start(bf16[256,768]{1,0:T(8,128)(2,1)S(1)} %bitcast.25), channel_id=1, source_target_pairs={{0,1},{1,0},{2,3},{3,2},{4,5},{5,4},{6,7},{7,6},{8,9},{9,8},{10,11... | collective-permute-start | bytes 1179656 | tf_op jit(solution)/shard_map/ppermute | solution.py:29
  154.3 10.5 %collective-permute-start.6 = (bf16[32,768]{1,0:T(8,128)(2,1)S(1)}, bf16[32,768]{1,0:T(8,128)(2,1)S(1)}, u32[]{:S(2)}, u32[]{:S(2)}) collective-permute-start(bf16[32,768]{1,0:T(8,128)(2,1)S(1)} %slice.119), channel_id=1, source_target_pairs={{0,1},{1,0},{2,3},{3,2},{4,5},{5,4},{6,7},{7,6},{8,9},{9,8},{10,11... | collective-permute-start | bytes 147464 | tf_op jit(solution)/shard_map/ppermute | solution.py:29
  165.5 12.5 %collective-permute-start.13 = (bf16[256,768]{1,0:T(8,128)(2,1)S(1)}, bf16[256,768]{1,0:T(8,128)(2,1)S(1)}, u32[]{:S(2)}, u32[]{:S(2)}) collective-permute-start(bf16[256,768]{1,0:T(8,128)(2,1)S(1)} %collective-permute-done.12), channel_id=1, source_target_pairs={{0,32},{32,0},{64,96},{96,64},{128,160},{160,128},{192,224},{224,1... | collective-permute-start | bytes 1179656 | tf_op jit(solution)/shard_map/ppermute | solution.py:29
  169.3 12.5 %collective-permute-start.11 = (bf16[32,768]{1,0:T(8,128)(2,1)S(1)}, bf16[32,768]{1,0:T(8,128)(2,1)S(1)}, u32[]{:S(2)}, u32[]{:S(2)}) collective-permute-start(bf16[32,768]{1,0:T(8,128)(2,1)S(1)} %fusion.18), channel_id=1, source_target_pairs={{0,16},{1,17},{2,18},{3,19},{4,20},{5,21},{6,22},{7,23},{8,24},{9,... | collective-permute-start | bytes 147464 | tf_op jit(solution)/shard_map/ppermute | solution.py:29

commit v5 on v4

--- a/solution.py
+++ b/solution.py
@@ -59,8 +59,7 @@
             out[pl.ds((z * 2 + block) * part, part), :] = value[z * part : (z + 1) * part]
 
 
-def early_kernel(me, piece, w0, w1, cotangent, out, passed, held):
-    passed[...] = cotangent[...]
+def early_kernel(me, piece, w0, w1, out, held):
     products(me, piece, (w0, w1), held, out)
 
 
@@ -86,7 +85,19 @@
         out[...] = (late[...] + got[...].astype(F32)).astype(BF16)
 
 
-def order_kernel(me, line, across, out):
+def stack_kernel(me, mine0, mine1, got, out):
+    part = mine0.shape[0]
+    out[:part] = mine0[...]
+    out[part : 2 * part] = got[:part]
+    out[2 * part : 3 * part] = mine1[...]
+    out[3 * part :] = got[part:]
+
+
+def sum_kernel(me, mine, got, _, out):
+    out[...] = (mine[...] + got[...].astype(F32)).astype(BF16)
+
+
+def order_kernel(me, line, across, _, out):
     half = line.shape[0]
     part = half // 8
     swapped = (me[0] ^ (me[1] >> 1)) & 1
@@ -139,7 +150,7 @@
         in_specs=[pl.BlockSpec(memory_space=pltpu.SMEM)] + [vmem] * (len(args) - 1),
         out_specs=[vmem] * len(outs),
         scratch_shapes=scratch,
-        compiler_params=pltpu.CompilerParams(vmem_limit_bytes=32 * 1024 * 1024),
+        compiler_params=pltpu.CompilerParams(vmem_limit_bytes=12 * 1024 * 1024),
         cost_estimate=pl.CostEstimate(
             flops=flops, bytes_accessed=3 * 1024 * 1024, transcendentals=0
         ),
@@ -167,17 +178,15 @@
 
     size = tokens // 2
     held = [pltpu.VMEM((tokens // 4, depth), BF16)]
-    early, passed = call(
-        early_kernel,
-        [shape(size, width, F32), shape(2 * part, width, BF16)],
-        held, flops, me, line, weight, partner, cotangent,
-    )
-
-    other = swap(passed, "row", 2)
+    (early,) = call(
+        early_kernel, [shape(size, width, F32)], held, flops, me, line, weight, partner
+    )
+
+    other = swap(cotangent, "row", 2)
     pairs = [jnp.where(upper, a, b) for a, b in ((other, cotangent), (cotangent, other))]
     mine = [jnp.where(odd, p[part:], p[:part]) for p in pairs]
     got = swap(jnp.concatenate([jnp.where(odd, p[:part], p[part:]) for p in pairs]), "col", 1)
-    both = jnp.concatenate([mine[0], got[:part], mine[1], got[part:]])
+    (both,) = call(stack_kernel, [shape(4 * part, width, BF16)], [], 0, me, *mine, got)
 
     late, send = call(
         send_kernel,
@@ -193,19 +202,20 @@
     size = tokens // 8
     got = spread(mine, "row", Y_GROUPS)
     mine = total([got[y * size : (y + 1) * size] for y in range(4)])
-    pre = mine + swap(mine.astype(BF16), "row", 2).astype(F32)
+    sent = mine.astype(BF16)
+    pre = mine + swap(sent, "row", 2).astype(F32)
 
     size = tokens // 16
     value = gelu_value(jnp.where(upper, pre[size:], pre[:size])).astype(BF16)
     grad = (both.astype(F32) * gelu_slope(pre)).astype(BF16)
-    mine, got = value[:part], swap(value[part:], "col", 1)
-    output = jnp.concatenate([jnp.where(odd, got, mine), jnp.where(odd, mine, got)])
+    mine, fetched = value[:part], swap(value[part:], "col", 1)
+    output = jnp.concatenate([jnp.where(odd, fetched, mine), jnp.where(odd, mine, fetched)])
 
     g0 = lax.all_gather(grad, "row", axis=0, tiled=True, axis_index_groups=Y_GROUPS)
     g1 = swap(g0, "row", 1)
 
     size = tokens // 2
-    (near,) = call(order_kernel, [shape(size, depth, BF16)], [], 0, me, line, across)
+    (near,) = call(order_kernel, [shape(size, depth, BF16)], [], 0, me, line, across, sent)
     far = swap(near, "col", 1)
 
     size = tokens // 4
@@ -221,7 +231,10 @@
         held, flops, me, first, g1, weight, partner,
     )
 
-    mine = total([keep, swap(send, "col", 2)]).astype(BF16)
+    (mine,) = call(
+        sum_kernel, [shape(size, depth, BF16)], [], size * depth,
+        me, keep, swap(send, "col", 2), fetched,
+    )
     size = tokens // 16
     got = spread(mine, "col", Z_GROUPS)
     mine = total([got[k * size : (k + 1) * size] for k in range(4)])

time: 183 us -> 180 us (0.984)
  starting transfers between devices: 100 us -> 93.8 us
  waiting for transfers between devices: 31.3 us -> 35.4 us
    ppermute x14, starting transfers between devices: 92.5 us -> 83.5 us  [swap(): return lax.ppermute(value, axis, [(i, i ^ mask) for i in range(size)])]
    all_to_all x2, waiting for transfers between devices: 4.19 us -> 11.7 us  [spread(): lax.all_to_all(value, axis, split_axis=0, concat_axis=0, axis_index_group...]
    ppermute x14, waiting for transfers between devices: 27.1 us -> 23.7 us  [swap(): return lax.ppermute(value, axis, [(i, i ^ mask) for i in range(size)])]
    all_to_all x2, starting transfers between devices: 7.94 us -> 10.2 us  [spread(): lax.all_to_all(value, axis, split_axis=0, concat_axis=0, axis_index_group...]
    pallas_call x6 -> x8, Pallas kernels: 9.17 us -> 9.56 us  [call(): pl.pallas_call(kernel, out_shape=outs, in_specs=[pl.BlockSpec(memory_spac...]
  transfers between devices with their start and end apart: 16 -> 16, of which waited for: 8 -> 8; matrix products, arithmetic and copies ran while one was open for 5% -> 5% of each run, Pallas kernels for 3% -> 2%
where the time goes in v5:
time: 180 us; the launch traced here: 179 us
  starting transfers between devices  93.8 us (52%)
  waiting for transfers between devices  35.4 us (20%)
  blocking collectives  27.6 us (15%)
  Pallas kernels  9.56 us (5%)
  other arithmetic  6.2 us (3%)
  matrix products  3.45 us (2%)
  local copies, waits for them, and re-layouts  2.15 us (1%)
    ppermute x14, starting transfers between devices, swap(): return lax.ppermute(value, axis, [(i, i ^ mask) for i in range(size)])  83.5 us
    ppermute x14, waiting for transfers between devices, swap(): return lax.ppermute(value, axis, [(i, i ^ mask) for i in range(size)])  23.7 us
    all_gather x1, blocking collectives, shards(): lax.all_gather(pair, 'col', axis=0, tiled=True, axis_index_groups=Z_GROUPS)  15.8 us
    all_gather x1, blocking collectives, shards(): lax.all_gather(grad, 'row', axis=0, tiled=True, axis_index_groups=Y_GROUPS)  11.8 us
    all_to_all x2, waiting for transfers between devices, spread(): lax.all_to_all(value, axis, split_axis=0, concat_axis=0, axis_index_group...  11.7 us
    all_to_all x2, starting transfers between devices, spread(): lax.all_to_all(value, axis, split_axis=0, concat_axis=0, axis_index_group...  10.2 us
    pallas_call x8, Pallas kernels, call(): pl.pallas_call(kernel, out_shape=outs, in_specs=[pl.BlockSpec(memory_spac...  9.56 us
  transfers between devices with their start and end apart: 16, of which 8 were waited for; matrix products, arithmetic and copies ran while one was open for 5% of the time, Pallas kernels for 2%

profile of v5, /device:TPU:1, one launch (start us, length us, event | category | flops | bytes accessed | tf_op | source)
XLA Modules:
  0.0 179.1 jit_solution(14729656680018749844)
XLA Ops:
  0.6 4.0 %collective-permute-start.1 = (bf16[768,768]{1,0:T(8,128)(2,1)}, bf16[768,768]{1,0:T(8,128)(2,1)S(1)}, u32[]{:S(2)}, u32[]{:S(2)}) collective-permute-start(bf16[768,768]{1,0:T(8,128)(2,1)} %w0.7), channel_id=1, source_target_pairs={{0,1},{1,0},{2,3},{3,2},{4,5},{5,4},{6,7},{7,6},{8,9},{9,8},{10,11... | collective-permute-start | bytes 3538952 | tf_op jit(solution)/shard_map/ppermute | solution.py:29
  4.6 8.8 %collective-permute-start = (bf16[32,768]{1,0:T(8,128)(2,1)}, bf16[32,768]{1,0:T(8,128)(2,1)S(1)}, u32[]{:S(2)}, u32[]{:S(2)}) collective-permute-start(bf16[32,768]{1,0:T(8,128)(2,1)} %param.3), channel_id=1, source_target_pairs={{0,16},{1,17},{2,18},{3,19},{4,20},{5,21},{6,22},{7,23},{8,24},{9,... | collective-permute-start | bytes 147464 | tf_op jit(solution)/shard_map/ppermute | solution.py:29
  13.4 1.7 collective-permute-done
  15.9 15.8 %all_gather.6.piece.line = bf16[256,768]{1,0:T(8,128)(2,1)S(1)} all-gather(bf16[64,768]{1,0:T(8,128)(2,1)S(1)} %pad_maximum_fusion), channel_id=1, replica_groups={{0,4,8,12},{1,5,9,13},{2,6,10,14},{3,7,11,15},{16,20,24,28},{17,21,25,2..., dimensions={0}, use_global_device_ids=true | all-gather | bytes 491520 | tf_op jit(solution)/shard_map/all_gather | solution.py:176
  31.7 4.4 %collective-permute-start.2 = (bf16[256,768]{1,0:T(8,128)(2,1)S(1)}, bf16[256,768]{1,0:T(8,128)(2,1)S(1)}, u32[]{:S(2)}, u32[]{:S(2)}) collective-permute-start(bf16[256,768]{1,0:T(8,128)(2,1)S(1)} %all_gather.6.piece.line), channel_id=1, source_target_pairs={{0,2},{1,3},{2,0},{3,1},{4,6},{5,7},{6,4},{7,5},{8,10},{9,11},{10,... | collective-permute-start | bytes 1179656 | tf_op jit(solution)/shard_map/ppermute | solution.py:29
  36.1 10.8 %collective-permute-start.3 = (bf16[64,768]{1,0:T(8,128)(2,1)}, bf16[64,768]{1,0:T(8,128)(2,1)S(1)}, u32[]{:S(2)}, u32[]{:S(2)}) collective-permute-start(bf16[64,768]{1,0:T(8,128)(2,1)} %param.5), channel_id=1, source_target_pairs={{0,64},{32,96},{64,0},{96,32},{128,192},{160,224},{192,128},{224,1... | collective-permute-start | bytes 294920 | tf_op jit(solution)/shard_map/ppermute | solution.py:29
  50.5 1.4 shard_map.59
  51.9 8.2 %collective-permute-start.4 = (bf16[512,768]{1,0:T(8,128)(2,1)S(1)}, bf16[512,768]{1,0:T(8,128)(2,1)S(1)}, u32[]{:S(2)}, u32[]{:S(2)}) collective-permute-start(bf16[512,768]{1,0:T(8,128)(2,1)S(1)} %get-tuple-element.8), channel_id=1, source_target_pairs={{0,32},{32,0},{64,96},{96,64},{128,160},{160,128},{192,224},{224,1... | collective-permute-start | bytes 2359304 | tf_op jit(solution)/shard_map/ppermute | solution.py:29
  60.1 1.9 %collective-permute-done.4.got = bf16[512,768]{1,0:T(8,128)(2,1)S(1)} collective-permute-done((bf16[512,768]{1,0:T(8,128)(2,1)S(1)}, bf16[512,768]{1,0:T(8,128)(2,1)S(1)}, u32[]{:S(2)}, u32[]{:S(2)}) %collective-permute-start.4) | collective-permute-done | bytes 786464 | tf_op jit(solution)/shard_map/ppermute | solution.py:29
  61.9 1.6 shard_map.60
  63.5 4.3 %all-to-all-start = ((bf16[4,128,768]{2,1,0:T(8,128)(2,1)}), bf16[4,128,768]{2,1,0:T(8,128)(2,1)}, u32[]{:S(2)}, u32[]{:S(2)}) async-start(bf16[4,128,768]{2,1,0:T(8,128)(2,1)} %bitcast.2), calls=%async_computation | async-start | bytes 1572864 | tf_op jit(solution)/shard_map/all_to_all | solution.py:33
  67.9 11.7 %all-to-all-done = bf16[4,128,768]{2,1,0:T(8,128)(2,1)} async-done(((bf16[4,128,768]{2,1,0:T(8,128)(2,1)}), bf16[4,128,768]{2,1,0:T(8,128)(2,1)}, u32[]{:S(2)}, u32[]{:S(2)}) %all-to-all-start) | async-done | bytes 786464 | tf_op jit(solution)/shard_map/all_to_all | solution.py:33
  79.6 1.3 bitcast_convert_fusion._
  81.0 12.6 %collective-permute-start.5 = (bf16[128,768]{1,0:T(8,128)(2,1)S(1)}, bf16[128,768]{1,0:T(8,128)(2,1)S(1)}, u32[]{:S(2)}, u32[]{:S(2)}) collective-permute-start(bf16[128,768]{1,0:T(8,128)(2,1)S(1)} %bitcast_convert_fusion._), channel_id=1, source_target_pairs={{0,64},{32,96},{64,0},{96,32},{128,192},{160,224},{192,128},{224,1... | collective-permute-start | bytes 589832 | tf_op jit(solution)/shard_map/ppermute | solution.py:29
  93.6 1.9 %collective-permute-start.7 = (bf16[64,768]{1,0:T(8,128)(2,1)S(1)}, bf16[64,768]{1,0:T(8,128)(2,1)S(1)}, u32[]{:S(2)}, u32[]{:S(2)}) collective-permute-start(bf16[64,768]{1,0:T(8,128)(2,1)S(1)} %pad_maximum_fusion.2), channel_id=1, source_target_pairs={{0,1},{1,0},{2,3},{3,2},{4,5},{5,4},{6,7},{7,6},{8,9},{9,8},{10,11... | collective-permute-start | bytes 294920 | tf_op jit(solution)/shard_map/ppermute | solution.py:29
  95.6 3.5 %collective-permute-done.7.got = bf16[64,768]{1,0:T(8,128)(2,1)S(1)} collective-permute-done((bf16[64,768]{1,0:T(8,128)(2,1)S(1)}, bf16[64,768]{1,0:T(8,128)(2,1)S(1)}, u32[]{:S(2)}, u32[]{:S(2)}) %collective-permute-start.7) | collective-permute-done | bytes 98336 | tf_op jit(solution)/shard_map/ppermute | solution.py:29
  100.2 1.9 %collective-permute-start.8 = (bf16[512,768]{1,0:T(8,128)(2,1)S(1)}, bf16[512,768]{1,0:T(8,128)(2,1)S(1)}, u32[]{:S(2)}, u32[]{:S(2)}) collective-permute-start(bf16[512,768]{1,0:T(8,128)(2,1)S(1)} %shard_map.62), channel_id=1, source_target_pairs={{0,1},{1,0},{2,3},{3,2},{4,5},{5,4},{6,7},{7,6},{8,9},{9,8},{10,11... | collective-permute-start | bytes 2359304 | tf_op jit(solution)/shard_map/ppermute | solution.py:29
  102.2 1.5 fusion.15
  103.7 11.8 %all_gather.7.grad = bf16[512,768]{1,0:T(8,128)(2,1)S(1)} all-gather(bf16[128,768]{1,0:T(8,128)(2,1)S(1)} %get-tuple-element.11), channel_id=1, replica_groups={{0,128,256,384},{32,160,288,416},{64,192,320,448},{96,224,352,480},{1,1..., dimensions={0}, use_global_device_ids=true | all-gather | bytes 983040 | tf_op jit(solution)/shard_map/all_gather | solution.py:214
  115.5 6.5 %collective-permute-start.9 = (bf16[512,768]{1,0:T(8,128)(2,1)S(1)}, bf16[512,768]{1,0:T(8,128)(2,1)S(1)}, u32[]{:S(2)}, u32[]{:S(2)}) collective-permute-start(bf16[512,768]{1,0:T(8,128)(2,1)S(1)} %all_gather.7.grad), channel_id=1, source_target_pairs={{0,32},{32,0},{64,96},{96,64},{128,160},{160,128},{192,224},{224,1... | collective-permute-start | bytes 2359304 | tf_op jit(solution)/shard_map/ppermute | solution.py:29
  122.0 1.3 shard_map.63.first
  123.9 1.4 shard_map.64
  125.4 3.6 %collective-permute-start.10 = (bf16[256,768]{1,0:T(8,128)(2,1)S(1)}, bf16[256,768]{1,0:T(8,128)(2,1)S(1)}, u32[]{:S(2)}, u32[]{:S(2)}) collective-permute-start(bf16[256,768]{1,0:T(8,128)(2,1)S(1)} %get-tuple-element.10), channel_id=1, source_target_pairs={{0,2},{1,3},{2,0},{3,1},{4,6},{5,7},{6,4},{7,5},{8,10},{9,11},{10,... | collective-permute-start | bytes 1179656 | tf_op jit(solution)/shard_map/ppermute | solution.py:29
  129.0 4.4 %collective-permute-start.6 = (bf16[32,768]{1,0:T(8,128)(2,1)S(1)}, bf16[32,768]{1,0:T(8,128)(2,1)S(1)}, u32[]{:S(2)}, u32[]{:S(2)}) collective-permute-start(bf16[32,768]{1,0:T(8,128)(2,1)S(1)} %slice.111), channel_id=1, source_target_pairs={{0,1},{1,0},{2,3},{3,2},{4,5},{5,4},{6,7},{7,6},{8,9},{9,8},{10,11... | collective-permute-start | bytes 147464 | tf_op jit(solution)/shard_map/ppermute | solution.py:29
  133.4 7.6 %collective-permute-done.6._ = bf16[32,768]{1,0:T(8,128)(2,1)S(1)} collective-permute-done((bf16[32,768]{1,0:T(8,128)(2,1)S(1)}, bf16[32,768]{1,0:T(8,128)(2,1)S(1)}, u32[]{:S(2)}, u32[]{:S(2)}) %collective-permute-start.6) | collective-permute-done | bytes 49184 | tf_op jit(solution)/shard_map/ppermute | solution.py:29
  141.0 1.4 shard_map.65
  142.4 5.9 %all-to-all-start.1 = ((bf16[4,64,768]{2,1,0:T(8,128)(2,1)}), bf16[4,64,768]{2,1,0:T(8,128)(2,1)}, u32[]{:S(2)}, u32[]{:S(2)}) async-start(bf16[4,64,768]{2,1,0:T(8,128)(2,1)} %bitcast.4), calls=%async_computation.1 | async-start | bytes 786432 | tf_op jit(solution)/shard_map/all_to_all | solution.py:33
  149.1 2.4 %collective-permute-start.12 = (bf16[256,768]{1,0:T(8,128)(2,1)S(1)}, bf16[256,768]{1,0:T(8,128)(2,1)}, u32[]{:S(2)}, u32[]{:S(2)}) collective-permute-start(bf16[256,768]{1,0:T(8,128)(2,1)S(1)} %bitcast.25), channel_id=1, source_target_pairs={{0,1},{1,0},{2,3},{3,2},{4,5},{5,4},{6,7},{7,6},{8,9},{9,8},{10,11... | collective-permute-start | bytes 1179656 | tf_op jit(solution)/shard_map/ppermute | solution.py:29
  152.2 7.6 %collective-permute-done.12 = bf16[256,768]{1,0:T(8,128)(2,1)} collective-permute-done((bf16[256,768]{1,0:T(8,128)(2,1)S(1)}, bf16[256,768]{1,0:T(8,128)(2,1)}, u32[]{:S(2)}, u32[]{:S(2)}) %collective-permute-start.12) | collective-permute-done | bytes 393248 | tf_op jit(solution)/shard_map/ppermute | solution.py:29
  159.8 4.9 %collective-permute-start.13 = (bf16[256,768]{1,0:T(8,128)(2,1)}, bf16[256,768]{1,0:T(8,128)(2,1)S(1)}, u32[]{:S(2)}, u32[]{:S(2)}) collective-permute-start(bf16[256,768]{1,0:T(8,128)(2,1)} %collective-permute-done.12), channel_id=1, source_target_pairs={{0,32},{32,0},{64,96},{96,64},{128,160},{160,128},{192,224},{224,1... | collective-permute-start | bytes 1179656 | tf_op jit(solution)/shard_map/ppermute | solution.py:29
  165.8 9.2 %collective-permute-start.11 = (bf16[32,768]{1,0:T(8,128)(2,1)S(1)}, bf16[32,768]{1,0:T(8,128)(2,1)S(1)}, u32[]{:S(2)}, u32[]{:S(2)}) collective-permute-start(bf16[32,768]{1,0:T(8,128)(2,1)S(1)} %fusion.18), channel_id=1, source_target_pairs={{0,16},{1,17},{2,18},{3,19},{4,20},{5,21},{6,22},{7,23},{8,24},{9,... | collective-permute-start | bytes 147464 | tf_op jit(solution)/shard_map/ppermute | solution.py:29
  175.0 3.5 %multiply_convert_fusion = bf16[768,768]{1,0:T(8,128)(2,1)} fusion(bf16[512,768]{1,0:T(8,128)(2,1)S(1)} %copy-done.5, bf16[512,768]{1,0:T(8,128)(2,1)S(1)} %copy-done.7, bf16[256,768]{1,0:T(8,128)(2,1)S(1)} %collective-permute-done.13, bf16[256,768]{1,0:T(8,128)(2,1)} %collective-permute-done.12, bf16[256,768]{1,0:T(8,128)(2,1)S(1)} %bitcast.23, ...), kind=kOutput, calls=%fused_computation | convolution fusion | flops 1218576384 | bytes 4325376 | tf_op jit(solution)/shard_map/dot_general | solution.py:247
  (47 shorter events, 9.4 us)
Async XLA Ops:
  0.6 46.4 %collective-permute-start.1 = (bf16[768,768]{1,0:T(8,128)(2,1)}, bf16[768,768]{1,0:T(8,128)(2,1)S(1)}, u32[]{:S(2)}, u32[]{:S(2)}) collective-permute-start(bf16[768,768]{1,0:T(8,128)(2,1)} %w0.7), channel_id=1, source_target_pairs={{0,1},{1,0},{2,3},{3,2},{4,5},{5,4},{6,7},{7,6},{8,9},{9,8},{10,11... | collective-permute-start | bytes 3538952 | tf_op jit(solution)/shard_map/ppermute | solution.py:29
  4.6 10.5 %collective-permute-start = (bf16[32,768]{1,0:T(8,128)(2,1)}, bf16[32,768]{1,0:T(8,128)(2,1)S(1)}, u32[]{:S(2)}, u32[]{:S(2)}) collective-permute-start(bf16[32,768]{1,0:T(8,128)(2,1)} %param.3), channel_id=1, source_target_pairs={{0,16},{1,17},{2,18},{3,19},{4,20},{5,21},{6,22},{7,23},{8,24},{9,... | collective-permute-start | bytes 147464 | tf_op jit(solution)/shard_map/ppermute | solution.py:29
  31.7 18.8 %collective-permute-start.2 = (bf16[256,768]{1,0:T(8,128)(2,1)S(1)}, bf16[256,768]{1,0:T(8,128)(2,1)S(1)}, u32[]{:S(2)}, u32[]{:S(2)}) collective-permute-start(bf16[256,768]{1,0:T(8,128)(2,1)S(1)} %all_gather.6.piece.line), channel_id=1, source_target_pairs={{0,2},{1,3},{2,0},{3,1},{4,6},{5,7},{6,4},{7,5},{8,10},{9,11},{10,... | collective-permute-start | bytes 1179656 | tf_op jit(solution)/shard_map/ppermute | solution.py:29
  36.1 14.4 %collective-permute-start.3 = (bf16[64,768]{1,0:T(8,128)(2,1)}, bf16[64,768]{1,0:T(8,128)(2,1)S(1)}, u32[]{:S(2)}, u32[]{:S(2)}) collective-permute-start(bf16[64,768]{1,0:T(8,128)(2,1)} %param.5), channel_id=1, source_target_pairs={{0,64},{32,96},{64,0},{96,32},{128,192},{160,224},{192,128},{224,1... | collective-permute-start | bytes 294920 | tf_op jit(solution)/shard_map/ppermute | solution.py:29
  47.0 1.3 copy-start
  48.3 2.2 %copy-start.1 = (bf16[768,768]{1,0:T(8,128)(2,1)S(1)}, bf16[768,768]{1,0:T(8,128)(2,1)}, u32[]{:S(2)}) copy-start(bf16[768,768]{1,0:T(8,128)(2,1)} %w0.7) | copy-start | bytes 3538948
  51.9 10.1 %collective-permute-start.4 = (bf16[512,768]{1,0:T(8,128)(2,1)S(1)}, bf16[512,768]{1,0:T(8,128)(2,1)S(1)}, u32[]{:S(2)}, u32[]{:S(2)}) collective-permute-start(bf16[512,768]{1,0:T(8,128)(2,1)S(1)} %get-tuple-element.8), channel_id=1, source_target_pairs={{0,32},{32,0},{64,96},{96,64},{128,160},{160,128},{192,224},{224,1... | collective-permute-start | bytes 2359304 | tf_op jit(solution)/shard_map/ppermute | solution.py:29
  63.5 4.4 %copy-start.9 = (bf16[64,768]{1,0:T(8,128)(2,1)S(1)}, bf16[64,768]{1,0:T(8,128)(2,1)}, u32[]{:S(2)}) copy-start(bf16[64,768]{1,0:T(8,128)(2,1)} %param.5) | copy-start | bytes 294916
  63.5 16.1 %all-to-all-start = ((bf16[4,128,768]{2,1,0:T(8,128)(2,1)}), bf16[4,128,768]{2,1,0:T(8,128)(2,1)}, u32[]{:S(2)}, u32[]{:S(2)}) async-start(bf16[4,128,768]{2,1,0:T(8,128)(2,1)} %bitcast.2), calls=%async_computation | async-start | bytes 1572864 | tf_op jit(solution)/shard_map/all_to_all | solution.py:33
  81.0 21.2 %collective-permute-start.5 = (bf16[128,768]{1,0:T(8,128)(2,1)S(1)}, bf16[128,768]{1,0:T(8,128)(2,1)S(1)}, u32[]{:S(2)}, u32[]{:S(2)}) collective-permute-start(bf16[128,768]{1,0:T(8,128)(2,1)S(1)} %bitcast_convert_fusion._), channel_id=1, source_target_pairs={{0,64},{32,96},{64,0},{96,32},{128,192},{160,224},{192,128},{224,1... | collective-permute-start | bytes 589832 | tf_op jit(solution)/shard_map/ppermute | solution.py:29
  93.6 5.4 %collective-permute-start.7 = (bf16[64,768]{1,0:T(8,128)(2,1)S(1)}, bf16[64,768]{1,0:T(8,128)(2,1)S(1)}, u32[]{:S(2)}, u32[]{:S(2)}) collective-permute-start(bf16[64,768]{1,0:T(8,128)(2,1)S(1)} %pad_maximum_fusion.2), channel_id=1, source_target_pairs={{0,1},{1,0},{2,3},{3,2},{4,5},{5,4},{6,7},{7,6},{8,9},{9,8},{10,11... | collective-permute-start | bytes 294920 | tf_op jit(solution)/shard_map/ppermute | solution.py:29
  100.2 23.2 %copy-start.6 = (bf16[512,768]{1,0:T(8,128)(2,1)}, bf16[512,768]{1,0:T(8,128)(2,1)S(1)}, u32[]{:S(2)}) copy-start(bf16[512,768]{1,0:T(8,128)(2,1)S(1)} %shard_map.62) | copy-start | bytes 2359300
  100.2 21.8 %collective-permute-start.8 = (bf16[512,768]{1,0:T(8,128)(2,1)S(1)}, bf16[512,768]{1,0:T(8,128)(2,1)S(1)}, u32[]{:S(2)}, u32[]{:S(2)}) collective-permute-start(bf16[512,768]{1,0:T(8,128)(2,1)S(1)} %shard_map.62), channel_id=1, source_target_pairs={{0,1},{1,0},{2,3},{3,2},{4,5},{5,4},{6,7},{7,6},{8,9},{9,8},{10,11... | collective-permute-start | bytes 2359304 | tf_op jit(solution)/shard_map/ppermute | solution.py:29
  115.5 8.4 %collective-permute-start.9 = (bf16[512,768]{1,0:T(8,128)(2,1)S(1)}, bf16[512,768]{1,0:T(8,128)(2,1)S(1)}, u32[]{:S(2)}, u32[]{:S(2)}) collective-permute-start(bf16[512,768]{1,0:T(8,128)(2,1)S(1)} %all_gather.7.grad), channel_id=1, source_target_pairs={{0,32},{32,0},{64,96},{96,64},{128,160},{160,128},{192,224},{224,1... | collective-permute-start | bytes 2359304 | tf_op jit(solution)/shard_map/ppermute | solution.py:29
  122.0 1.4 copy-start.4
  123.9 1.4 copy-start.2
  125.4 15.7 %collective-permute-start.10 = (bf16[256,768]{1,0:T(8,128)(2,1)S(1)}, bf16[256,768]{1,0:T(8,128)(2,1)S(1)}, u32[]{:S(2)}, u32[]{:S(2)}) collective-permute-start(bf16[256,768]{1,0:T(8,128)(2,1)S(1)} %get-tuple-element.10), channel_id=1, source_target_pairs={{0,2},{1,3},{2,0},{3,1},{4,6},{5,7},{6,4},{7,5},{8,10},{9,11},{10,... | collective-permute-start | bytes 1179656 | tf_op jit(solution)/shard_map/ppermute | solution.py:29
  129.0 12.0 %collective-permute-start.6 = (bf16[32,768]{1,0:T(8,128)(2,1)S(1)}, bf16[32,768]{1,0:T(8,128)(2,1)S(1)}, u32[]{:S(2)}, u32[]{:S(2)}) collective-permute-start(bf16[32,768]{1,0:T(8,128)(2,1)S(1)} %slice.111), channel_id=1, source_target_pairs={{0,1},{1,0},{2,3},{3,2},{4,5},{5,4},{6,7},{7,6},{8,9},{9,8},{10,11... | collective-permute-start | bytes 147464 | tf_op jit(solution)/shard_map/ppermute | solution.py:29
  142.4 22.3 %copy-start.3 = (bf16[512,768]{1,0:T(8,128)(2,1)S(1)}, bf16[512,768]{1,0:T(8,128)(2,1)}, u32[]{:S(2)}) copy-start(bf16[512,768]{1,0:T(8,128)(2,1)} %copy-done.2) | copy-start | bytes 2359300
  142.4 22.3 %all-to-all-start.1 = ((bf16[4,64,768]{2,1,0:T(8,128)(2,1)}), bf16[4,64,768]{2,1,0:T(8,128)(2,1)}, u32[]{:S(2)}, u32[]{:S(2)}) async-start(bf16[4,64,768]{2,1,0:T(8,128)(2,1)} %bitcast.4), calls=%async_computation.1 | async-start | bytes 786432 | tf_op jit(solution)/shard_map/all_to_all | solution.py:33
  148.3 26.7 %copy-start.5 = (bf16[512,768]{1,0:T(8,128)(2,1)S(1)}, bf16[512,768]{1,0:T(8,128)(2,1)}, u32[]{:S(2)}) copy-start(bf16[512,768]{1,0:T(8,128)(2,1)} %copy-done.4) | copy-start | bytes 2359300
  148.3 26.7 %copy-start.7 = (bf16[512,768]{1,0:T(8,128)(2,1)S(1)}, bf16[512,768]{1,0:T(8,128)(2,1)}, u32[]{:S(2)}) copy-start(bf16[512,768]{1,0:T(8,128)(2,1)} %copy-done.6) | copy-start | bytes 2359300
  149.1 25.9 %copy-start.8 = (bf16[8,1,32,768]{3,2,1,0:T(8,128)(2,1)S(1)}, bf16[8,1,32,768]{3,2,1,0:T(8,128)(2,1)}, u32[]{:S(2)}) copy-start(bf16[8,1,32,768]{3,2,1,0:T(8,128)(2,1)} %get-tuple-element.13) | copy-start | bytes 1179652
  149.1 10.7 %collective-permute-start.12 = (bf16[256,768]{1,0:T(8,128)(2,1)S(1)}, bf16[256,768]{1,0:T(8,128)(2,1)}, u32[]{:S(2)}, u32[]{:S(2)}) collective-permute-start(bf16[256,768]{1,0:T(8,128)(2,1)S(1)} %bitcast.25), channel_id=1, source_target_pairs={{0,1},{1,0},{2,3},{3,2},{4,5},{5,4},{6,7},{7,6},{8,9},{9,8},{10,11... | collective-permute-start | bytes 1179656 | tf_op jit(solution)/shard_map/ppermute | solution.py:29
  159.8 15.2 %collective-permute-start.13 = (bf16[256,768]{1,0:T(8,128)(2,1)}, bf16[256,768]{1,0:T(8,128)(2,1)S(1)}, u32[]{:S(2)}, u32[]{:S(2)}) collective-permute-start(bf16[256,768]{1,0:T(8,128)(2,1)} %collective-permute-done.12), channel_id=1, source_target_pairs={{0,32},{32,0},{64,96},{96,64},{128,160},{160,128},{192,224},{224,1... | collective-permute-start | bytes 1179656 | tf_op jit(solution)/shard_map/ppermute | solution.py:29
  165.8 12.7 %collective-permute-start.11 = (bf16[32,768]{1,0:T(8,128)(2,1)S(1)}, bf16[32,768]{1,0:T(8,128)(2,1)S(1)}, u32[]{:S(2)}, u32[]{:S(2)}) collective-permute-start(bf16[32,768]{1,0:T(8,128)(2,1)S(1)} %fusion.18), channel_id=1, source_target_pairs={{0,16},{1,17},{2,18},{3,19},{4,20},{5,21},{6,22},{7,23},{8,24},{9,... | collective-permute-start | bytes 147464 | tf_op jit(solution)/shard_map/ppermute | solution.py:29

commit v6 on v5

--- a/solution.py
+++ b/solution.py
@@ -85,16 +85,13 @@
         out[...] = (late[...] + got[...].astype(F32)).astype(BF16)
 
 
-def stack_kernel(me, mine0, mine1, got, out):
+def stack_kernel(me, mine0, mine1, got, value, out, passed):
+    passed[...] = value[...]
     part = mine0.shape[0]
     out[:part] = mine0[...]
     out[part : 2 * part] = got[:part]
     out[2 * part : 3 * part] = mine1[...]
     out[3 * part :] = got[part:]
-
-
-def sum_kernel(me, mine, got, _, out):
-    out[...] = (mine[...] + got[...].astype(F32)).astype(BF16)
 
 
 def order_kernel(me, line, across, _, out):
@@ -186,7 +183,7 @@
     pairs = [jnp.where(upper, a, b) for a, b in ((other, cotangent), (cotangent, other))]
     mine = [jnp.where(odd, p[part:], p[:part]) for p in pairs]
     got = swap(jnp.concatenate([jnp.where(odd, p[:part], p[part:]) for p in pairs]), "col", 1)
-    (both,) = call(stack_kernel, [shape(4 * part, width, BF16)], [], 0, me, *mine, got)
+    cotangents = [*mine, got]
 
     late, send = call(
         send_kernel,
@@ -202,7 +199,9 @@
     size = tokens // 8
     got = spread(mine, "row", Y_GROUPS)
     mine = total([got[y * size : (y + 1) * size] for y in range(4)])
-    sent = mine.astype(BF16)
+    both, sent = call(
+        stack_kernel, [shape(size, width, BF16)] * 2, [], 0, me, *cotangents, mine.astype(BF16)
+    )
     pre = mine + swap(sent, "row", 2).astype(F32)
 
     size = tokens // 16
@@ -231,10 +230,7 @@
         held, flops, me, first, g1, weight, partner,
     )
 
-    (mine,) = call(
-        sum_kernel, [shape(size, depth, BF16)], [], size * depth,
-        me, keep, swap(send, "col", 2), fetched,
-    )
+    mine = total([keep, swap(send, "col", 2)]).astype(BF16)
     size = tokens // 16
     got = spread(mine, "col", Z_GROUPS)
     mine = total([got[k * size : (k + 1) * size] for k in range(4)])

time: 180 us -> 180 us (level)
  waiting for transfers between devices: 35.4 us -> 32.7 us
  starting transfers between devices: 93.8 us -> 96.2 us
    all_to_all x2, starting transfers between devices: 10.2 us -> 17.5 us  [spread(): lax.all_to_all(value, axis, split_axis=0, concat_axis=0, axis_index_group...]
    ppermute x14, starting transfers between devices: 83.5 us -> 78.6 us  [swap(): return lax.ppermute(value, axis, [(i, i ^ mask) for i in range(size)])]
    all_to_all x2, waiting for transfers between devices: 11.7 us -> 9.77 us  [spread(): lax.all_to_all(value, axis, split_axis=0, concat_axis=0, axis_index_group...]
    pallas_call x8 -> x7, Pallas kernels: 9.56 us -> 8.22 us  [call(): pl.pallas_call(kernel, out_shape=outs, in_specs=[pl.BlockSpec(memory_spac...]
  transfers between devices with their start and end apart: 16 -> 16, of which waited for: 8 -> 8; matrix products, arithmetic and copies ran while one was open for 5% -> 6% of each run, Pallas kernels for 2% -> 2%
where the time goes in v6:
time: 180 us
  starting transfers between devices  96.2 us (53%)
  waiting for transfers between devices  32.7 us (18%)
  blocking collectives  28 us (16%)
  Pallas kernels  8.22 us (5%)
  other arithmetic  7.75 us (4%)
  matrix products  3.69 us (2%)
  local copies, waits for them, and re-layouts  2.15 us (1%)
    ppermute x14, starting transfers between devices, swap(): return lax.ppermute(value, axis, [(i, i ^ mask) for i in range(size)])  78.6 us
    ppermute x14, waiting for transfers between devices, swap(): return lax.ppermute(value, axis, [(i, i ^ mask) for i in range(size)])  22.9 us
    all_to_all x2, starting transfers between devices, spread(): lax.all_to_all(value, axis, split_axis=0, concat_axis=0, axis_index_group...  17.5 us
    all_gather x1, blocking collectives, shards(): lax.all_gather(pair, 'col', axis=0, tiled=True, axis_index_groups=Z_GROUPS)  15.8 us
    all_gather x1, blocking collectives, shards(): lax.all_gather(grad, 'row', axis=0, tiled=True, axis_index_groups=Y_GROUPS)  12.2 us
    all_to_all x2, waiting for transfers between devices, spread(): lax.all_to_all(value, axis, split_axis=0, concat_axis=0, axis_index_group...  9.77 us
    pallas_call x7, Pallas kernels, call(): pl.pallas_call(kernel, out_shape=outs, in_specs=[pl.BlockSpec(memory_spac...  8.22 us
    dot_general x1, matrix products, shards(): lax.dot_general(jnp.concatenate([near, far]), jnp.concatenate(own + other...  3.69 us
  transfers between devices with their start and end apart: 16, of which 8 were waited for; matrix products, arithmetic and copies ran while one was open for 6% of the time, Pallas kernels for 2%

profile of v6, /device:TPU:1, one launch (start us, length us, event | category | flops | bytes accessed | tf_op | source)
XLA Modules:
  0.0 179.6 jit_solution(17988217773547259118)
XLA Ops:
  0.6 4.0 %collective-permute-start.1 = (bf16[768,768]{1,0:T(8,128)(2,1)}, bf16[768,768]{1,0:T(8,128)(2,1)S(1)}, u32[]{:S(2)}, u32[]{:S(2)}) collective-permute-start(bf16[768,768]{1,0:T(8,128)(2,1)} %w0.7), channel_id=1, source_target_pairs={{0,1},{1,0},{2,3},{3,2},{4,5},{5,4},{6,7},{7,6},{8,9},{9,8},{10,11... | collective-permute-start | bytes 3538952 | tf_op jit(solution)/shard_map/ppermute | solution.py:29
  4.6 8.8 %collective-permute-start = (bf16[32,768]{1,0:T(8,128)(2,1)}, bf16[32,768]{1,0:T(8,128)(2,1)S(1)}, u32[]{:S(2)}, u32[]{:S(2)}) collective-permute-start(bf16[32,768]{1,0:T(8,128)(2,1)} %param.3), channel_id=1, source_target_pairs={{0,16},{1,17},{2,18},{3,19},{4,20},{5,21},{6,22},{7,23},{8,24},{9,... | collective-permute-start | bytes 147464 | tf_op jit(solution)/shard_map/ppermute | solution.py:29
  13.4 1.7 collective-permute-done
  15.9 15.8 %all_gather.6.piece.line = bf16[256,768]{1,0:T(8,128)(2,1)S(1)} all-gather(bf16[64,768]{1,0:T(8,128)(2,1)S(1)} %pad_maximum_fusion), channel_id=1, replica_groups={{0,4,8,12},{1,5,9,13},{2,6,10,14},{3,7,11,15},{16,20,24,28},{17,21,25,2..., dimensions={0}, use_global_device_ids=true | all-gather | bytes 491520 | tf_op jit(solution)/shard_map/all_gather | solution.py:173
  31.7 4.4 %collective-permute-start.2 = (bf16[256,768]{1,0:T(8,128)(2,1)S(1)}, bf16[256,768]{1,0:T(8,128)(2,1)S(1)}, u32[]{:S(2)}, u32[]{:S(2)}) collective-permute-start(bf16[256,768]{1,0:T(8,128)(2,1)S(1)} %all_gather.6.piece.line), channel_id=1, source_target_pairs={{0,2},{1,3},{2,0},{3,1},{4,6},{5,7},{6,4},{7,5},{8,10},{9,11},{10,... | collective-permute-start | bytes 1179656 | tf_op jit(solution)/shard_map/ppermute | solution.py:29
  36.1 10.8 %collective-permute-start.3 = (bf16[64,768]{1,0:T(8,128)(2,1)}, bf16[64,768]{1,0:T(8,128)(2,1)S(1)}, u32[]{:S(2)}, u32[]{:S(2)}) collective-permute-start(bf16[64,768]{1,0:T(8,128)(2,1)} %param.5), channel_id=1, source_target_pairs={{0,64},{32,96},{64,0},{96,32},{128,192},{160,224},{192,128},{224,1... | collective-permute-start | bytes 294920 | tf_op jit(solution)/shard_map/ppermute | solution.py:29
  47.0 1.3 copy-done
  48.3 1.3 shard_map.58.early
  50.5 1.4 shard_map.59
  51.9 8.2 %collective-permute-start.4 = (bf16[512,768]{1,0:T(8,128)(2,1)S(1)}, bf16[512,768]{1,0:T(8,128)(2,1)S(1)}, u32[]{:S(2)}, u32[]{:S(2)}) collective-permute-start(bf16[512,768]{1,0:T(8,128)(2,1)S(1)} %get-tuple-element.10), channel_id=1, source_target_pairs={{0,32},{32,0},{64,96},{96,64},{128,160},{160,128},{192,224},{224,1... | collective-permute-start | bytes 2359304 | tf_op jit(solution)/shard_map/ppermute | solution.py:29
  60.1 1.9 %collective-permute-done.4.got = bf16[512,768]{1,0:T(8,128)(2,1)S(1)} collective-permute-done((bf16[512,768]{1,0:T(8,128)(2,1)S(1)}, bf16[512,768]{1,0:T(8,128)(2,1)S(1)}, u32[]{:S(2)}, u32[]{:S(2)}) %collective-permute-start.4) | collective-permute-done | bytes 786464 | tf_op jit(solution)/shard_map/ppermute | solution.py:29
  61.9 1.6 shard_map.60
  63.5 4.3 %all-to-all-start = ((bf16[4,128,768]{2,1,0:T(8,128)(2,1)}), bf16[4,128,768]{2,1,0:T(8,128)(2,1)}, u32[]{:S(2)}, u32[]{:S(2)}) async-start(bf16[4,128,768]{2,1,0:T(8,128)(2,1)} %bitcast.2), calls=%async_computation | async-start | bytes 1572864 | tf_op jit(solution)/shard_map/all_to_all | solution.py:33
  67.9 1.9 %collective-permute-start.5 = (bf16[64,768]{1,0:T(8,128)(2,1)S(1)}, bf16[64,768]{1,0:T(8,128)(2,1)S(1)}, u32[]{:S(2)}, u32[]{:S(2)}) collective-permute-start(bf16[64,768]{1,0:T(8,128)(2,1)S(1)} %pad_maximum_fusion.1), channel_id=1, source_target_pairs={{0,1},{1,0},{2,3},{3,2},{4,5},{5,4},{6,7},{7,6},{8,9},{9,8},{10,11... | collective-permute-start | bytes 294920 | tf_op jit(solution)/shard_map/ppermute | solution.py:29
  69.9 9.8 %all-to-all-done = bf16[4,128,768]{2,1,0:T(8,128)(2,1)} async-done(((bf16[4,128,768]{2,1,0:T(8,128)(2,1)}), bf16[4,128,768]{2,1,0:T(8,128)(2,1)}, u32[]{:S(2)}, u32[]{:S(2)}) %all-to-all-start) | async-done | bytes 786464 | tf_op jit(solution)/shard_map/all_to_all | solution.py:33
  79.6 1.3 bitcast_convert_fusion.value
  81.6 12.6 %collective-permute-start.6 = (bf16[128,768]{1,0:T(8,128)(2,1)S(1)}, bf16[128,768]{1,0:T(8,128)(2,1)S(1)}, u32[]{:S(2)}, u32[]{:S(2)}) collective-permute-start(bf16[128,768]{1,0:T(8,128)(2,1)S(1)} %get-tuple-element.11._), channel_id=1, source_target_pairs={{0,64},{32,96},{64,0},{96,32},{128,192},{160,224},{192,128},{224,1... | collective-permute-start | bytes 589832 | tf_op jit(solution)/shard_map/ppermute | solution.py:29
  94.8 1.9 %collective-permute-start.8 = (bf16[512,768]{1,0:T(8,128)(2,1)S(1)}, bf16[512,768]{1,0:T(8,128)(2,1)S(1)}, u32[]{:S(2)}, u32[]{:S(2)}) collective-permute-start(bf16[512,768]{1,0:T(8,128)(2,1)S(1)} %shard_map.62), channel_id=1, source_target_pairs={{0,1},{1,0},{2,3},{3,2},{4,5},{5,4},{6,7},{7,6},{8,9},{9,8},{10,11... | collective-permute-start | bytes 2359304 | tf_op jit(solution)/shard_map/ppermute | solution.py:29
  97.9 2.3 %fusion.15 = (bf16[128,768]{1,0:T(8,128)(2,1)S(1)}, f32[128,768]{1,0:T(8,128)}) fusion(bf16[128,768]{1,0:T(8,128)(2,1)S(1)} %get-tuple-element.12, bf16[128,768]{1,0:T(8,128)(2,1)S(1)} %collective-permute-done.6, bf16[4,128,768]{2,1,0:T(8,128)(2,1)} %all-to-all-done), kind=kLoop, calls=%fused_computation.18 | loop fusion | flops 1966080 | bytes 1769472 | tf_op jit(solution)/shard_map/convert_element_type | solution.py:209
  100.1 12.2 %all_gather.7.grad = bf16[512,768]{1,0:T(8,128)(2,1)S(1)} all-gather(bf16[128,768]{1,0:T(8,128)(2,1)S(1)} %get-tuple-element.15), channel_id=1, replica_groups={{0,128,256,384},{32,160,288,416},{64,192,320,448},{96,224,352,480},{1,1..., dimensions={0}, use_global_device_ids=true | all-gather | bytes 983040 | tf_op jit(solution)/shard_map/all_gather | solution.py:213
  112.3 5.7 %collective-permute-start.9 = (bf16[512,768]{1,0:T(8,128)(2,1)S(1)}, bf16[512,768]{1,0:T(8,128)(2,1)S(1)}, u32[]{:S(2)}, u32[]{:S(2)}) collective-permute-start(bf16[512,768]{1,0:T(8,128)(2,1)S(1)} %all_gather.7.grad), channel_id=1, source_target_pairs={{0,32},{32,0},{64,96},{96,64},{128,160},{160,128},{192,224},{224,1... | collective-permute-start | bytes 2359304 | tf_op jit(solution)/shard_map/ppermute | solution.py:29
  118.0 1.3 shard_map.63.first
  119.9 1.4 shard_map.64
  121.4 2.6 %collective-permute-start.10 = (bf16[256,768]{1,0:T(8,128)(2,1)S(1)}, bf16[256,768]{1,0:T(8,128)(2,1)S(1)}, u32[]{:S(2)}, u32[]{:S(2)}) collective-permute-start(bf16[256,768]{1,0:T(8,128)(2,1)S(1)} %get-tuple-element.14), channel_id=1, source_target_pairs={{0,2},{1,3},{2,0},{3,1},{4,6},{5,7},{6,4},{7,5},{8,10},{9,11},{10,... | collective-permute-start | bytes 1179656 | tf_op jit(solution)/shard_map/ppermute | solution.py:29
  124.0 11.1 %collective-permute-done.10 = bf16[256,768]{1,0:T(8,128)(2,1)S(1)} collective-permute-done((bf16[256,768]{1,0:T(8,128)(2,1)S(1)}, bf16[256,768]{1,0:T(8,128)(2,1)S(1)}, u32[]{:S(2)}, u32[]{:S(2)}) %collective-permute-start.10) | collective-permute-done | bytes 393248 | tf_op jit(solution)/shard_map/ppermute | solution.py:29
  135.9 13.2 %all-to-all-start.1 = ((bf16[4,64,768]{2,1,0:T(8,128)(2,1)}), bf16[4,64,768]{2,1,0:T(8,128)(2,1)S(1)}, u32[]{:S(2)}, u32[]{:S(2)}) async-start(bf16[4,64,768]{2,1,0:T(8,128)(2,1)} %bitcast.4), calls=%async_computation.1 | async-start | bytes 786432 | tf_op jit(solution)/shard_map/all_to_all | solution.py:33
  149.9 2.0 %collective-permute-start.12 = (bf16[256,768]{1,0:T(8,128)(2,1)S(1)}, bf16[256,768]{1,0:T(8,128)(2,1)}, u32[]{:S(2)}, u32[]{:S(2)}) collective-permute-start(bf16[256,768]{1,0:T(8,128)(2,1)S(1)} %bitcast.25), channel_id=1, source_target_pairs={{0,1},{1,0},{2,3},{3,2},{4,5},{5,4},{6,7},{7,6},{8,9},{9,8},{10,11... | collective-permute-start | bytes 1179656 | tf_op jit(solution)/shard_map/ppermute | solution.py:29
  153.0 3.4 %collective-permute-start.7 = (bf16[32,768]{1,0:T(8,128)(2,1)S(1)}, bf16[32,768]{1,0:T(8,128)(2,1)S(1)}, u32[]{:S(2)}, u32[]{:S(2)}) collective-permute-start(bf16[32,768]{1,0:T(8,128)(2,1)S(1)} %slice.115), channel_id=1, source_target_pairs={{0,1},{1,0},{2,3},{3,2},{4,5},{5,4},{6,7},{7,6},{8,9},{9,8},{10,11... | collective-permute-start | bytes 147464 | tf_op jit(solution)/shard_map/ppermute | solution.py:29
  156.4 5.8 %collective-permute-done.7 = bf16[32,768]{1,0:T(8,128)(2,1)S(1)} collective-permute-done((bf16[32,768]{1,0:T(8,128)(2,1)S(1)}, bf16[32,768]{1,0:T(8,128)(2,1)S(1)}, u32[]{:S(2)}, u32[]{:S(2)}) %collective-permute-start.7) | collective-permute-done | bytes 49184 | tf_op jit(solution)/shard_map/ppermute | solution.py:29
  162.8 4.2 %collective-permute-start.13 = (bf16[256,768]{1,0:T(8,128)(2,1)}, bf16[256,768]{1,0:T(8,128)(2,1)}, u32[]{:S(2)}, u32[]{:S(2)}) collective-permute-start(bf16[256,768]{1,0:T(8,128)(2,1)} %collective-permute-done.12), channel_id=1, source_target_pairs={{0,32},{32,0},{64,96},{96,64},{128,160},{160,128},{192,224},{224,1... | collective-permute-start | bytes 1179656 | tf_op jit(solution)/shard_map/ppermute | solution.py:29
  167.2 8.1 %collective-permute-start.11 = (bf16[32,768]{1,0:T(8,128)(2,1)S(1)}, bf16[32,768]{1,0:T(8,128)(2,1)S(1)}, u32[]{:S(2)}, u32[]{:S(2)}) collective-permute-start(bf16[32,768]{1,0:T(8,128)(2,1)S(1)} %fusion.18), channel_id=1, source_target_pairs={{0,16},{1,17},{2,18},{3,19},{4,20},{5,21},{6,22},{7,23},{8,24},{9,... | collective-permute-start | bytes 147464 | tf_op jit(solution)/shard_map/ppermute | solution.py:29
  175.3 3.7 %multiply_convert_fusion = bf16[768,768]{1,0:T(8,128)(2,1)} fusion(bf16[512,768]{1,0:T(8,128)(2,1)S(1)} %copy-done.5, bf16[512,768]{1,0:T(8,128)(2,1)S(1)} %copy-done.7, bf16[256,768]{1,0:T(8,128)(2,1)} %collective-permute-done.13, bf16[256,768]{1,0:T(8,128)(2,1)} %collective-permute-done.12, bf16[256,768]{1,0:T(8,128)(2,1)S(1)} %bitcast.23, ...), kind=kOutput, calls=%fused_computation | convolution fusion | flops 1218576384 | bytes 4325376 | tf_op jit(solution)/shard_map/dot_general | solution.py:243
  (45 shorter events, 8.7 us)
Async XLA Ops:
  0.6 46.4 %collective-permute-start.1 = (bf16[768,768]{1,0:T(8,128)(2,1)}, bf16[768,768]{1,0:T(8,128)(2,1)S(1)}, u32[]{:S(2)}, u32[]{:S(2)}) collective-permute-start(bf16[768,768]{1,0:T(8,128)(2,1)} %w0.7), channel_id=1, source_target_pairs={{0,1},{1,0},{2,3},{3,2},{4,5},{5,4},{6,7},{7,6},{8,9},{9,8},{10,11... | collective-permute-start | bytes 3538952 | tf_op jit(solution)/shard_map/ppermute | solution.py:29
  4.6 10.5 %collective-permute-start = (bf16[32,768]{1,0:T(8,128)(2,1)}, bf16[32,768]{1,0:T(8,128)(2,1)S(1)}, u32[]{:S(2)}, u32[]{:S(2)}) collective-permute-start(bf16[32,768]{1,0:T(8,128)(2,1)} %param.3), channel_id=1, source_target_pairs={{0,16},{1,17},{2,18},{3,19},{4,20},{5,21},{6,22},{7,23},{8,24},{9,... | collective-permute-start | bytes 147464 | tf_op jit(solution)/shard_map/ppermute | solution.py:29
  31.7 18.8 %collective-permute-start.2 = (bf16[256,768]{1,0:T(8,128)(2,1)S(1)}, bf16[256,768]{1,0:T(8,128)(2,1)S(1)}, u32[]{:S(2)}, u32[]{:S(2)}) collective-permute-start(bf16[256,768]{1,0:T(8,128)(2,1)S(1)} %all_gather.6.piece.line), channel_id=1, source_target_pairs={{0,2},{1,3},{2,0},{3,1},{4,6},{5,7},{6,4},{7,5},{8,10},{9,11},{10,... | collective-permute-start | bytes 1179656 | tf_op jit(solution)/shard_map/ppermute | solution.py:29
  36.1 14.4 %collective-permute-start.3 = (bf16[64,768]{1,0:T(8,128)(2,1)}, bf16[64,768]{1,0:T(8,128)(2,1)S(1)}, u32[]{:S(2)}, u32[]{:S(2)}) collective-permute-start(bf16[64,768]{1,0:T(8,128)(2,1)} %param.5), channel_id=1, source_target_pairs={{0,64},{32,96},{64,0},{96,32},{128,192},{160,224},{192,128},{224,1... | collective-permute-start | bytes 294920 | tf_op jit(solution)/shard_map/ppermute | solution.py:29
  47.0 1.3 copy-start
  48.3 2.2 %copy-start.1 = (bf16[768,768]{1,0:T(8,128)(2,1)S(1)}, bf16[768,768]{1,0:T(8,128)(2,1)}, u32[]{:S(2)}) copy-start(bf16[768,768]{1,0:T(8,128)(2,1)} %w0.7) | copy-start | bytes 3538948
  51.9 10.1 %collective-permute-start.4 = (bf16[512,768]{1,0:T(8,128)(2,1)S(1)}, bf16[512,768]{1,0:T(8,128)(2,1)S(1)}, u32[]{:S(2)}, u32[]{:S(2)}) collective-permute-start(bf16[512,768]{1,0:T(8,128)(2,1)S(1)} %get-tuple-element.10), channel_id=1, source_target_pairs={{0,32},{32,0},{64,96},{96,64},{128,160},{160,128},{192,224},{224,1... | collective-permute-start | bytes 2359304 | tf_op jit(solution)/shard_map/ppermute | solution.py:29
  63.5 4.4 %copy-start.8 = (bf16[64,768]{1,0:T(8,128)(2,1)S(1)}, bf16[64,768]{1,0:T(8,128)(2,1)}, u32[]{:S(2)}) copy-start(bf16[64,768]{1,0:T(8,128)(2,1)} %param.5) | copy-start | bytes 294916
  63.5 16.1 %all-to-all-start = ((bf16[4,128,768]{2,1,0:T(8,128)(2,1)}), bf16[4,128,768]{2,1,0:T(8,128)(2,1)}, u32[]{:S(2)}, u32[]{:S(2)}) async-start(bf16[4,128,768]{2,1,0:T(8,128)(2,1)} %bitcast.2), calls=%async_computation | async-start | bytes 1572864 | tf_op jit(solution)/shard_map/all_to_all | solution.py:33
  67.9 13.0 %collective-permute-start.5 = (bf16[64,768]{1,0:T(8,128)(2,1)S(1)}, bf16[64,768]{1,0:T(8,128)(2,1)S(1)}, u32[]{:S(2)}, u32[]{:S(2)}) collective-permute-start(bf16[64,768]{1,0:T(8,128)(2,1)S(1)} %pad_maximum_fusion.1), channel_id=1, source_target_pairs={{0,1},{1,0},{2,3},{3,2},{4,5},{5,4},{6,7},{7,6},{8,9},{9,8},{10,11... | collective-permute-start | bytes 294920 | tf_op jit(solution)/shard_map/ppermute | solution.py:29
  81.6 16.3 %collective-permute-start.6 = (bf16[128,768]{1,0:T(8,128)(2,1)S(1)}, bf16[128,768]{1,0:T(8,128)(2,1)S(1)}, u32[]{:S(2)}, u32[]{:S(2)}) collective-permute-start(bf16[128,768]{1,0:T(8,128)(2,1)S(1)} %get-tuple-element.11._), channel_id=1, source_target_pairs={{0,64},{32,96},{64,0},{96,32},{128,192},{160,224},{192,128},{224,1... | collective-permute-start | bytes 589832 | tf_op jit(solution)/shard_map/ppermute | solution.py:29
  94.8 24.6 %copy-start.6 = (bf16[512,768]{1,0:T(8,128)(2,1)}, bf16[512,768]{1,0:T(8,128)(2,1)S(1)}, u32[]{:S(2)}) copy-start(bf16[512,768]{1,0:T(8,128)(2,1)S(1)} %shard_map.62) | copy-start | bytes 2359300
  94.8 23.2 %collective-permute-start.8 = (bf16[512,768]{1,0:T(8,128)(2,1)S(1)}, bf16[512,768]{1,0:T(8,128)(2,1)S(1)}, u32[]{:S(2)}, u32[]{:S(2)}) collective-permute-start(bf16[512,768]{1,0:T(8,128)(2,1)S(1)} %shard_map.62), channel_id=1, source_target_pairs={{0,1},{1,0},{2,3},{3,2},{4,5},{5,4},{6,7},{7,6},{8,9},{9,8},{10,11... | collective-permute-start | bytes 2359304 | tf_op jit(solution)/shard_map/ppermute | solution.py:29
  112.3 7.6 %collective-permute-start.9 = (bf16[512,768]{1,0:T(8,128)(2,1)S(1)}, bf16[512,768]{1,0:T(8,128)(2,1)S(1)}, u32[]{:S(2)}, u32[]{:S(2)}) collective-permute-start(bf16[512,768]{1,0:T(8,128)(2,1)S(1)} %all_gather.7.grad), channel_id=1, source_target_pairs={{0,32},{32,0},{64,96},{96,64},{128,160},{160,128},{192,224},{224,1... | collective-permute-start | bytes 2359304 | tf_op jit(solution)/shard_map/ppermute | solution.py:29
  118.0 1.4 copy-start.4
  119.9 1.4 copy-start.2
  121.4 13.7 %collective-permute-start.10 = (bf16[256,768]{1,0:T(8,128)(2,1)S(1)}, bf16[256,768]{1,0:T(8,128)(2,1)S(1)}, u32[]{:S(2)}, u32[]{:S(2)}) collective-permute-start(bf16[256,768]{1,0:T(8,128)(2,1)S(1)} %get-tuple-element.14), channel_id=1, source_target_pairs={{0,2},{1,3},{2,0},{3,1},{4,6},{5,7},{6,4},{7,5},{8,10},{9,11},{10,... | collective-permute-start | bytes 1179656 | tf_op jit(solution)/shard_map/ppermute | solution.py:29
  135.9 31.2 %copy-start.3 = (bf16[512,768]{1,0:T(8,128)(2,1)S(1)}, bf16[512,768]{1,0:T(8,128)(2,1)}, u32[]{:S(2)}) copy-start(bf16[512,768]{1,0:T(8,128)(2,1)} %copy-done.2) | copy-start | bytes 2359300
  135.9 31.2 %all-to-all-start.1 = ((bf16[4,64,768]{2,1,0:T(8,128)(2,1)}), bf16[4,64,768]{2,1,0:T(8,128)(2,1)S(1)}, u32[]{:S(2)}, u32[]{:S(2)}) async-start(bf16[4,64,768]{2,1,0:T(8,128)(2,1)} %bitcast.4), calls=%async_computation.1 | async-start | bytes 786432 | tf_op jit(solution)/shard_map/all_to_all | solution.py:33
  149.9 25.4 %copy-start.5 = (bf16[512,768]{1,0:T(8,128)(2,1)S(1)}, bf16[512,768]{1,0:T(8,128)(2,1)}, u32[]{:S(2)}) copy-start(bf16[512,768]{1,0:T(8,128)(2,1)} %copy-done.4) | copy-start | bytes 2359300
  149.9 25.4 %copy-start.7 = (bf16[512,768]{1,0:T(8,128)(2,1)S(1)}, bf16[512,768]{1,0:T(8,128)(2,1)}, u32[]{:S(2)}) copy-start(bf16[512,768]{1,0:T(8,128)(2,1)} %copy-done.6) | copy-start | bytes 2359300
  149.9 12.9 %collective-permute-start.12 = (bf16[256,768]{1,0:T(8,128)(2,1)S(1)}, bf16[256,768]{1,0:T(8,128)(2,1)}, u32[]{:S(2)}, u32[]{:S(2)}) collective-permute-start(bf16[256,768]{1,0:T(8,128)(2,1)S(1)} %bitcast.25), channel_id=1, source_target_pairs={{0,1},{1,0},{2,3},{3,2},{4,5},{5,4},{6,7},{7,6},{8,9},{9,8},{10,11... | collective-permute-start | bytes 1179656 | tf_op jit(solution)/shard_map/ppermute | solution.py:29
  153.0 9.1 %collective-permute-start.7 = (bf16[32,768]{1,0:T(8,128)(2,1)S(1)}, bf16[32,768]{1,0:T(8,128)(2,1)S(1)}, u32[]{:S(2)}, u32[]{:S(2)}) collective-permute-start(bf16[32,768]{1,0:T(8,128)(2,1)S(1)} %slice.115), channel_id=1, source_target_pairs={{0,1},{1,0},{2,3},{3,2},{4,5},{5,4},{6,7},{7,6},{8,9},{9,8},{10,11... | collective-permute-start | bytes 147464 | tf_op jit(solution)/shard_map/ppermute | solution.py:29
  162.8 12.4 %collective-permute-start.13 = (bf16[256,768]{1,0:T(8,128)(2,1)}, bf16[256,768]{1,0:T(8,128)(2,1)}, u32[]{:S(2)}, u32[]{:S(2)}) collective-permute-start(bf16[256,768]{1,0:T(8,128)(2,1)} %collective-permute-done.12), channel_id=1, source_target_pairs={{0,32},{32,0},{64,96},{96,64},{128,160},{160,128},{192,224},{224,1... | collective-permute-start | bytes 1179656 | tf_op jit(solution)/shard_map/ppermute | solution.py:29
  167.2 11.8 %collective-permute-start.11 = (bf16[32,768]{1,0:T(8,128)(2,1)S(1)}, bf16[32,768]{1,0:T(8,128)(2,1)S(1)}, u32[]{:S(2)}, u32[]{:S(2)}) collective-permute-start(bf16[32,768]{1,0:T(8,128)(2,1)S(1)} %fusion.18), channel_id=1, source_target_pairs={{0,16},{1,17},{2,18},{3,19},{4,20},{5,21},{6,22},{7,23},{8,24},{9,... | collective-permute-start | bytes 147464 | tf_op jit(solution)/shard_map/ppermute | solution.py:29

commit v7 on v6

--- a/solution.py
+++ b/solution.py
@@ -202,7 +202,7 @@
     both, sent = call(
         stack_kernel, [shape(size, width, BF16)] * 2, [], 0, me, *cotangents, mine.astype(BF16)
     )
-    pre = mine + swap(sent, "row", 2).astype(F32)
+    pre = sent.astype(F32) + swap(sent, "row", 2).astype(F32)
 
     size = tokens // 16
     value = gelu_value(jnp.where(upper, pre[size:], pre[:size])).astype(BF16)

time: 180 us -> 179 us (level)
  transfers between devices with their start and end apart: 16 -> 16, of which waited for: 8 -> 8; matrix products, arithmetic and copies ran while one was open for 6% -> 5% of each run, Pallas kernels for 2% -> 2%
where the time goes in v7:
time: 179 us; the launch traced here: 178 us
  starting transfers between devices  96.1 us (54%)
  waiting for transfers between devices  32.7 us (18%)
  blocking collectives  28 us (16%)
  Pallas kernels  8.24 us (5%)
  other arithmetic  6.45 us (4%)
  matrix products  3.69 us (2%)
  local copies, waits for them, and re-layouts  2.15 us (1%)
    ppermute x14, starting transfers between devices, swap(): return lax.ppermute(value, axis, [(i, i ^ mask) for i in range(size)])  78.6 us
    ppermute x14, waiting for transfers between devices, swap(): return lax.ppermute(value, axis, [(i, i ^ mask) for i in range(size)])  23 us
    all_to_all x2, starting transfers between devices, spread(): lax.all_to_all(value, axis, split_axis=0, concat_axis=0, axis_index_group...  17.5 us
    all_gather x1, blocking collectives, shards(): lax.all_gather(pair, 'col', axis=0, tiled=True, axis_index_groups=Z_GROUPS)  15.8 us
    all_gather x1, blocking collectives, shards(): lax.all_gather(grad, 'row', axis=0, tiled=True, axis_index_groups=Y_GROUPS)  12.2 us
    all_to_all x2, waiting for transfers between devices, spread(): lax.all_to_all(value, axis, split_axis=0, concat_axis=0, axis_index_group...  9.79 us
    pallas_call x7, Pallas kernels, call(): pl.pallas_call(kernel, out_shape=outs, in_specs=[pl.BlockSpec(memory_spac...  8.24 us
    dot_general x1, matrix products, shards(): lax.dot_general(jnp.concatenate([near, far]), jnp.concatenate(own + other...  3.69 us
  transfers between devices with their start and end apart: 16, of which 8 were waited for; matrix products, arithmetic and copies ran while one was open for 5% of the time, Pallas kernels for 2%

profile of v7, /device:TPU:1, one launch (start us, length us, event | category | flops | bytes accessed | tf_op | source)
XLA Modules:
  0.0 178.3 jit_solution(16656688933705077237)
XLA Ops:
  0.6 4.0 %collective-permute-start.3 = (bf16[768,768]{1,0:T(8,128)(2,1)}, bf16[768,768]{1,0:T(8,128)(2,1)S(1)}, u32[]{:S(2)}, u32[]{:S(2)}) collective-permute-start(bf16[768,768]{1,0:T(8,128)(2,1)} %w0.7), channel_id=1, source_target_pairs={{0,1},{1,0},{2,3},{3,2},{4,5},{5,4},{6,7},{7,6},{8,9},{9,8},{10,11... | collective-permute-start | bytes 3538952 | tf_op jit(solution)/shard_map/ppermute | solution.py:29
  4.6 8.8 %collective-permute-start.2 = (bf16[32,768]{1,0:T(8,128)(2,1)}, bf16[32,768]{1,0:T(8,128)(2,1)S(1)}, u32[]{:S(2)}, u32[]{:S(2)}) collective-permute-start(bf16[32,768]{1,0:T(8,128)(2,1)} %param.3), channel_id=1, source_target_pairs={{0,16},{1,17},{2,18},{3,19},{4,20},{5,21},{6,22},{7,23},{8,24},{9,... | collective-permute-start | bytes 147464 | tf_op jit(solution)/shard_map/ppermute | solution.py:29
  13.4 1.7 collective-permute-done.2
  15.9 15.8 %all_gather.6.piece.line = bf16[256,768]{1,0:T(8,128)(2,1)S(1)} all-gather(bf16[64,768]{1,0:T(8,128)(2,1)S(1)} %pad_maximum_fusion.1), channel_id=1, replica_groups={{0,4,8,12},{1,5,9,13},{2,6,10,14},{3,7,11,15},{16,20,24,28},{17,21,25,2..., dimensions={0}, use_global_device_ids=true | all-gather | bytes 491520 | tf_op jit(solution)/shard_map/all_gather | solution.py:173
  31.7 4.4 %collective-permute-start.4 = (bf16[256,768]{1,0:T(8,128)(2,1)S(1)}, bf16[256,768]{1,0:T(8,128)(2,1)S(1)}, u32[]{:S(2)}, u32[]{:S(2)}) collective-permute-start(bf16[256,768]{1,0:T(8,128)(2,1)S(1)} %all_gather.6.piece.line), channel_id=1, source_target_pairs={{0,2},{1,3},{2,0},{3,1},{4,6},{5,7},{6,4},{7,5},{8,10},{9,11},{10,... | collective-permute-start | bytes 1179656 | tf_op jit(solution)/shard_map/ppermute | solution.py:29
  36.1 10.8 %collective-permute-start = (bf16[64,768]{1,0:T(8,128)(2,1)}, bf16[64,768]{1,0:T(8,128)(2,1)S(1)}, u32[]{:S(2)}, u32[]{:S(2)}) collective-permute-start(bf16[64,768]{1,0:T(8,128)(2,1)} %param.5), channel_id=1, source_target_pairs={{0,64},{32,96},{64,0},{96,32},{128,192},{160,224},{192,128},{224,1... | collective-permute-start | bytes 294920 | tf_op jit(solution)/shard_map/ppermute | solution.py:29
  47.0 1.3 copy-done
  48.3 1.3 shard_map.58.early
  50.5 1.4 shard_map.59
  51.9 8.2 %collective-permute-start.5 = (bf16[512,768]{1,0:T(8,128)(2,1)S(1)}, bf16[512,768]{1,0:T(8,128)(2,1)S(1)}, u32[]{:S(2)}, u32[]{:S(2)}) collective-permute-start(bf16[512,768]{1,0:T(8,128)(2,1)S(1)} %get-tuple-element.10), channel_id=1, source_target_pairs={{0,32},{32,0},{64,96},{96,64},{128,160},{160,128},{192,224},{224,1... | collective-permute-start | bytes 2359304 | tf_op jit(solution)/shard_map/ppermute | solution.py:29
  60.1 1.9 %collective-permute-done.5.got = bf16[512,768]{1,0:T(8,128)(2,1)S(1)} collective-permute-done((bf16[512,768]{1,0:T(8,128)(2,1)S(1)}, bf16[512,768]{1,0:T(8,128)(2,1)S(1)}, u32[]{:S(2)}, u32[]{:S(2)}) %collective-permute-start.5) | collective-permute-done | bytes 786464 | tf_op jit(solution)/shard_map/ppermute | solution.py:29
  61.9 1.6 shard_map.60
  63.5 4.3 %all-to-all-start = ((bf16[4,128,768]{2,1,0:T(8,128)(2,1)}), bf16[4,128,768]{2,1,0:T(8,128)(2,1)}, u32[]{:S(2)}, u32[]{:S(2)}) async-start(bf16[4,128,768]{2,1,0:T(8,128)(2,1)} %bitcast.2), calls=%async_computation | async-start | bytes 1572864 | tf_op jit(solution)/shard_map/all_to_all | solution.py:33
  67.9 1.9 %collective-permute-start.1 = (bf16[64,768]{1,0:T(8,128)(2,1)S(1)}, bf16[64,768]{1,0:T(8,128)(2,1)S(1)}, u32[]{:S(2)}, u32[]{:S(2)}) collective-permute-start(bf16[64,768]{1,0:T(8,128)(2,1)S(1)} %pad_maximum_fusion), channel_id=1, source_target_pairs={{0,1},{1,0},{2,3},{3,2},{4,5},{5,4},{6,7},{7,6},{8,9},{9,8},{10,11... | collective-permute-start | bytes 294920 | tf_op jit(solution)/shard_map/ppermute | solution.py:29
  69.9 9.8 %all-to-all-done = bf16[4,128,768]{2,1,0:T(8,128)(2,1)} async-done(((bf16[4,128,768]{2,1,0:T(8,128)(2,1)}), bf16[4,128,768]{2,1,0:T(8,128)(2,1)}, u32[]{:S(2)}, u32[]{:S(2)}) %all-to-all-start) | async-done | bytes 786464 | tf_op jit(solution)/shard_map/all_to_all | solution.py:33
  79.6 1.3 fusion.16.value
  81.6 12.6 %collective-permute-start.6 = (bf16[128,768]{1,0:T(8,128)(2,1)S(1)}, bf16[128,768]{1,0:T(8,128)(2,1)S(1)}, u32[]{:S(2)}, u32[]{:S(2)}) collective-permute-start(bf16[128,768]{1,0:T(8,128)(2,1)S(1)} %get-tuple-element.11._), channel_id=1, source_target_pairs={{0,64},{32,96},{64,0},{96,32},{128,192},{160,224},{192,128},{224,1... | collective-permute-start | bytes 589832 | tf_op jit(solution)/shard_map/ppermute | solution.py:29
  94.8 1.9 %collective-permute-start.8 = (bf16[512,768]{1,0:T(8,128)(2,1)S(1)}, bf16[512,768]{1,0:T(8,128)(2,1)S(1)}, u32[]{:S(2)}, u32[]{:S(2)}) collective-permute-start(bf16[512,768]{1,0:T(8,128)(2,1)S(1)} %shard_map.62), channel_id=1, source_target_pairs={{0,1},{1,0},{2,3},{3,2},{4,5},{5,4},{6,7},{7,6},{8,9},{9,8},{10,11... | collective-permute-start | bytes 2359304 | tf_op jit(solution)/shard_map/ppermute | solution.py:29
  96.7 1.1 collective-permute-done.6
  98.8 12.2 %all_gather.7.grad = bf16[512,768]{1,0:T(8,128)(2,1)S(1)} all-gather(bf16[128,768]{1,0:T(8,128)(2,1)S(1)} %get-tuple-element.17), channel_id=1, replica_groups={{0,128,256,384},{32,160,288,416},{64,192,320,448},{96,224,352,480},{1,1..., dimensions={0}, use_global_device_ids=true | all-gather | bytes 983040 | tf_op jit(solution)/shard_map/all_gather | solution.py:213
  111.0 5.7 %collective-permute-start.9 = (bf16[512,768]{1,0:T(8,128)(2,1)S(1)}, bf16[512,768]{1,0:T(8,128)(2,1)S(1)}, u32[]{:S(2)}, u32[]{:S(2)}) collective-permute-start(bf16[512,768]{1,0:T(8,128)(2,1)S(1)} %all_gather.7.grad), channel_id=1, source_target_pairs={{0,32},{32,0},{64,96},{96,64},{128,160},{160,128},{192,224},{224,1... | collective-permute-start | bytes 2359304 | tf_op jit(solution)/shard_map/ppermute | solution.py:29
  116.7 1.3 shard_map.63.first
  118.6 1.4 shard_map.64
  120.1 2.6 %collective-permute-start.10 = (bf16[256,768]{1,0:T(8,128)(2,1)S(1)}, bf16[256,768]{1,0:T(8,128)(2,1)S(1)}, u32[]{:S(2)}, u32[]{:S(2)}) collective-permute-start(bf16[256,768]{1,0:T(8,128)(2,1)S(1)} %get-tuple-element.14), channel_id=1, source_target_pairs={{0,2},{1,3},{2,0},{3,1},{4,6},{5,7},{6,4},{7,5},{8,10},{9,11},{10,... | collective-permute-start | bytes 1179656 | tf_op jit(solution)/shard_map/ppermute | solution.py:29
  122.7 11.1 %collective-permute-done.10 = bf16[256,768]{1,0:T(8,128)(2,1)S(1)} collective-permute-done((bf16[256,768]{1,0:T(8,128)(2,1)S(1)}, bf16[256,768]{1,0:T(8,128)(2,1)S(1)}, u32[]{:S(2)}, u32[]{:S(2)}) %collective-permute-start.10) | collective-permute-done | bytes 393248 | tf_op jit(solution)/shard_map/ppermute | solution.py:29
  134.6 13.2 %all-to-all-start.1 = ((bf16[4,64,768]{2,1,0:T(8,128)(2,1)}), bf16[4,64,768]{2,1,0:T(8,128)(2,1)S(1)}, u32[]{:S(2)}, u32[]{:S(2)}) async-start(bf16[4,64,768]{2,1,0:T(8,128)(2,1)} %bitcast.4), calls=%async_computation.1 | async-start | bytes 786432 | tf_op jit(solution)/shard_map/all_to_all | solution.py:33
  148.6 2.0 %collective-permute-start.12 = (bf16[256,768]{1,0:T(8,128)(2,1)S(1)}, bf16[256,768]{1,0:T(8,128)(2,1)}, u32[]{:S(2)}, u32[]{:S(2)}) collective-permute-start(bf16[256,768]{1,0:T(8,128)(2,1)S(1)} %bitcast.23), channel_id=1, source_target_pairs={{0,1},{1,0},{2,3},{3,2},{4,5},{5,4},{6,7},{7,6},{8,9},{9,8},{10,11... | collective-permute-start | bytes 1179656 | tf_op jit(solution)/shard_map/ppermute | solution.py:29
  151.7 3.4 %collective-permute-start.7 = (bf16[32,768]{1,0:T(8,128)(2,1)S(1)}, bf16[32,768]{1,0:T(8,128)(2,1)S(1)}, u32[]{:S(2)}, u32[]{:S(2)}) collective-permute-start(bf16[32,768]{1,0:T(8,128)(2,1)S(1)} %slice.115), channel_id=1, source_target_pairs={{0,1},{1,0},{2,3},{3,2},{4,5},{5,4},{6,7},{7,6},{8,9},{9,8},{10,11... | collective-permute-start | bytes 147464 | tf_op jit(solution)/shard_map/ppermute | solution.py:29
  155.1 5.8 %collective-permute-done.7 = bf16[32,768]{1,0:T(8,128)(2,1)S(1)} collective-permute-done((bf16[32,768]{1,0:T(8,128)(2,1)S(1)}, bf16[32,768]{1,0:T(8,128)(2,1)S(1)}, u32[]{:S(2)}, u32[]{:S(2)}) %collective-permute-start.7) | collective-permute-done | bytes 49184 | tf_op jit(solution)/shard_map/ppermute | solution.py:29
  161.6 4.2 %collective-permute-start.13 = (bf16[256,768]{1,0:T(8,128)(2,1)}, bf16[256,768]{1,0:T(8,128)(2,1)}, u32[]{:S(2)}, u32[]{:S(2)}) collective-permute-start(bf16[256,768]{1,0:T(8,128)(2,1)} %collective-permute-done.12), channel_id=1, source_target_pairs={{0,32},{32,0},{64,96},{96,64},{128,160},{160,128},{192,224},{224,1... | collective-permute-start | bytes 1179656 | tf_op jit(solution)/shard_map/ppermute | solution.py:29
  165.9 8.0 %collective-permute-start.11 = (bf16[32,768]{1,0:T(8,128)(2,1)S(1)}, bf16[32,768]{1,0:T(8,128)(2,1)S(1)}, u32[]{:S(2)}, u32[]{:S(2)}) collective-permute-start(bf16[32,768]{1,0:T(8,128)(2,1)S(1)} %fusion.19), channel_id=1, source_target_pairs={{0,16},{1,17},{2,18},{3,19},{4,20},{5,21},{6,22},{7,23},{8,24},{9,... | collective-permute-start | bytes 147464 | tf_op jit(solution)/shard_map/ppermute | solution.py:29
  174.0 3.7 %multiply_convert_fusion = bf16[768,768]{1,0:T(8,128)(2,1)} fusion(bf16[512,768]{1,0:T(8,128)(2,1)S(1)} %copy-done.5, bf16[512,768]{1,0:T(8,128)(2,1)S(1)} %copy-done.7, bf16[256,768]{1,0:T(8,128)(2,1)} %collective-permute-done.13, bf16[256,768]{1,0:T(8,128)(2,1)} %collective-permute-done.12, bf16[256,768]{1,0:T(8,128)(2,1)S(1)} %bitcast.21, ...), kind=kOutput, calls=%fused_computation | convolution fusion | flops 1218576384 | bytes 4325376 | tf_op jit(solution)/shard_map/dot_general | solution.py:243
  (45 shorter events, 8.6 us)
Async XLA Ops:
  0.6 46.4 %collective-permute-start.3 = (bf16[768,768]{1,0:T(8,128)(2,1)}, bf16[768,768]{1,0:T(8,128)(2,1)S(1)}, u32[]{:S(2)}, u32[]{:S(2)}) collective-permute-start(bf16[768,768]{1,0:T(8,128)(2,1)} %w0.7), channel_id=1, source_target_pairs={{0,1},{1,0},{2,3},{3,2},{4,5},{5,4},{6,7},{7,6},{8,9},{9,8},{10,11... | collective-permute-start | bytes 3538952 | tf_op jit(solution)/shard_map/ppermute | solution.py:29
  4.6 10.5 %collective-permute-start.2 = (bf16[32,768]{1,0:T(8,128)(2,1)}, bf16[32,768]{1,0:T(8,128)(2,1)S(1)}, u32[]{:S(2)}, u32[]{:S(2)}) collective-permute-start(bf16[32,768]{1,0:T(8,128)(2,1)} %param.3), channel_id=1, source_target_pairs={{0,16},{1,17},{2,18},{3,19},{4,20},{5,21},{6,22},{7,23},{8,24},{9,... | collective-permute-start | bytes 147464 | tf_op jit(solution)/shard_map/ppermute | solution.py:29
  31.7 18.8 %collective-permute-start.4 = (bf16[256,768]{1,0:T(8,128)(2,1)S(1)}, bf16[256,768]{1,0:T(8,128)(2,1)S(1)}, u32[]{:S(2)}, u32[]{:S(2)}) collective-permute-start(bf16[256,768]{1,0:T(8,128)(2,1)S(1)} %all_gather.6.piece.line), channel_id=1, source_target_pairs={{0,2},{1,3},{2,0},{3,1},{4,6},{5,7},{6,4},{7,5},{8,10},{9,11},{10,... | collective-permute-start | bytes 1179656 | tf_op jit(solution)/shard_map/ppermute | solution.py:29
  36.1 14.4 %collective-permute-start = (bf16[64,768]{1,0:T(8,128)(2,1)}, bf16[64,768]{1,0:T(8,128)(2,1)S(1)}, u32[]{:S(2)}, u32[]{:S(2)}) collective-permute-start(bf16[64,768]{1,0:T(8,128)(2,1)} %param.5), channel_id=1, source_target_pairs={{0,64},{32,96},{64,0},{96,32},{128,192},{160,224},{192,128},{224,1... | collective-permute-start | bytes 294920 | tf_op jit(solution)/shard_map/ppermute | solution.py:29
  47.0 1.3 copy-start
  48.3 2.2 %copy-start.1 = (bf16[768,768]{1,0:T(8,128)(2,1)S(1)}, bf16[768,768]{1,0:T(8,128)(2,1)}, u32[]{:S(2)}) copy-start(bf16[768,768]{1,0:T(8,128)(2,1)} %w0.7) | copy-start | bytes 3538948
  51.9 10.1 %collective-permute-start.5 = (bf16[512,768]{1,0:T(8,128)(2,1)S(1)}, bf16[512,768]{1,0:T(8,128)(2,1)S(1)}, u32[]{:S(2)}, u32[]{:S(2)}) collective-permute-start(bf16[512,768]{1,0:T(8,128)(2,1)S(1)} %get-tuple-element.10), channel_id=1, source_target_pairs={{0,32},{32,0},{64,96},{96,64},{128,160},{160,128},{192,224},{224,1... | collective-permute-start | bytes 2359304 | tf_op jit(solution)/shard_map/ppermute | solution.py:29
  63.5 4.3 %copy-start.8 = (bf16[64,768]{1,0:T(8,128)(2,1)S(1)}, bf16[64,768]{1,0:T(8,128)(2,1)}, u32[]{:S(2)}) copy-start(bf16[64,768]{1,0:T(8,128)(2,1)} %param.5) | copy-start | bytes 294916
  63.5 16.1 %all-to-all-start = ((bf16[4,128,768]{2,1,0:T(8,128)(2,1)}), bf16[4,128,768]{2,1,0:T(8,128)(2,1)}, u32[]{:S(2)}, u32[]{:S(2)}) async-start(bf16[4,128,768]{2,1,0:T(8,128)(2,1)} %bitcast.2), calls=%async_computation | async-start | bytes 1572864 | tf_op jit(solution)/shard_map/all_to_all | solution.py:33
  67.9 13.0 %collective-permute-start.1 = (bf16[64,768]{1,0:T(8,128)(2,1)S(1)}, bf16[64,768]{1,0:T(8,128)(2,1)S(1)}, u32[]{:S(2)}, u32[]{:S(2)}) collective-permute-start(bf16[64,768]{1,0:T(8,128)(2,1)S(1)} %pad_maximum_fusion), channel_id=1, source_target_pairs={{0,1},{1,0},{2,3},{3,2},{4,5},{5,4},{6,7},{7,6},{8,9},{9,8},{10,11... | collective-permute-start | bytes 294920 | tf_op jit(solution)/shard_map/ppermute | solution.py:29
  81.6 16.3 %collective-permute-start.6 = (bf16[128,768]{1,0:T(8,128)(2,1)S(1)}, bf16[128,768]{1,0:T(8,128)(2,1)S(1)}, u32[]{:S(2)}, u32[]{:S(2)}) collective-permute-start(bf16[128,768]{1,0:T(8,128)(2,1)S(1)} %get-tuple-element.11._), channel_id=1, source_target_pairs={{0,64},{32,96},{64,0},{96,32},{128,192},{160,224},{192,128},{224,1... | collective-permute-start | bytes 589832 | tf_op jit(solution)/shard_map/ppermute | solution.py:29
  94.8 23.3 %copy-start.6 = (bf16[512,768]{1,0:T(8,128)(2,1)}, bf16[512,768]{1,0:T(8,128)(2,1)S(1)}, u32[]{:S(2)}) copy-start(bf16[512,768]{1,0:T(8,128)(2,1)S(1)} %shard_map.62) | copy-start | bytes 2359300
  94.8 21.9 %collective-permute-start.8 = (bf16[512,768]{1,0:T(8,128)(2,1)S(1)}, bf16[512,768]{1,0:T(8,128)(2,1)S(1)}, u32[]{:S(2)}, u32[]{:S(2)}) collective-permute-start(bf16[512,768]{1,0:T(8,128)(2,1)S(1)} %shard_map.62), channel_id=1, source_target_pairs={{0,1},{1,0},{2,3},{3,2},{4,5},{5,4},{6,7},{7,6},{8,9},{9,8},{10,11... | collective-permute-start | bytes 2359304 | tf_op jit(solution)/shard_map/ppermute | solution.py:29
  111.0 7.6 %collective-permute-start.9 = (bf16[512,768]{1,0:T(8,128)(2,1)S(1)}, bf16[512,768]{1,0:T(8,128)(2,1)S(1)}, u32[]{:S(2)}, u32[]{:S(2)}) collective-permute-start(bf16[512,768]{1,0:T(8,128)(2,1)S(1)} %all_gather.7.grad), channel_id=1, source_target_pairs={{0,32},{32,0},{64,96},{96,64},{128,160},{160,128},{192,224},{224,1... | collective-permute-start | bytes 2359304 | tf_op jit(solution)/shard_map/ppermute | solution.py:29
  116.7 1.4 copy-start.4
  118.6 1.5 copy-start.2
  120.1 13.7 %collective-permute-start.10 = (bf16[256,768]{1,0:T(8,128)(2,1)S(1)}, bf16[256,768]{1,0:T(8,128)(2,1)S(1)}, u32[]{:S(2)}, u32[]{:S(2)}) collective-permute-start(bf16[256,768]{1,0:T(8,128)(2,1)S(1)} %get-tuple-element.14), channel_id=1, source_target_pairs={{0,2},{1,3},{2,0},{3,1},{4,6},{5,7},{6,4},{7,5},{8,10},{9,11},{10,... | collective-permute-start | bytes 1179656 | tf_op jit(solution)/shard_map/ppermute | solution.py:29
  134.6 31.1 %copy-start.3 = (bf16[512,768]{1,0:T(8,128)(2,1)S(1)}, bf16[512,768]{1,0:T(8,128)(2,1)}, u32[]{:S(2)}) copy-start(bf16[512,768]{1,0:T(8,128)(2,1)} %copy-done.2) | copy-start | bytes 2359300
  134.6 31.2 %all-to-all-start.1 = ((bf16[4,64,768]{2,1,0:T(8,128)(2,1)}), bf16[4,64,768]{2,1,0:T(8,128)(2,1)S(1)}, u32[]{:S(2)}, u32[]{:S(2)}) async-start(bf16[4,64,768]{2,1,0:T(8,128)(2,1)} %bitcast.4), calls=%async_computation.1 | async-start | bytes 786432 | tf_op jit(solution)/shard_map/all_to_all | solution.py:33
  148.6 25.4 %copy-start.5 = (bf16[512,768]{1,0:T(8,128)(2,1)S(1)}, bf16[512,768]{1,0:T(8,128)(2,1)}, u32[]{:S(2)}) copy-start(bf16[512,768]{1,0:T(8,128)(2,1)} %copy-done.4) | copy-start | bytes 2359300
  148.6 25.4 %copy-start.7 = (bf16[512,768]{1,0:T(8,128)(2,1)S(1)}, bf16[512,768]{1,0:T(8,128)(2,1)}, u32[]{:S(2)}) copy-start(bf16[512,768]{1,0:T(8,128)(2,1)} %copy-done.6) | copy-start | bytes 2359300
  148.6 13.0 %collective-permute-start.12 = (bf16[256,768]{1,0:T(8,128)(2,1)S(1)}, bf16[256,768]{1,0:T(8,128)(2,1)}, u32[]{:S(2)}, u32[]{:S(2)}) collective-permute-start(bf16[256,768]{1,0:T(8,128)(2,1)S(1)} %bitcast.23), channel_id=1, source_target_pairs={{0,1},{1,0},{2,3},{3,2},{4,5},{5,4},{6,7},{7,6},{8,9},{9,8},{10,11... | collective-permute-start | bytes 1179656 | tf_op jit(solution)/shard_map/ppermute | solution.py:29
  151.7 9.2 %collective-permute-start.7 = (bf16[32,768]{1,0:T(8,128)(2,1)S(1)}, bf16[32,768]{1,0:T(8,128)(2,1)S(1)}, u32[]{:S(2)}, u32[]{:S(2)}) collective-permute-start(bf16[32,768]{1,0:T(8,128)(2,1)S(1)} %slice.115), channel_id=1, source_target_pairs={{0,1},{1,0},{2,3},{3,2},{4,5},{5,4},{6,7},{7,6},{8,9},{9,8},{10,11... | collective-permute-start | bytes 147464 | tf_op jit(solution)/shard_map/ppermute | solution.py:29
  161.6 12.4 %collective-permute-start.13 = (bf16[256,768]{1,0:T(8,128)(2,1)}, bf16[256,768]{1,0:T(8,128)(2,1)}, u32[]{:S(2)}, u32[]{:S(2)}) collective-permute-start(bf16[256,768]{1,0:T(8,128)(2,1)} %collective-permute-done.12), channel_id=1, source_target_pairs={{0,32},{32,0},{64,96},{96,64},{128,160},{160,128},{192,224},{224,1... | collective-permute-start | bytes 1179656 | tf_op jit(solution)/shard_map/ppermute | solution.py:29
  165.9 11.8 %collective-permute-start.11 = (bf16[32,768]{1,0:T(8,128)(2,1)S(1)}, bf16[32,768]{1,0:T(8,128)(2,1)S(1)}, u32[]{:S(2)}, u32[]{:S(2)}) collective-permute-start(bf16[32,768]{1,0:T(8,128)(2,1)S(1)} %fusion.19), channel_id=1, source_target_pairs={{0,16},{1,17},{2,18},{3,19},{4,20},{5,21},{6,22},{7,23},{8,24},{9,... | collective-permute-start | bytes 147464 | tf_op jit(solution)/shard_map/ppermute | solution.py:29

commit v8 on v7

--- a/solution.py
+++ b/solution.py
@@ -63,7 +63,7 @@
     products(me, piece, (w0, w1), held, out)
 
 
-def send_kernel(me, early, piece, _, w0, w1, late, send, held):
+def send_kernel(me, early, piece, w0, w1, late, send, held):
     products(me, piece, (w0, w1), held, late)
 
     @pl.when(own_first(me))
@@ -85,13 +85,24 @@
         out[...] = (late[...] + got[...].astype(F32)).astype(BF16)
 
 
-def stack_kernel(me, mine0, mine1, got, value, out, passed):
-    passed[...] = value[...]
-    part = mine0.shape[0]
-    out[:part] = mine0[...]
-    out[part : 2 * part] = got[:part]
-    out[2 * part : 3 * part] = mine1[...]
-    out[3 * part :] = got[part:]
+def hold_kernel(me, value, out):
+    out[...] = value[...]
+
+
+def pick_kernel(me, own, other, _, mine, theirs):
+    part = own.shape[0] // 2
+    upper, odd = (me[0] >> 1) & 1, me[1] & 1
+    for piece, z in ((own, upper), (other, 1 - upper)):
+        to = pl.ds(pl.multiple_of(z * part, part), part)
+        mine[to, :] = piece[pl.ds(pl.multiple_of(odd * part, part), part), :]
+        theirs[to, :] = piece[pl.ds(pl.multiple_of((1 - odd) * part, part), part), :]
+
+
+def stack_kernel(me, mine, got, out):
+    part = mine.shape[0] // 2
+    for z in range(2):
+        out[2 * z * part : (2 * z + 1) * part] = mine[z * part : (z + 1) * part]
+        out[(2 * z + 1) * part : (2 * z + 2) * part] = got[z * part : (z + 1) * part]
 
 
 def order_kernel(me, line, across, _, out):
@@ -179,16 +190,10 @@
         early_kernel, [shape(size, width, F32)], held, flops, me, line, weight, partner
     )
 
-    other = swap(cotangent, "row", 2)
-    pairs = [jnp.where(upper, a, b) for a, b in ((other, cotangent), (cotangent, other))]
-    mine = [jnp.where(odd, p[part:], p[:part]) for p in pairs]
-    got = swap(jnp.concatenate([jnp.where(odd, p[:part], p[part:]) for p in pairs]), "col", 1)
-    cotangents = [*mine, got]
-
     late, send = call(
         send_kernel,
         [shape(size, width, F32), shape(size, width, BF16)],
-        held, flops, me, early, across, other, weight, partner,
+        held, flops, me, early, across, weight, partner,
     )
 
     (mine,) = call(
@@ -199,10 +204,18 @@
     size = tokens // 8
     got = spread(mine, "row", Y_GROUPS)
     mine = total([got[y * size : (y + 1) * size] for y in range(4)])
-    both, sent = call(
-        stack_kernel, [shape(size, width, BF16)] * 2, [], 0, me, *cotangents, mine.astype(BF16)
+    (sent,) = call(
+        hold_kernel, [shape(size, width, BF16)], [], 0, me, mine.astype(BF16)
     )
     pre = sent.astype(F32) + swap(sent, "row", 2).astype(F32)
+
+    other = swap(cotangent, "row", 2)
+    mine, theirs = call(
+        pick_kernel, [shape(2 * part, width, BF16)] * 2, [], 0, me, cotangent, other, sent
+    )
+    (both,) = call(
+        stack_kernel, [shape(4 * part, width, BF16)], [], 0, me, mine, swap(theirs, "col", 1)
+    )
 
     size = tokens // 16
     value = gelu_value(jnp.where(upper, pre[size:], pre[:size])).astype(BF16)

time: 179 us -> 171 us (0.955)
  waiting for transfers between devices: 32.7 us -> 22.5 us
  blocking collectives: 28 us -> 34 us
  starting transfers between devices: 96.1 us -> 90.4 us
    all_to_all x2, waiting for transfers between devices: 9.79 us -> 0.52 us  [spread(): lax.all_to_all(value, axis, split_axis=0, concat_axis=0, axis_index_group...]
    all_to_all x2, starting transfers between devices: 17.5 us -> 9.61 us  [spread(): lax.all_to_all(value, axis, split_axis=0, concat_axis=0, axis_index_group...]
    all_gather x1, blocking collectives: 12.2 us -> 18.2 us  [shards(): lax.all_gather(grad, 'row', axis=0, tiled=True, axis_index_groups=Y_GROUPS)]
    ppermute x14, starting transfers between devices: 78.6 us -> 80.8 us  [swap(): return lax.ppermute(value, axis, [(i, i ^ mask) for i in range(size)])]
    pallas_call x7 -> x9, Pallas kernels: 8.24 us -> 9.33 us  [call(): pl.pallas_call(kernel, out_shape=outs, in_specs=[pl.BlockSpec(memory_spac...]
  transfers between devices with their start and end apart: 16 -> 16, of which waited for: 8 -> 7; matrix products, arithmetic and copies ran while one was open for 5% -> 6% of each run, Pallas kernels for 2% -> 3%
where the time goes in v8:
time: 171 us; the launch traced here: 170 us
  starting transfers between devices  90.4 us (53%)
  blocking collectives  34 us (20%)
  waiting for transfers between devices  22.5 us (13%)
  Pallas kernels  9.33 us (5%)
  other arithmetic  6.4 us (4%)
  matrix products  3.57 us (2%)
  local copies, waits for them, and re-layouts  2.28 us (1%)
    ppermute x14, starting transfers between devices, swap(): return lax.ppermute(value, axis, [(i, i ^ mask) for i in range(size)])  80.8 us
    ppermute x14, waiting for transfers between devices, swap(): return lax.ppermute(value, axis, [(i, i ^ mask) for i in range(size)])  22 us
    all_gather x1, blocking collectives, shards(): lax.all_gather(grad, 'row', axis=0, tiled=True, axis_index_groups=Y_GROUPS)  18.2 us
    all_gather x1, blocking collectives, shards(): lax.all_gather(pair, 'col', axis=0, tiled=True, axis_index_groups=Z_GROUPS)  15.8 us
    all_to_all x2, starting transfers between devices, spread(): lax.all_to_all(value, axis, split_axis=0, concat_axis=0, axis_index_group...  9.61 us
    pallas_call x9, Pallas kernels, call(): pl.pallas_call(kernel, out_shape=outs, in_specs=[pl.BlockSpec(memory_spac...  9.33 us
    dot_general x1, matrix products, shards(): lax.dot_general(jnp.concatenate([near, far]), jnp.concatenate(own + other...  3.57 us
  transfers between devices with their start and end apart: 16, of which 7 were waited for; matrix products, arithmetic and copies ran while one was open for 6% of the time, Pallas kernels for 3%

profile of v8, /device:TPU:1, one launch (start us, length us, event | category | flops | bytes accessed | tf_op | source)
XLA Modules:
  0.0 169.6 jit_solution(4496337379785617905)
XLA Ops:
  0.6 4.0 %collective-permute-start.1 = (bf16[768,768]{1,0:T(8,128)(2,1)}, bf16[768,768]{1,0:T(8,128)(2,1)S(1)}, u32[]{:S(2)}, u32[]{:S(2)}) collective-permute-start(bf16[768,768]{1,0:T(8,128)(2,1)} %w0.7), channel_id=1, source_target_pairs={{0,1},{1,0},{2,3},{3,2},{4,5},{5,4},{6,7},{7,6},{8,9},{9,8},{10,11... | collective-permute-start | bytes 3538952 | tf_op jit(solution)/shard_map/ppermute | solution.py:29
  4.6 8.8 %collective-permute-start = (bf16[32,768]{1,0:T(8,128)(2,1)}, bf16[32,768]{1,0:T(8,128)(2,1)S(1)}, u32[]{:S(2)}, u32[]{:S(2)}) collective-permute-start(bf16[32,768]{1,0:T(8,128)(2,1)} %param.3), channel_id=1, source_target_pairs={{0,16},{1,17},{2,18},{3,19},{4,20},{5,21},{6,22},{7,23},{8,24},{9,... | collective-permute-start | bytes 147464 | tf_op jit(solution)/shard_map/ppermute | solution.py:29
  13.4 1.7 collective-permute-done
  15.9 15.8 %all_gather.6.piece.line = bf16[256,768]{1,0:T(8,128)(2,1)S(1)} all-gather(bf16[64,768]{1,0:T(8,128)(2,1)S(1)} %pad_maximum_fusion), channel_id=1, replica_groups={{0,4,8,12},{1,5,9,13},{2,6,10,14},{3,7,11,15},{16,20,24,28},{17,21,25,2..., dimensions={0}, use_global_device_ids=true | all-gather | bytes 491520 | tf_op jit(solution)/shard_map/all_gather | solution.py:184
  31.7 4.4 %collective-permute-start.2 = (bf16[256,768]{1,0:T(8,128)(2,1)S(1)}, bf16[256,768]{1,0:T(8,128)(2,1)S(1)}, u32[]{:S(2)}, u32[]{:S(2)}) collective-permute-start(bf16[256,768]{1,0:T(8,128)(2,1)S(1)} %all_gather.6.piece.line), channel_id=1, source_target_pairs={{0,2},{1,3},{2,0},{3,1},{4,6},{5,7},{6,4},{7,5},{8,10},{9,11},{10,... | collective-permute-start | bytes 1179656 | tf_op jit(solution)/shard_map/ppermute | solution.py:29
  36.1 1.3 copy-done
  37.4 1.3 shard_map.58.early
  38.7 3.1 %collective-permute-done.2.piece.across = bf16[256,768]{1,0:T(8,128)(2,1)S(1)} collective-permute-done((bf16[256,768]{1,0:T(8,128)(2,1)S(1)}, bf16[256,768]{1,0:T(8,128)(2,1)S(1)}, u32[]{:S(2)}, u32[]{:S(2)}) %collective-permute-start.2) | collective-permute-done | bytes 393248 | tf_op jit(solution)/shard_map/ppermute | solution.py:29
  41.8 1.4 shard_map.59
  43.3 8.3 %collective-permute-start.3 = (bf16[512,768]{1,0:T(8,128)(2,1)S(1)}, bf16[512,768]{1,0:T(8,128)(2,1)S(1)}, u32[]{:S(2)}, u32[]{:S(2)}) collective-permute-start(bf16[512,768]{1,0:T(8,128)(2,1)S(1)} %get-tuple-element.10), channel_id=1, source_target_pairs={{0,32},{32,0},{64,96},{96,64},{128,160},{160,128},{192,224},{224,1... | collective-permute-start | bytes 2359304 | tf_op jit(solution)/shard_map/ppermute | solution.py:29
  51.5 1.9 %collective-permute-done.3.got = bf16[512,768]{1,0:T(8,128)(2,1)S(1)} collective-permute-done((bf16[512,768]{1,0:T(8,128)(2,1)S(1)}, bf16[512,768]{1,0:T(8,128)(2,1)S(1)}, u32[]{:S(2)}, u32[]{:S(2)}) %collective-permute-start.3) | collective-permute-done | bytes 786464 | tf_op jit(solution)/shard_map/ppermute | solution.py:29
  53.4 1.6 shard_map.60
  55.0 4.3 %all-to-all-start = ((bf16[4,128,768]{2,1,0:T(8,128)(2,1)}), bf16[4,128,768]{2,1,0:T(8,128)(2,1)}, u32[]{:S(2)}, u32[]{:S(2)}) async-start(bf16[4,128,768]{2,1,0:T(8,128)(2,1)} %bitcast.2), calls=%async_computation | async-start | bytes 1572864 | tf_op jit(solution)/shard_map/all_to_all | solution.py:33
  59.3 11.6 %collective-permute-start.6 = (bf16[64,768]{1,0:T(8,128)(2,1)S(1)}, bf16[64,768]{1,0:T(8,128)(2,1)S(1)}, u32[]{:S(2)}, u32[]{:S(2)}) collective-permute-start(bf16[64,768]{1,0:T(8,128)(2,1)S(1)} %copy-done.8), channel_id=1, source_target_pairs={{0,64},{32,96},{64,0},{96,32},{128,192},{160,224},{192,128},{224,1... | collective-permute-start | bytes 294920 | tf_op jit(solution)/shard_map/ppermute | solution.py:29
  71.4 1.3 fusion.16.value
  73.3 11.3 %collective-permute-start.4 = (bf16[128,768]{1,0:T(8,128)(2,1)S(1)}, bf16[128,768]{1,0:T(8,128)(2,1)S(1)}, u32[]{:S(2)}, u32[]{:S(2)}) collective-permute-start(bf16[128,768]{1,0:T(8,128)(2,1)S(1)} %shard_map.61._), channel_id=1, source_target_pairs={{0,64},{32,96},{64,0},{96,32},{128,192},{160,224},{192,128},{224,1... | collective-permute-start | bytes 589832 | tf_op jit(solution)/shard_map/ppermute | solution.py:29
  85.2 2.2 %collective-permute-start.7 = (bf16[64,768]{1,0:T(8,128)(2,1)S(1)}, bf16[64,768]{1,0:T(8,128)(2,1)S(1)}, u32[]{:S(2)}, u32[]{:S(2)}) collective-permute-start(bf16[64,768]{1,0:T(8,128)(2,1)S(1)} %get-tuple-element.12), channel_id=1, source_target_pairs={{0,1},{1,0},{2,3},{3,2},{4,5},{5,4},{6,7},{7,6},{8,9},{9,8},{10,11... | collective-permute-start | bytes 294920 | tf_op jit(solution)/shard_map/ppermute | solution.py:29
  87.9 3.1 %collective-permute-start.8 = (bf16[512,768]{1,0:T(8,128)(2,1)S(1)}, bf16[512,768]{1,0:T(8,128)(2,1)S(1)}, u32[]{:S(2)}, u32[]{:S(2)}) collective-permute-start(bf16[512,768]{1,0:T(8,128)(2,1)S(1)} %shard_map.64), channel_id=1, source_target_pairs={{0,1},{1,0},{2,3},{3,2},{4,5},{5,4},{6,7},{7,6},{8,9},{9,8},{10,11... | collective-permute-start | bytes 2359304 | tf_op jit(solution)/shard_map/ppermute | solution.py:29
  92.6 18.2 %all_gather.7.grad = bf16[512,768]{1,0:T(8,128)(2,1)S(1)} all-gather(bf16[128,768]{1,0:T(8,128)(2,1)S(1)} %get-tuple-element.17), channel_id=1, replica_groups={{0,128,256,384},{32,160,288,416},{64,192,320,448},{96,224,352,480},{1,1..., dimensions={0}, use_global_device_ids=true | all-gather | bytes 983040 | tf_op jit(solution)/shard_map/all_gather | solution.py:226
  110.8 6.9 %collective-permute-start.9 = (bf16[512,768]{1,0:T(8,128)(2,1)S(1)}, bf16[512,768]{1,0:T(8,128)(2,1)S(1)}, u32[]{:S(2)}, u32[]{:S(2)}) collective-permute-start(bf16[512,768]{1,0:T(8,128)(2,1)S(1)} %all_gather.7.grad), channel_id=1, source_target_pairs={{0,32},{32,0},{64,96},{96,64},{128,160},{160,128},{192,224},{224,1... | collective-permute-start | bytes 2359304 | tf_op jit(solution)/shard_map/ppermute | solution.py:29
  117.8 1.3 shard_map.65.first
  119.7 1.4 shard_map.66
  121.1 4.8 %collective-permute-start.10 = (bf16[256,768]{1,0:T(8,128)(2,1)S(1)}, bf16[256,768]{1,0:T(8,128)(2,1)S(1)}, u32[]{:S(2)}, u32[]{:S(2)}) collective-permute-start(bf16[256,768]{1,0:T(8,128)(2,1)S(1)} %get-tuple-element.14), channel_id=1, source_target_pairs={{0,2},{1,3},{2,0},{3,1},{4,6},{5,7},{6,4},{7,5},{8,10},{9,11},{10,... | collective-permute-start | bytes 1179656 | tf_op jit(solution)/shard_map/ppermute | solution.py:29
  125.9 8.9 %collective-permute-done.10 = bf16[256,768]{1,0:T(8,128)(2,1)S(1)} collective-permute-done((bf16[256,768]{1,0:T(8,128)(2,1)S(1)}, bf16[256,768]{1,0:T(8,128)(2,1)S(1)}, u32[]{:S(2)}, u32[]{:S(2)}) %collective-permute-start.10) | collective-permute-done | bytes 393248 | tf_op jit(solution)/shard_map/ppermute | solution.py:29
  135.6 5.3 %all-to-all-start.1 = ((bf16[4,64,768]{2,1,0:T(8,128)(2,1)}), bf16[4,64,768]{2,1,0:T(8,128)(2,1)S(1)}, u32[]{:S(2)}, u32[]{:S(2)}) async-start(bf16[4,64,768]{2,1,0:T(8,128)(2,1)} %bitcast.4), calls=%async_computation.1 | async-start | bytes 786432 | tf_op jit(solution)/shard_map/all_to_all | solution.py:33
  141.9 2.2 %collective-permute-start.12 = (bf16[256,768]{1,0:T(8,128)(2,1)}, bf16[256,768]{1,0:T(8,128)(2,1)}, u32[]{:S(2)}, u32[]{:S(2)}) collective-permute-start(bf16[256,768]{1,0:T(8,128)(2,1)} %bitcast.11), channel_id=1, source_target_pairs={{0,1},{1,0},{2,3},{3,2},{4,5},{5,4},{6,7},{7,6},{8,9},{9,8},{10,11... | collective-permute-start | bytes 1179656 | tf_op jit(solution)/shard_map/ppermute | solution.py:29
  144.1 1.1 multiply_convert_fusion.1
  145.2 3.2 %collective-permute-start.5 = (bf16[32,768]{1,0:T(8,128)(2,1)S(1)}, bf16[32,768]{1,0:T(8,128)(2,1)S(1)}, u32[]{:S(2)}, u32[]{:S(2)}) collective-permute-start(bf16[32,768]{1,0:T(8,128)(2,1)S(1)} %slice.91), channel_id=1, source_target_pairs={{0,1},{1,0},{2,3},{3,2},{4,5},{5,4},{6,7},{7,6},{8,9},{9,8},{10,11... | collective-permute-start | bytes 147464 | tf_op jit(solution)/shard_map/ppermute | solution.py:29
  148.4 6.0 %collective-permute-done.5 = bf16[32,768]{1,0:T(8,128)(2,1)S(1)} collective-permute-done((bf16[32,768]{1,0:T(8,128)(2,1)S(1)}, bf16[32,768]{1,0:T(8,128)(2,1)S(1)}, u32[]{:S(2)}, u32[]{:S(2)}) %collective-permute-start.5) | collective-permute-done | bytes 49184 | tf_op jit(solution)/shard_map/ppermute | solution.py:29
  155.0 4.2 %collective-permute-start.13 = (bf16[256,768]{1,0:T(8,128)(2,1)}, bf16[256,768]{1,0:T(8,128)(2,1)}, u32[]{:S(2)}, u32[]{:S(2)}) collective-permute-start(bf16[256,768]{1,0:T(8,128)(2,1)} %collective-permute-done.12), channel_id=1, source_target_pairs={{0,32},{32,0},{64,96},{96,64},{128,160},{160,128},{192,224},{224,1... | collective-permute-start | bytes 1179656 | tf_op jit(solution)/shard_map/ppermute | solution.py:29
  159.4 5.9 %collective-permute-start.11 = (bf16[32,768]{1,0:T(8,128)(2,1)S(1)}, bf16[32,768]{1,0:T(8,128)(2,1)S(1)}, u32[]{:S(2)}, u32[]{:S(2)}) collective-permute-start(bf16[32,768]{1,0:T(8,128)(2,1)S(1)} %fusion.19), channel_id=1, source_target_pairs={{0,16},{1,17},{2,18},{3,19},{4,20},{5,21},{6,22},{7,23},{8,24},{9,... | collective-permute-start | bytes 147464 | tf_op jit(solution)/shard_map/ppermute | solution.py:29
  165.4 3.6 %multiply_convert_fusion = bf16[768,768]{1,0:T(8,128)(2,1)} fusion(bf16[512,768]{1,0:T(8,128)(2,1)S(1)} %copy-done.5, bf16[512,768]{1,0:T(8,128)(2,1)S(1)} %copy-done.7, bf16[256,768]{1,0:T(8,128)(2,1)} %collective-permute-done.13, bf16[256,768]{1,0:T(8,128)(2,1)} %collective-permute-done.12, bf16[256,768]{1,0:T(8,128)(2,1)S(1)} %bitcast.21, ...), kind=kOutput, calls=%fused_computation | convolution fusion | flops 1218576384 | bytes 4325376 | tf_op jit(solution)/shard_map/dot_general | solution.py:256
  (46 shorter events, 8.3 us)
Async XLA Ops:
  0.6 35.5 %collective-permute-start.1 = (bf16[768,768]{1,0:T(8,128)(2,1)}, bf16[768,768]{1,0:T(8,128)(2,1)S(1)}, u32[]{:S(2)}, u32[]{:S(2)}) collective-permute-start(bf16[768,768]{1,0:T(8,128)(2,1)} %w0.7), channel_id=1, source_target_pairs={{0,1},{1,0},{2,3},{3,2},{4,5},{5,4},{6,7},{7,6},{8,9},{9,8},{10,11... | collective-permute-start | bytes 3538952 | tf_op jit(solution)/shard_map/ppermute | solution.py:29
  4.6 10.5 %collective-permute-start = (bf16[32,768]{1,0:T(8,128)(2,1)}, bf16[32,768]{1,0:T(8,128)(2,1)S(1)}, u32[]{:S(2)}, u32[]{:S(2)}) collective-permute-start(bf16[32,768]{1,0:T(8,128)(2,1)} %param.3), channel_id=1, source_target_pairs={{0,16},{1,17},{2,18},{3,19},{4,20},{5,21},{6,22},{7,23},{8,24},{9,... | collective-permute-start | bytes 147464 | tf_op jit(solution)/shard_map/ppermute | solution.py:29
  31.7 10.2 %collective-permute-start.2 = (bf16[256,768]{1,0:T(8,128)(2,1)S(1)}, bf16[256,768]{1,0:T(8,128)(2,1)S(1)}, u32[]{:S(2)}, u32[]{:S(2)}) collective-permute-start(bf16[256,768]{1,0:T(8,128)(2,1)S(1)} %all_gather.6.piece.line), channel_id=1, source_target_pairs={{0,2},{1,3},{2,0},{3,1},{4,6},{5,7},{6,4},{7,5},{8,10},{9,11},{10,... | collective-permute-start | bytes 1179656 | tf_op jit(solution)/shard_map/ppermute | solution.py:29
  36.1 1.3 copy-start
  37.4 4.4 %copy-start.1 = (bf16[768,768]{1,0:T(8,128)(2,1)S(1)}, bf16[768,768]{1,0:T(8,128)(2,1)}, u32[]{:S(2)}) copy-start(bf16[768,768]{1,0:T(8,128)(2,1)} %w0.7) | copy-start | bytes 3538948
  43.3 10.2 %collective-permute-start.3 = (bf16[512,768]{1,0:T(8,128)(2,1)S(1)}, bf16[512,768]{1,0:T(8,128)(2,1)S(1)}, u32[]{:S(2)}, u32[]{:S(2)}) collective-permute-start(bf16[512,768]{1,0:T(8,128)(2,1)S(1)} %get-tuple-element.10), channel_id=1, source_target_pairs={{0,32},{32,0},{64,96},{96,64},{128,160},{160,128},{192,224},{224,1... | collective-permute-start | bytes 2359304 | tf_op jit(solution)/shard_map/ppermute | solution.py:29
  55.0 4.3 %copy-start.8 = (bf16[64,768]{1,0:T(8,128)(2,1)S(1)}, bf16[64,768]{1,0:T(8,128)(2,1)}, u32[]{:S(2)}) copy-start(bf16[64,768]{1,0:T(8,128)(2,1)} %own.1) | copy-start | bytes 294916
  55.0 16.4 %all-to-all-start = ((bf16[4,128,768]{2,1,0:T(8,128)(2,1)}), bf16[4,128,768]{2,1,0:T(8,128)(2,1)}, u32[]{:S(2)}, u32[]{:S(2)}) async-start(bf16[4,128,768]{2,1,0:T(8,128)(2,1)} %bitcast.2), calls=%async_computation | async-start | bytes 1572864 | tf_op jit(solution)/shard_map/all_to_all | solution.py:33
  59.3 25.3 %collective-permute-start.6 = (bf16[64,768]{1,0:T(8,128)(2,1)S(1)}, bf16[64,768]{1,0:T(8,128)(2,1)S(1)}, u32[]{:S(2)}, u32[]{:S(2)}) collective-permute-start(bf16[64,768]{1,0:T(8,128)(2,1)S(1)} %copy-done.8), channel_id=1, source_target_pairs={{0,64},{32,96},{64,0},{96,32},{128,192},{160,224},{192,128},{224,1... | collective-permute-start | bytes 294920 | tf_op jit(solution)/shard_map/ppermute | solution.py:29
  73.3 18.4 %collective-permute-start.4 = (bf16[128,768]{1,0:T(8,128)(2,1)S(1)}, bf16[128,768]{1,0:T(8,128)(2,1)S(1)}, u32[]{:S(2)}, u32[]{:S(2)}) collective-permute-start(bf16[128,768]{1,0:T(8,128)(2,1)S(1)} %shard_map.61._), channel_id=1, source_target_pairs={{0,64},{32,96},{64,0},{96,32},{128,192},{160,224},{192,128},{224,1... | collective-permute-start | bytes 589832 | tf_op jit(solution)/shard_map/ppermute | solution.py:29
  85.2 5.9 %collective-permute-start.7 = (bf16[64,768]{1,0:T(8,128)(2,1)S(1)}, bf16[64,768]{1,0:T(8,128)(2,1)S(1)}, u32[]{:S(2)}, u32[]{:S(2)}) collective-permute-start(bf16[64,768]{1,0:T(8,128)(2,1)S(1)} %get-tuple-element.12), channel_id=1, source_target_pairs={{0,1},{1,0},{2,3},{3,2},{4,5},{5,4},{6,7},{7,6},{8,9},{9,8},{10,11... | collective-permute-start | bytes 294920 | tf_op jit(solution)/shard_map/ppermute | solution.py:29
  87.9 31.2 %copy-start.6 = (bf16[512,768]{1,0:T(8,128)(2,1)}, bf16[512,768]{1,0:T(8,128)(2,1)S(1)}, u32[]{:S(2)}) copy-start(bf16[512,768]{1,0:T(8,128)(2,1)S(1)} %shard_map.64) | copy-start | bytes 2359300
  87.9 29.8 %collective-permute-start.8 = (bf16[512,768]{1,0:T(8,128)(2,1)S(1)}, bf16[512,768]{1,0:T(8,128)(2,1)S(1)}, u32[]{:S(2)}, u32[]{:S(2)}) collective-permute-start(bf16[512,768]{1,0:T(8,128)(2,1)S(1)} %shard_map.64), channel_id=1, source_target_pairs={{0,1},{1,0},{2,3},{3,2},{4,5},{5,4},{6,7},{7,6},{8,9},{9,8},{10,11... | collective-permute-start | bytes 2359304 | tf_op jit(solution)/shard_map/ppermute | solution.py:29
  110.8 8.8 %collective-permute-start.9 = (bf16[512,768]{1,0:T(8,128)(2,1)S(1)}, bf16[512,768]{1,0:T(8,128)(2,1)S(1)}, u32[]{:S(2)}, u32[]{:S(2)}) collective-permute-start(bf16[512,768]{1,0:T(8,128)(2,1)S(1)} %all_gather.7.grad), channel_id=1, source_target_pairs={{0,32},{32,0},{64,96},{96,64},{128,160},{160,128},{192,224},{224,1... | collective-permute-start | bytes 2359304 | tf_op jit(solution)/shard_map/ppermute | solution.py:29
  117.8 1.4 copy-start.4
  119.6 1.4 copy-start.2
  121.1 13.7 %collective-permute-start.10 = (bf16[256,768]{1,0:T(8,128)(2,1)S(1)}, bf16[256,768]{1,0:T(8,128)(2,1)S(1)}, u32[]{:S(2)}, u32[]{:S(2)}) collective-permute-start(bf16[256,768]{1,0:T(8,128)(2,1)S(1)} %get-tuple-element.14), channel_id=1, source_target_pairs={{0,2},{1,3},{2,0},{3,1},{4,6},{5,7},{6,4},{7,5},{8,10},{9,11},{10,... | collective-permute-start | bytes 1179656 | tf_op jit(solution)/shard_map/ppermute | solution.py:29
  135.6 23.6 %copy-start.3 = (bf16[512,768]{1,0:T(8,128)(2,1)S(1)}, bf16[512,768]{1,0:T(8,128)(2,1)}, u32[]{:S(2)}) copy-start(bf16[512,768]{1,0:T(8,128)(2,1)} %copy-done.2) | copy-start | bytes 2359300
  135.6 23.7 %all-to-all-start.1 = ((bf16[4,64,768]{2,1,0:T(8,128)(2,1)}), bf16[4,64,768]{2,1,0:T(8,128)(2,1)S(1)}, u32[]{:S(2)}, u32[]{:S(2)}) async-start(bf16[4,64,768]{2,1,0:T(8,128)(2,1)} %bitcast.4), calls=%async_computation.1 | async-start | bytes 786432 | tf_op jit(solution)/shard_map/all_to_all | solution.py:33
  141.9 23.5 %copy-start.5 = (bf16[512,768]{1,0:T(8,128)(2,1)S(1)}, bf16[512,768]{1,0:T(8,128)(2,1)}, u32[]{:S(2)}) copy-start(bf16[512,768]{1,0:T(8,128)(2,1)} %copy-done.4) | copy-start | bytes 2359300
  141.9 23.5 %copy-start.7 = (bf16[512,768]{1,0:T(8,128)(2,1)S(1)}, bf16[512,768]{1,0:T(8,128)(2,1)}, u32[]{:S(2)}) copy-start(bf16[512,768]{1,0:T(8,128)(2,1)} %copy-done.6) | copy-start | bytes 2359300
  141.9 23.5 %copy-start.9 = (bf16[8,1,32,768]{3,2,1,0:T(8,128)(2,1)S(1)}, bf16[8,1,32,768]{3,2,1,0:T(8,128)(2,1)}, u32[]{:S(2)}) copy-start(bf16[8,1,32,768]{3,2,1,0:T(8,128)(2,1)} %get-tuple-element.15) | copy-start | bytes 1179652
  141.9 13.2 %collective-permute-start.12 = (bf16[256,768]{1,0:T(8,128)(2,1)}, bf16[256,768]{1,0:T(8,128)(2,1)}, u32[]{:S(2)}, u32[]{:S(2)}) collective-permute-start(bf16[256,768]{1,0:T(8,128)(2,1)} %bitcast.11), channel_id=1, source_target_pairs={{0,1},{1,0},{2,3},{3,2},{4,5},{5,4},{6,7},{7,6},{8,9},{9,8},{10,11... | collective-permute-start | bytes 1179656 | tf_op jit(solution)/shard_map/ppermute | solution.py:29
  145.2 9.2 %collective-permute-start.5 = (bf16[32,768]{1,0:T(8,128)(2,1)S(1)}, bf16[32,768]{1,0:T(8,128)(2,1)S(1)}, u32[]{:S(2)}, u32[]{:S(2)}) collective-permute-start(bf16[32,768]{1,0:T(8,128)(2,1)S(1)} %slice.91), channel_id=1, source_target_pairs={{0,1},{1,0},{2,3},{3,2},{4,5},{5,4},{6,7},{7,6},{8,9},{9,8},{10,11... | collective-permute-start | bytes 147464 | tf_op jit(solution)/shard_map/ppermute | solution.py:29
  155.0 10.3 %collective-permute-start.13 = (bf16[256,768]{1,0:T(8,128)(2,1)}, bf16[256,768]{1,0:T(8,128)(2,1)}, u32[]{:S(2)}, u32[]{:S(2)}) collective-permute-start(bf16[256,768]{1,0:T(8,128)(2,1)} %collective-permute-done.12), channel_id=1, source_target_pairs={{0,32},{32,0},{64,96},{96,64},{128,160},{160,128},{192,224},{224,1... | collective-permute-start | bytes 1179656 | tf_op jit(solution)/shard_map/ppermute | solution.py:29
  159.4 9.6 %collective-permute-start.11 = (bf16[32,768]{1,0:T(8,128)(2,1)S(1)}, bf16[32,768]{1,0:T(8,128)(2,1)S(1)}, u32[]{:S(2)}, u32[]{:S(2)}) collective-permute-start(bf16[32,768]{1,0:T(8,128)(2,1)S(1)} %fusion.19), channel_id=1, source_target_pairs={{0,16},{1,17},{2,18},{3,19},{4,20},{5,21},{6,22},{7,23},{8,24},{9,... | collective-permute-start | bytes 147464 | tf_op jit(solution)/shard_map/ppermute | solution.py:29

commit v9 on v8

--- a/solution.py
+++ b/solution.py
@@ -85,8 +85,12 @@
         out[...] = (late[...] + got[...].astype(F32)).astype(BF16)
 
 
-def hold_kernel(me, value, out):
-    out[...] = value[...]
+def four_kernel(me, got, out):
+    size = out.shape[0]
+    value = got[:size].astype(F32)
+    for y in range(1, 4):
+        value += got[y * size : (y + 1) * size].astype(F32)
+    out[...] = value.astype(BF16)
 
 
 def pick_kernel(me, own, other, _, mine, theirs):
@@ -132,7 +136,10 @@
     return values[0] + values[1]
 
 
-def first_kernel(me, grad, _, w0, w1, out, held):
+def first_kernel(me, grad, _, w0, w1, out, theirs, held):
+    part = theirs.shape[0] // 8
+    for z in range(8):
+        theirs[z * part : (z + 1) * part] = grad[(2 * z + 1) * part : (2 * z + 2) * part]
     out[...] = back(me, grad, (w0, w1), held)
 
 
@@ -202,10 +209,8 @@
         [], size * width, me, early, late, swap(send, "row", 1),
     )
     size = tokens // 8
-    got = spread(mine, "row", Y_GROUPS)
-    mine = total([got[y * size : (y + 1) * size] for y in range(4)])
     (sent,) = call(
-        hold_kernel, [shape(size, width, BF16)], [], 0, me, mine.astype(BF16)
+        four_kernel, [shape(size, width, BF16)], [], 0, me, spread(mine, "row", Y_GROUPS)
     )
     pre = sent.astype(F32) + swap(sent, "row", 2).astype(F32)
 
@@ -232,9 +237,9 @@
 
     size = tokens // 4
     held = [pltpu.VMEM((2, size, width), BF16)]
-    (first,) = call(
+    first, theirs = call(
         first_kernel,
-        [shape(size, depth, F32)],
+        [shape(size, depth, F32), shape(size, width, BF16)],
         held, flops, me, g0, far, weight, partner,
     )
     keep, send = call(
@@ -251,7 +256,7 @@
 
     split = [g.reshape(8, 2, part, width) for g in (g0, g1)]
     own = [g[:, 0].reshape(-1, width) for g in split]
-    others = [swap(split[0][:, 1].reshape(-1, width), "col", 1)]
+    others = [swap(theirs, "col", 1)]
     others += [swap(others[0], "row", 1)]
     weight_sum = lax.dot_general(
         jnp.concatenate([near, far]),

time: 171 us -> 170 us (level)
  waiting for transfers between devices: 22.5 us -> 19.1 us
  local copies, waits for them, and re-layouts: 2.28 us -> 4.44 us
    ppermute x14, waiting for transfers between devices: 22 us -> 19.1 us  [swap(): return lax.ppermute(value, axis, [(i, i ^ mask) for i in range(size)])]
    ppermute x14, starting transfers between devices: 80.8 us -> 83.1 us  [swap(): return lax.ppermute(value, axis, [(i, i ^ mask) for i in range(size)])]
    all_to_all x2, starting transfers between devices: 9.61 us -> 7.81 us  [spread(): lax.all_to_all(value, axis, split_axis=0, concat_axis=0, axis_index_group...]
  transfers between devices with their start and end apart: 16 -> 16, of which waited for: 7 -> 6; matrix products, arithmetic and copies ran while one was open for 6% -> 7% of each run, Pallas kernels for 3% -> 3%
where the time goes in v9:
time: 170 us; the launch traced here: 169 us
  starting transfers between devices  90.9 us (53%)
  blocking collectives  32.5 us (19%)
  waiting for transfers between devices  19.1 us (11%)
  Pallas kernels  9.79 us (6%)
  other arithmetic  7.7 us (5%)
  local copies, waits for them, and re-layouts  4.44 us (3%)
  matrix products  3.45 us (2%)
    ppermute x14, starting transfers between devices, swap(): return lax.ppermute(value, axis, [(i, i ^ mask) for i in range(size)])  83.1 us
    ppermute x14, waiting for transfers between devices, swap(): return lax.ppermute(value, axis, [(i, i ^ mask) for i in range(size)])  19.1 us
    all_gather x1, blocking collectives, shards(): lax.all_gather(grad, 'row', axis=0, tiled=True, axis_index_groups=Y_GROUPS)  16.7 us
    all_gather x1, blocking collectives, shards(): lax.all_gather(pair, 'col', axis=0, tiled=True, axis_index_groups=Z_GROUPS)  15.8 us
    pallas_call x9, Pallas kernels, call(): pl.pallas_call(kernel, out_shape=outs, in_specs=[pl.BlockSpec(memory_spac...  9.79 us
    all_to_all x2, starting transfers between devices, spread(): lax.all_to_all(value, axis, split_axis=0, concat_axis=0, axis_index_group...  7.81 us
    dot_general x1, matrix products, shards(): lax.dot_general(jnp.concatenate([near, far]), jnp.concatenate(own + other...  3.45 us
  transfers between devices with their start and end apart: 16, of which 6 were waited for; matrix products, arithmetic and copies ran while one was open for 7% of the time, Pallas kernels for 3%

profile of v9, /device:TPU:1, one launch (start us, length us, event | category | flops | bytes accessed | tf_op | source)
XLA Modules:
  0.0 168.9 jit_solution(16683946907626175922)
XLA Ops:
  0.6 4.0 %collective-permute-start.1 = (bf16[768,768]{1,0:T(8,128)(2,1)}, bf16[768,768]{1,0:T(8,128)(2,1)S(1)}, u32[]{:S(2)}, u32[]{:S(2)}) collective-permute-start(bf16[768,768]{1,0:T(8,128)(2,1)} %w0.7), channel_id=1, source_target_pairs={{0,1},{1,0},{2,3},{3,2},{4,5},{5,4},{6,7},{7,6},{8,9},{9,8},{10,11... | collective-permute-start | bytes 3538952 | tf_op jit(solution)/shard_map/ppermute | solution.py:29
  4.6 8.8 %collective-permute-start = (bf16[32,768]{1,0:T(8,128)(2,1)}, bf16[32,768]{1,0:T(8,128)(2,1)S(1)}, u32[]{:S(2)}, u32[]{:S(2)}) collective-permute-start(bf16[32,768]{1,0:T(8,128)(2,1)} %param.3), channel_id=1, source_target_pairs={{0,16},{1,17},{2,18},{3,19},{4,20},{5,21},{6,22},{7,23},{8,24},{9,... | collective-permute-start | bytes 147464 | tf_op jit(solution)/shard_map/ppermute | solution.py:29
  13.4 1.7 collective-permute-done
  15.9 15.8 %all_gather.6.piece.line = bf16[256,768]{1,0:T(8,128)(2,1)S(1)} all-gather(bf16[64,768]{1,0:T(8,128)(2,1)S(1)} %pad_maximum_fusion), channel_id=1, replica_groups={{0,4,8,12},{1,5,9,13},{2,6,10,14},{3,7,11,15},{16,20,24,28},{17,21,25,2..., dimensions={0}, use_global_device_ids=true | all-gather | bytes 491520 | tf_op jit(solution)/shard_map/all_gather | solution.py:191
  31.7 4.4 %collective-permute-start.2 = (bf16[256,768]{1,0:T(8,128)(2,1)S(1)}, bf16[256,768]{1,0:T(8,128)(2,1)S(1)}, u32[]{:S(2)}, u32[]{:S(2)}) collective-permute-start(bf16[256,768]{1,0:T(8,128)(2,1)S(1)} %all_gather.6.piece.line), channel_id=1, source_target_pairs={{0,2},{1,3},{2,0},{3,1},{4,6},{5,7},{6,4},{7,5},{8,10},{9,11},{10,... | collective-permute-start | bytes 1179656 | tf_op jit(solution)/shard_map/ppermute | solution.py:29
  36.2 1.3 copy-done
  37.4 1.3 shard_map.58.early
  38.7 3.1 %collective-permute-done.2.piece.across = bf16[256,768]{1,0:T(8,128)(2,1)S(1)} collective-permute-done((bf16[256,768]{1,0:T(8,128)(2,1)S(1)}, bf16[256,768]{1,0:T(8,128)(2,1)S(1)}, u32[]{:S(2)}, u32[]{:S(2)}) %collective-permute-start.2) | collective-permute-done | bytes 393248 | tf_op jit(solution)/shard_map/ppermute | solution.py:29
  41.8 1.4 shard_map.59
  43.3 8.3 %collective-permute-start.3 = (bf16[512,768]{1,0:T(8,128)(2,1)S(1)}, bf16[512,768]{1,0:T(8,128)(2,1)S(1)}, u32[]{:S(2)}, u32[]{:S(2)}) collective-permute-start(bf16[512,768]{1,0:T(8,128)(2,1)S(1)} %get-tuple-element.12), channel_id=1, source_target_pairs={{0,32},{32,0},{64,96},{96,64},{128,160},{160,128},{192,224},{224,1... | collective-permute-start | bytes 2359304 | tf_op jit(solution)/shard_map/ppermute | solution.py:29
  51.5 1.9 %collective-permute-done.3.got = bf16[512,768]{1,0:T(8,128)(2,1)S(1)} collective-permute-done((bf16[512,768]{1,0:T(8,128)(2,1)S(1)}, bf16[512,768]{1,0:T(8,128)(2,1)S(1)}, u32[]{:S(2)}, u32[]{:S(2)}) %collective-permute-start.3) | collective-permute-done | bytes 786464 | tf_op jit(solution)/shard_map/ppermute | solution.py:29
  53.4 1.6 shard_map.60
  55.0 3.5 %all-to-all-start = ((bf16[4,128,768]{2,1,0:T(8,128)(2,1)}), bf16[4,128,768]{2,1,0:T(8,128)(2,1)S(1)}, u32[]{:S(2)}, u32[]{:S(2)}) async-start(bf16[4,128,768]{2,1,0:T(8,128)(2,1)} %bitcast.2), calls=%async_computation | async-start | bytes 1572864 | tf_op jit(solution)/shard_map/all_to_all | solution.py:33
  58.5 12.2 %collective-permute-start.6 = (bf16[64,768]{1,0:T(8,128)(2,1)}, bf16[64,768]{1,0:T(8,128)(2,1)}, u32[]{:S(2)}, u32[]{:S(2)}) collective-permute-start(bf16[64,768]{1,0:T(8,128)(2,1)} %own.1), channel_id=1, source_target_pairs={{0,64},{32,96},{64,0},{96,32},{128,192},{160,224},{192,128},{224,1... | collective-permute-start | bytes 294920 | tf_op jit(solution)/shard_map/ppermute | solution.py:29
  71.4 11.7 %collective-permute-start.4 = (bf16[128,768]{1,0:T(8,128)(2,1)S(1)}, bf16[128,768]{1,0:T(8,128)(2,1)S(1)}, u32[]{:S(2)}, u32[]{:S(2)}) collective-permute-start(bf16[128,768]{1,0:T(8,128)(2,1)S(1)} %shard_map.61._), channel_id=1, source_target_pairs={{0,64},{32,96},{64,0},{96,32},{128,192},{160,224},{192,128},{224,1... | collective-permute-start | bytes 589832 | tf_op jit(solution)/shard_map/ppermute | solution.py:29
  84.9 2.2 %collective-permute-start.7 = (bf16[64,768]{1,0:T(8,128)(2,1)S(1)}, bf16[64,768]{1,0:T(8,128)(2,1)S(1)}, u32[]{:S(2)}, u32[]{:S(2)}) collective-permute-start(bf16[64,768]{1,0:T(8,128)(2,1)S(1)} %get-tuple-element.14), channel_id=1, source_target_pairs={{0,1},{1,0},{2,3},{3,2},{4,5},{5,4},{6,7},{7,6},{8,9},{9,8},{10,11... | collective-permute-start | bytes 294920 | tf_op jit(solution)/shard_map/ppermute | solution.py:29
  87.7 3.1 %collective-permute-start.8 = (bf16[512,768]{1,0:T(8,128)(2,1)S(1)}, bf16[512,768]{1,0:T(8,128)(2,1)S(1)}, u32[]{:S(2)}, u32[]{:S(2)}) collective-permute-start(bf16[512,768]{1,0:T(8,128)(2,1)S(1)} %shard_map.64), channel_id=1, source_target_pairs={{0,1},{1,0},{2,3},{3,2},{4,5},{5,4},{6,7},{7,6},{8,9},{9,8},{10,11... | collective-permute-start | bytes 2359304 | tf_op jit(solution)/shard_map/ppermute | solution.py:29
  92.4 16.7 %all_gather.7.grad = bf16[512,768]{1,0:T(8,128)(2,1)S(1)} all-gather(bf16[128,768]{1,0:T(8,128)(2,1)S(1)} %get-tuple-element.19), channel_id=1, replica_groups={{0,128,256,384},{32,160,288,416},{64,192,320,448},{96,224,352,480},{1,1..., dimensions={0}, use_global_device_ids=true | all-gather | bytes 983040 | tf_op jit(solution)/shard_map/all_gather | solution.py:231
  109.1 6.3 %collective-permute-start.9 = (bf16[512,768]{1,0:T(8,128)(2,1)S(1)}, bf16[512,768]{1,0:T(8,128)(2,1)S(1)}, u32[]{:S(2)}, u32[]{:S(2)}) collective-permute-start(bf16[512,768]{1,0:T(8,128)(2,1)S(1)} %all_gather.7.grad), channel_id=1, source_target_pairs={{0,32},{32,0},{64,96},{96,64},{128,160},{160,128},{192,224},{224,1... | collective-permute-start | bytes 2359304 | tf_op jit(solution)/shard_map/ppermute | solution.py:29
  115.5 1.4 shard_map.65
  117.4 1.4 shard_map.66
  118.8 4.7 %collective-permute-start.10 = (bf16[256,768]{1,0:T(8,128)(2,1)S(1)}, bf16[256,768]{1,0:T(8,128)(2,1)S(1)}, u32[]{:S(2)}, u32[]{:S(2)}) collective-permute-start(bf16[256,768]{1,0:T(8,128)(2,1)S(1)} %get-tuple-element.17), channel_id=1, source_target_pairs={{0,2},{1,3},{2,0},{3,1},{4,6},{5,7},{6,4},{7,5},{8,10},{9,11},{10,... | collective-permute-start | bytes 1179656 | tf_op jit(solution)/shard_map/ppermute | solution.py:29
  123.5 9.0 %collective-permute-done.10 = bf16[256,768]{1,0:T(8,128)(2,1)S(1)} collective-permute-done((bf16[256,768]{1,0:T(8,128)(2,1)S(1)}, bf16[256,768]{1,0:T(8,128)(2,1)S(1)}, u32[]{:S(2)}, u32[]{:S(2)}) %collective-permute-start.10) | collective-permute-done | bytes 393248 | tf_op jit(solution)/shard_map/ppermute | solution.py:29
  133.4 4.3 %all-to-all-start.1 = ((bf16[4,64,768]{2,1,0:T(8,128)(2,1)}), bf16[4,64,768]{2,1,0:T(8,128)(2,1)}, u32[]{:S(2)}, u32[]{:S(2)}) async-start(bf16[4,64,768]{2,1,0:T(8,128)(2,1)} %bitcast.4), calls=%async_computation.1 | async-start | bytes 786432 | tf_op jit(solution)/shard_map/all_to_all | solution.py:33
  137.7 3.0 %collective-permute-start.12 = (bf16[256,768]{1,0:T(8,128)(2,1)S(1)}, bf16[256,768]{1,0:T(8,128)(2,1)}, u32[]{:S(2)}, u32[]{:S(2)}) collective-permute-start(bf16[256,768]{1,0:T(8,128)(2,1)S(1)} %get-tuple-element.18), channel_id=1, source_target_pairs={{0,1},{1,0},{2,3},{3,2},{4,5},{5,4},{6,7},{7,6},{8,9},{9,8},{10,11... | collective-permute-start | bytes 1179656 | tf_op jit(solution)/shard_map/ppermute | solution.py:29
  140.7 1.8 %multiply_convert_fusion.1 = bf16[64,768]{1,0:T(8,128)(2,1)} fusion(f32[128,768]{1,0:T(8,128)} %get-tuple-element.20, pred[]{:T(512)S(6)} %eq.7), kind=kLoop, calls=%fused_computation.22 | loop fusion | flops 294912 | bytes 491521 | tf_op jit(solution)/shard_map/convert_element_type | solution.py:226
  142.5 1.4 slice.63
  143.9 2.3 %collective-permute-start.5 = (bf16[32,768]{1,0:T(8,128)(2,1)}, bf16[32,768]{1,0:T(8,128)(2,1)}, u32[]{:S(2)}, u32[]{:S(2)}) collective-permute-start(bf16[32,768]{1,0:T(8,128)(2,1)} %slice.63), channel_id=1, source_target_pairs={{0,1},{1,0},{2,3},{3,2},{4,5},{5,4},{6,7},{7,6},{8,9},{9,8},{10,11... | collective-permute-start | bytes 147464 | tf_op jit(solution)/shard_map/ppermute | solution.py:29
  147.0 3.0 %collective-permute-done.5 = bf16[32,768]{1,0:T(8,128)(2,1)} collective-permute-done((bf16[32,768]{1,0:T(8,128)(2,1)}, bf16[32,768]{1,0:T(8,128)(2,1)}, u32[]{:S(2)}, u32[]{:S(2)}) %collective-permute-start.5) | collective-permute-done | bytes 49184 | tf_op jit(solution)/shard_map/ppermute | solution.py:29
  151.5 4.2 %collective-permute-start.13 = (bf16[256,768]{1,0:T(8,128)(2,1)}, bf16[256,768]{1,0:T(8,128)(2,1)S(1)}, u32[]{:S(2)}, u32[]{:S(2)}) collective-permute-start(bf16[256,768]{1,0:T(8,128)(2,1)} %collective-permute-done.12), channel_id=1, source_target_pairs={{0,32},{32,0},{64,96},{96,64},{128,160},{160,128},{192,224},{224,1... | collective-permute-start | bytes 1179656 | tf_op jit(solution)/shard_map/ppermute | solution.py:29
  156.8 8.0 %collective-permute-start.11 = (bf16[32,768]{1,0:T(8,128)(2,1)S(1)}, bf16[32,768]{1,0:T(8,128)(2,1)S(1)}, u32[]{:S(2)}, u32[]{:S(2)}) collective-permute-start(bf16[32,768]{1,0:T(8,128)(2,1)S(1)} %fusion.18), channel_id=1, source_target_pairs={{0,16},{1,17},{2,18},{3,19},{4,20},{5,21},{6,22},{7,23},{8,24},{9,... | collective-permute-start | bytes 147464 | tf_op jit(solution)/shard_map/ppermute | solution.py:29
  164.9 3.5 %multiply_convert_fusion = bf16[768,768]{1,0:T(8,128)(2,1)} fusion(bf16[512,768]{1,0:T(8,128)(2,1)S(1)} %copy-done.9, bf16[512,768]{1,0:T(8,128)(2,1)S(1)} %copy-done.7, bf16[256,768]{1,0:T(8,128)(2,1)S(1)} %collective-permute-done.13, bf16[256,768]{1,0:T(8,128)(2,1)} %collective-permute-done.12, bf16[256,768]{1,0:T(8,128)(2,1)S(1)} %bitcast.21, ...), kind=kOutput, calls=%fused_computation | convolution fusion | flops 1218576384 | bytes 4325376 | tf_op jit(solution)/shard_map/dot_general | solution.py:261
  (49 shorter events, 10.8 us)
Async XLA Ops:
  0.6 35.5 %collective-permute-start.1 = (bf16[768,768]{1,0:T(8,128)(2,1)}, bf16[768,768]{1,0:T(8,128)(2,1)S(1)}, u32[]{:S(2)}, u32[]{:S(2)}) collective-permute-start(bf16[768,768]{1,0:T(8,128)(2,1)} %w0.7), channel_id=1, source_target_pairs={{0,1},{1,0},{2,3},{3,2},{4,5},{5,4},{6,7},{7,6},{8,9},{9,8},{10,11... | collective-permute-start | bytes 3538952 | tf_op jit(solution)/shard_map/ppermute | solution.py:29
  4.6 10.5 %collective-permute-start = (bf16[32,768]{1,0:T(8,128)(2,1)}, bf16[32,768]{1,0:T(8,128)(2,1)S(1)}, u32[]{:S(2)}, u32[]{:S(2)}) collective-permute-start(bf16[32,768]{1,0:T(8,128)(2,1)} %param.3), channel_id=1, source_target_pairs={{0,16},{1,17},{2,18},{3,19},{4,20},{5,21},{6,22},{7,23},{8,24},{9,... | collective-permute-start | bytes 147464 | tf_op jit(solution)/shard_map/ppermute | solution.py:29
  31.7 10.2 %collective-permute-start.2 = (bf16[256,768]{1,0:T(8,128)(2,1)S(1)}, bf16[256,768]{1,0:T(8,128)(2,1)S(1)}, u32[]{:S(2)}, u32[]{:S(2)}) collective-permute-start(bf16[256,768]{1,0:T(8,128)(2,1)S(1)} %all_gather.6.piece.line), channel_id=1, source_target_pairs={{0,2},{1,3},{2,0},{3,1},{4,6},{5,7},{6,4},{7,5},{8,10},{9,11},{10,... | collective-permute-start | bytes 1179656 | tf_op jit(solution)/shard_map/ppermute | solution.py:29
  36.1 1.3 copy-start
  37.4 4.4 %copy-start.1 = (bf16[768,768]{1,0:T(8,128)(2,1)S(1)}, bf16[768,768]{1,0:T(8,128)(2,1)}, u32[]{:S(2)}) copy-start(bf16[768,768]{1,0:T(8,128)(2,1)} %w0.7) | copy-start | bytes 3538948
  41.8 1.4 copy-start.4
  43.3 10.2 %collective-permute-start.3 = (bf16[512,768]{1,0:T(8,128)(2,1)S(1)}, bf16[512,768]{1,0:T(8,128)(2,1)S(1)}, u32[]{:S(2)}, u32[]{:S(2)}) collective-permute-start(bf16[512,768]{1,0:T(8,128)(2,1)S(1)} %get-tuple-element.12), channel_id=1, source_target_pairs={{0,32},{32,0},{64,96},{96,64},{128,160},{160,128},{192,224},{224,1... | collective-permute-start | bytes 2359304 | tf_op jit(solution)/shard_map/ppermute | solution.py:29
  55.0 15.8 %all-to-all-start = ((bf16[4,128,768]{2,1,0:T(8,128)(2,1)}), bf16[4,128,768]{2,1,0:T(8,128)(2,1)S(1)}, u32[]{:S(2)}, u32[]{:S(2)}) async-start(bf16[4,128,768]{2,1,0:T(8,128)(2,1)} %bitcast.2), calls=%async_computation | async-start | bytes 1572864 | tf_op jit(solution)/shard_map/all_to_all | solution.py:33
  58.5 24.6 %collective-permute-start.6 = (bf16[64,768]{1,0:T(8,128)(2,1)}, bf16[64,768]{1,0:T(8,128)(2,1)}, u32[]{:S(2)}, u32[]{:S(2)}) collective-permute-start(bf16[64,768]{1,0:T(8,128)(2,1)} %own.1), channel_id=1, source_target_pairs={{0,64},{32,96},{64,0},{96,32},{128,192},{160,224},{192,128},{224,1... | collective-permute-start | bytes 294920 | tf_op jit(solution)/shard_map/ppermute | solution.py:29
  70.7 16.4 %copy-start.5 = (bf16[256,768]{1,0:T(8,128)(2,1)S(1)}, bf16[256,768]{1,0:T(8,128)(2,1)}, u32[]{:S(2)}) copy-start(bf16[256,768]{1,0:T(8,128)(2,1)} %copy-done.4) | copy-start | bytes 1179652
  71.4 20.0 %collective-permute-start.4 = (bf16[128,768]{1,0:T(8,128)(2,1)S(1)}, bf16[128,768]{1,0:T(8,128)(2,1)S(1)}, u32[]{:S(2)}, u32[]{:S(2)}) collective-permute-start(bf16[128,768]{1,0:T(8,128)(2,1)S(1)} %shard_map.61._), channel_id=1, source_target_pairs={{0,64},{32,96},{64,0},{96,32},{128,192},{160,224},{192,128},{224,1... | collective-permute-start | bytes 589832 | tf_op jit(solution)/shard_map/ppermute | solution.py:29
  83.1 0.9 copy-start.10
  84.9 5.9 %collective-permute-start.7 = (bf16[64,768]{1,0:T(8,128)(2,1)S(1)}, bf16[64,768]{1,0:T(8,128)(2,1)S(1)}, u32[]{:S(2)}, u32[]{:S(2)}) collective-permute-start(bf16[64,768]{1,0:T(8,128)(2,1)S(1)} %get-tuple-element.14), channel_id=1, source_target_pairs={{0,1},{1,0},{2,3},{3,2},{4,5},{5,4},{6,7},{7,6},{8,9},{9,8},{10,11... | collective-permute-start | bytes 294920 | tf_op jit(solution)/shard_map/ppermute | solution.py:29
  87.7 29.1 %copy-start.6 = (bf16[512,768]{1,0:T(8,128)(2,1)}, bf16[512,768]{1,0:T(8,128)(2,1)S(1)}, u32[]{:S(2)}) copy-start(bf16[512,768]{1,0:T(8,128)(2,1)S(1)} %shard_map.64) | copy-start | bytes 2359300
  87.7 27.7 %collective-permute-start.8 = (bf16[512,768]{1,0:T(8,128)(2,1)S(1)}, bf16[512,768]{1,0:T(8,128)(2,1)S(1)}, u32[]{:S(2)}, u32[]{:S(2)}) collective-permute-start(bf16[512,768]{1,0:T(8,128)(2,1)S(1)} %shard_map.64), channel_id=1, source_target_pairs={{0,1},{1,0},{2,3},{3,2},{4,5},{5,4},{6,7},{7,6},{8,9},{9,8},{10,11... | collective-permute-start | bytes 2359304 | tf_op jit(solution)/shard_map/ppermute | solution.py:29
  109.1 8.2 %collective-permute-start.9 = (bf16[512,768]{1,0:T(8,128)(2,1)S(1)}, bf16[512,768]{1,0:T(8,128)(2,1)S(1)}, u32[]{:S(2)}, u32[]{:S(2)}) collective-permute-start(bf16[512,768]{1,0:T(8,128)(2,1)S(1)} %all_gather.7.grad), channel_id=1, source_target_pairs={{0,32},{32,0},{64,96},{96,64},{128,160},{160,128},{192,224},{224,1... | collective-permute-start | bytes 2359304 | tf_op jit(solution)/shard_map/ppermute | solution.py:29
  115.5 1.4 copy-start.8
  117.4 1.4 copy-start.2
  118.8 13.7 %collective-permute-start.10 = (bf16[256,768]{1,0:T(8,128)(2,1)S(1)}, bf16[256,768]{1,0:T(8,128)(2,1)S(1)}, u32[]{:S(2)}, u32[]{:S(2)}) collective-permute-start(bf16[256,768]{1,0:T(8,128)(2,1)S(1)} %get-tuple-element.17), channel_id=1, source_target_pairs={{0,2},{1,3},{2,0},{3,1},{4,6},{5,7},{6,4},{7,5},{8,10},{9,11},{10,... | collective-permute-start | bytes 1179656 | tf_op jit(solution)/shard_map/ppermute | solution.py:29
  133.4 18.1 %copy-start.3 = (bf16[512,768]{1,0:T(8,128)(2,1)S(1)}, bf16[512,768]{1,0:T(8,128)(2,1)}, u32[]{:S(2)}) copy-start(bf16[512,768]{1,0:T(8,128)(2,1)} %copy-done.2) | copy-start | bytes 2359300
  133.4 22.3 %all-to-all-start.1 = ((bf16[4,64,768]{2,1,0:T(8,128)(2,1)}), bf16[4,64,768]{2,1,0:T(8,128)(2,1)}, u32[]{:S(2)}, u32[]{:S(2)}) async-start(bf16[4,64,768]{2,1,0:T(8,128)(2,1)} %bitcast.4), calls=%async_computation.1 | async-start | bytes 786432 | tf_op jit(solution)/shard_map/all_to_all | solution.py:33
  137.7 13.8 %collective-permute-start.12 = (bf16[256,768]{1,0:T(8,128)(2,1)S(1)}, bf16[256,768]{1,0:T(8,128)(2,1)}, u32[]{:S(2)}, u32[]{:S(2)}) collective-permute-start(bf16[256,768]{1,0:T(8,128)(2,1)S(1)} %get-tuple-element.18), channel_id=1, source_target_pairs={{0,1},{1,0},{2,3},{3,2},{4,5},{5,4},{6,7},{7,6},{8,9},{9,8},{10,11... | collective-permute-start | bytes 1179656 | tf_op jit(solution)/shard_map/ppermute | solution.py:29
  140.7 24.1 %copy-start.7 = (bf16[512,768]{1,0:T(8,128)(2,1)S(1)}, bf16[512,768]{1,0:T(8,128)(2,1)}, u32[]{:S(2)}) copy-start(bf16[512,768]{1,0:T(8,128)(2,1)} %copy-done.6) | copy-start | bytes 2359300
  140.7 24.1 %copy-start.9 = (bf16[512,768]{1,0:T(8,128)(2,1)S(1)}, bf16[512,768]{1,0:T(8,128)(2,1)}, u32[]{:S(2)}) copy-start(bf16[512,768]{1,0:T(8,128)(2,1)} %copy-done.8) | copy-start | bytes 2359300
  143.9 6.0 %collective-permute-start.5 = (bf16[32,768]{1,0:T(8,128)(2,1)}, bf16[32,768]{1,0:T(8,128)(2,1)}, u32[]{:S(2)}, u32[]{:S(2)}) collective-permute-start(bf16[32,768]{1,0:T(8,128)(2,1)} %slice.63), channel_id=1, source_target_pairs={{0,1},{1,0},{2,3},{3,2},{4,5},{5,4},{6,7},{7,6},{8,9},{9,8},{10,11... | collective-permute-start | bytes 147464 | tf_op jit(solution)/shard_map/ppermute | solution.py:29
  147.0 17.8 %copy-start.11 = (bf16[8,1,32,768]{3,2,1,0:T(8,128)(2,1)S(1)}, bf16[8,1,32,768]{3,2,1,0:T(8,128)(2,1)}, u32[]{:S(2)}) copy-start(bf16[8,1,32,768]{3,2,1,0:T(8,128)(2,1)} %slice.71) | copy-start | bytes 1179652
  151.5 13.3 %collective-permute-start.13 = (bf16[256,768]{1,0:T(8,128)(2,1)}, bf16[256,768]{1,0:T(8,128)(2,1)S(1)}, u32[]{:S(2)}, u32[]{:S(2)}) collective-permute-start(bf16[256,768]{1,0:T(8,128)(2,1)} %collective-permute-done.12), channel_id=1, source_target_pairs={{0,32},{32,0},{64,96},{96,64},{128,160},{160,128},{192,224},{224,1... | collective-permute-start | bytes 1179656 | tf_op jit(solution)/shard_map/ppermute | solution.py:29
  156.8 11.5 %collective-permute-start.11 = (bf16[32,768]{1,0:T(8,128)(2,1)S(1)}, bf16[32,768]{1,0:T(8,128)(2,1)S(1)}, u32[]{:S(2)}, u32[]{:S(2)}) collective-permute-start(bf16[32,768]{1,0:T(8,128)(2,1)S(1)} %fusion.18), channel_id=1, source_target_pairs={{0,16},{1,17},{2,18},{3,19},{4,20},{5,21},{6,22},{7,23},{8,24},{9,... | collective-permute-start | bytes 147464 | tf_op jit(solution)/shard_map/ppermute | solution.py:29

commit v10 on v9

--- a/solution.py
+++ b/solution.py
@@ -44,27 +44,28 @@
     return (z & 3) * 2 + ((z >> 2) ^ (me_col >> 4))
 
 
+def gather_place(z, x, me_col):
+    return (z & 3) * 4 + x * 2 + ((z >> 2) ^ (me_col >> 4))
+
+
 def own_first(me):
     return ((me[0] ^ (me[1] >> 1)) & 1) == 0
 
 
-def products(me, piece, weights, held, out):
+def products(me, line, x, weights, held, out):
     part = held.shape[0] // 8
     for z in range(8):
-        src = pl.multiple_of(line_place(z, me[1]) * part, part)
-        held[pl.ds(z * part, part), :] = piece[pl.ds(src, part), :]
+        src = pl.multiple_of(gather_place(z, x, me[1]) * part, part)
+        held[pl.ds(z * part, part), :] = line[pl.ds(src, part), :]
     for block, w in enumerate(weights):
         value = jnp.dot(held[...], w[...], preferred_element_type=F32)
         for z in range(8):
             out[pl.ds((z * 2 + block) * part, part), :] = value[z * part : (z + 1) * part]
 
 
-def early_kernel(me, piece, w0, w1, out, held):
-    products(me, piece, (w0, w1), held, out)
-
-
-def send_kernel(me, early, piece, w0, w1, late, send, held):
-    products(me, piece, (w0, w1), held, late)
+def up_kernel(me, line, w0, w1, early, late, send, held):
+    products(me, line, 0, (w0, w1), held, early)
+    products(me, line, 1, (w0, w1), held, late)
 
     @pl.when(own_first(me))
     def _():
@@ -109,15 +110,15 @@
         out[(2 * z + 1) * part : (2 * z + 2) * part] = got[z * part : (z + 1) * part]
 
 
-def order_kernel(me, line, across, _, out):
-    half = line.shape[0]
+def order_kernel(me, line, _, out):
+    half = line.shape[0] // 2
     part = half // 8
     swapped = (me[0] ^ (me[1] >> 1)) & 1
-    for s, piece in enumerate((line, across)):
+    for s in range(2):
         for z in range(8):
-            src = pl.multiple_of(line_place(z, me[1]) * part, part)
+            src = pl.multiple_of(gather_place(z, s, me[1]) * part, part)
             to = pl.multiple_of((s ^ swapped) * half + z * part, part)
-            out[pl.ds(to, part), :] = piece[pl.ds(src, part), :]
+            out[pl.ds(to, part), :] = line[pl.ds(src, part), :]
 
 
 def back(me, grad, weights, held):
@@ -186,21 +187,16 @@
     tokens = part * COLS
     flops = tokens * depth * width
 
-    pair = jnp.concatenate([acts, swap(acts, "col", 16)])
+    pair = jnp.concatenate([acts] + [swap(acts, "col", mask) for mask in (16, 2, 18)])
     partner = swap(weight, "col", 1)
     line = lax.all_gather(pair, "col", axis=0, tiled=True, axis_index_groups=Z_GROUPS)
-    across = swap(line, "col", 2)
 
     size = tokens // 2
     held = [pltpu.VMEM((tokens // 4, depth), BF16)]
-    (early,) = call(
-        early_kernel, [shape(size, width, F32)], held, flops, me, line, weight, partner
-    )
-
-    late, send = call(
-        send_kernel,
-        [shape(size, width, F32), shape(size, width, BF16)],
-        held, flops, me, early, across, weight, partner,
+    early, late, send = call(
+        up_kernel,
+        [shape(size, width, F32)] * 2 + [shape(size, width, BF16)],
+        held, 2 * flops, me, line, weight, partner,
     )
 
     (mine,) = call(
@@ -232,7 +228,7 @@
     g1 = swap(g0, "row", 1)
 
     size = tokens // 2
-    (near,) = call(order_kernel, [shape(size, depth, BF16)], [], 0, me, line, across, sent)
+    (near,) = call(order_kernel, [shape(size, depth, BF16)], [], 0, me, line, sent)
     far = swap(near, "col", 1)
 
     size = tokens // 4

time: 170 us -> 185 us (1.088)
  waiting for transfers between devices: 19.1 us -> 32 us
  blocking collectives: 32.5 us -> 35.5 us
    ppermute x14 -> x15, waiting for transfers between devices: 19.1 us -> 32 us  [swap(): return lax.ppermute(value, axis, [(i, i ^ mask) for i in range(size)])]
    all_gather x1, blocking collectives: 16.7 us -> 19 us  [shards(): lax.all_gather(grad, 'row', axis=0, tiled=True, axis_index_groups=Y_GROUPS)]
    all_to_all x2, starting transfers between devices: 7.81 us -> 9.99 us  [spread(): lax.all_to_all(value, axis, split_axis=0, concat_axis=0, axis_index_group...]
    pallas_call x9 -> x8, Pallas kernels: 9.79 us -> 8.75 us  [call(): pl.pallas_call(kernel, out_shape=outs, in_specs=[pl.BlockSpec(memory_spac...]
    ppermute x14 -> x15, starting transfers between devices: 83.1 us -> 82.1 us  [swap(): return lax.ppermute(value, axis, [(i, i ^ mask) for i in range(size)])]
  transfers between devices with their start and end apart: 16 -> 17, of which waited for: 6 -> 4; matrix products, arithmetic and copies ran while one was open for 7% -> 6% of each run, Pallas kernels for 3% -> 2%
where the time goes in v10:
time: 185 us; the launch traced here: 184 us
  starting transfers between devices  92.1 us (50%)
  blocking collectives  35.5 us (19%)
  waiting for transfers between devices  32 us (17%)
  Pallas kernels  8.75 us (5%)
  other arithmetic  7.01 us (4%)
  local copies, waits for them, and re-layouts  4.13 us (2%)
  matrix products  3.46 us (2%)
    ppermute x15, starting transfers between devices, swap(): return lax.ppermute(value, axis, [(i, i ^ mask) for i in range(size)])  82.1 us
    ppermute x15, waiting for transfers between devices, swap(): return lax.ppermute(value, axis, [(i, i ^ mask) for i in range(size)])  32 us
    all_gather x1, blocking collectives, shards(): lax.all_gather(grad, 'row', axis=0, tiled=True, axis_index_groups=Y_GROUPS)  19 us
    all_gather x1, blocking collectives, shards(): lax.all_gather(pair, 'col', axis=0, tiled=True, axis_index_groups=Z_GROUPS)  16.5 us
    all_to_all x2, starting transfers between devices, spread(): lax.all_to_all(value, axis, split_axis=0, concat_axis=0, axis_index_group...  9.99 us
    pallas_call x8, Pallas kernels, call(): pl.pallas_call(kernel, out_shape=outs, in_specs=[pl.BlockSpec(memory_spac...  8.75 us
  transfers between devices with their start and end apart: 17, of which 4 were waited for; matrix products, arithmetic and copies ran while one was open for 6% of the time, Pallas kernels for 2%

profile of v10, /device:TPU:1, one launch (start us, length us, event | category | flops | bytes accessed | tf_op | source)
XLA Modules:
  0.0 184.0 jit_solution(7271929535470775402)
XLA Ops:
  0.6 4.0 %collective-permute-start.3 = (bf16[768,768]{1,0:T(8,128)(2,1)}, bf16[768,768]{1,0:T(8,128)(2,1)S(1)}, u32[]{:S(2)}, u32[]{:S(2)}) collective-permute-start(bf16[768,768]{1,0:T(8,128)(2,1)} %w0.5), channel_id=1, source_target_pairs={{0,1},{1,0},{2,3},{3,2},{4,5},{5,4},{6,7},{7,6},{8,9},{9,8},{10,11... | collective-permute-start | bytes 3538952 | tf_op jit(solution)/shard_map/ppermute | solution.py:29
  4.6 4.4 %collective-permute-start.1 = (bf16[32,768]{1,0:T(8,128)(2,1)}, bf16[32,768]{1,0:T(8,128)(2,1)S(1)}, u32[]{:S(2)}, u32[]{:S(2)}) collective-permute-start(bf16[32,768]{1,0:T(8,128)(2,1)} %param.3), channel_id=1, source_target_pairs={{0,2},{1,3},{2,0},{3,1},{4,6},{5,7},{6,4},{7,5},{8,10},{9,11},{10,... | collective-permute-start | bytes 147464 | tf_op jit(solution)/shard_map/ppermute | solution.py:29
  9.0 8.8 %collective-permute-start = (bf16[32,768]{1,0:T(8,128)(2,1)}, bf16[32,768]{1,0:T(8,128)(2,1)S(1)}, u32[]{:S(2)}, u32[]{:S(2)}) collective-permute-start(bf16[32,768]{1,0:T(8,128)(2,1)} %param.3), channel_id=1, source_target_pairs={{0,16},{1,17},{2,18},{3,19},{4,20},{5,21},{6,22},{7,23},{8,24},{9,... | collective-permute-start | bytes 147464 | tf_op jit(solution)/shard_map/ppermute | solution.py:29
  17.8 2.2 %collective-permute-start.2 = (bf16[32,768]{1,0:T(8,128)(2,1)}, bf16[32,768]{1,0:T(8,128)(2,1)S(1)}, u32[]{:S(2)}, u32[]{:S(2)}) collective-permute-start(bf16[32,768]{1,0:T(8,128)(2,1)} %param.3), channel_id=1, source_target_pairs={{0,18},{1,19},{2,16},{3,17},{4,22},{5,23},{6,20},{7,21},{8,26},{9,... | collective-permute-start | bytes 147464 | tf_op jit(solution)/shard_map/ppermute | solution.py:29
  20.0 14.4 %collective-permute-done.1 = bf16[32,768]{1,0:T(8,128)(2,1)S(1)} collective-permute-done((bf16[32,768]{1,0:T(8,128)(2,1)}, bf16[32,768]{1,0:T(8,128)(2,1)S(1)}, u32[]{:S(2)}, u32[]{:S(2)}) %collective-permute-start.1) | collective-permute-done | bytes 49184 | tf_op jit(solution)/shard_map/ppermute | solution.py:29
  35.2 16.5 %all_gather.6.line = bf16[512,768]{1,0:T(8,128)(2,1)S(1)} all-gather(bf16[128,768]{1,0:T(8,128)(2,1)S(1)} %pad_maximum_fusion), channel_id=1, replica_groups={{0,4,8,12},{1,5,9,13},{2,6,10,14},{3,7,11,15},{16,20,24,28},{17,21,25,2..., dimensions={0}, use_global_device_ids=true | all-gather | bytes 983040 | tf_op jit(solution)/shard_map/all_gather | solution.py:192
  51.7 1.3 copy-done
  53.0 2.0 %shard_map.58 = (f32[512,768]{1,0:T(8,128)S(1)}, f32[512,768]{1,0:T(8,128)S(1)}, bf16[512,768]{1,0:T(8,128)(2,1)S(1)}) custom-call(s32[2]{0:T(128)S(1)} %pad_add_fusion.me, bf16[512,768]{1,0:T(8,128)(2,1)S(1)} %all_gather.6.line, bf16[768,768]{1,0:T(8,128)(2,1)S(1)} %copy-done, bf16[768,768]{1,0:T(8,128)(2,1)S(1)} %collective-permute-done.3.w1), custom_call_target="tpu_custom_call" | custom-call | flops 1207959552 | bytes 3145728 | tf_op jit(solution)/shard_map/pallas_call | solution.py:163
  55.0 7.9 %collective-permute-start.4 = (bf16[512,768]{1,0:T(8,128)(2,1)S(1)}, bf16[512,768]{1,0:T(8,128)(2,1)S(1)}, u32[]{:S(2)}, u32[]{:S(2)}) collective-permute-start(bf16[512,768]{1,0:T(8,128)(2,1)S(1)} %get-tuple-element.14), channel_id=1, source_target_pairs={{0,32},{32,0},{64,96},{96,64},{128,160},{160,128},{192,224},{224,1... | collective-permute-start | bytes 2359304 | tf_op jit(solution)/shard_map/ppermute | solution.py:29
  63.0 1.9 %collective-permute-done.4.got = bf16[512,768]{1,0:T(8,128)(2,1)S(1)} collective-permute-done((bf16[512,768]{1,0:T(8,128)(2,1)S(1)}, bf16[512,768]{1,0:T(8,128)(2,1)S(1)}, u32[]{:S(2)}, u32[]{:S(2)}) %collective-permute-start.4) | collective-permute-done | bytes 786464 | tf_op jit(solution)/shard_map/ppermute | solution.py:29
  64.9 1.6 shard_map.59
  66.4 4.3 %all-to-all-start = ((bf16[4,128,768]{2,1,0:T(8,128)(2,1)}), bf16[4,128,768]{2,1,0:T(8,128)(2,1)S(1)}, u32[]{:S(2)}, u32[]{:S(2)}) async-start(bf16[4,128,768]{2,1,0:T(8,128)(2,1)} %bitcast.2), calls=%async_computation | async-start | bytes 1572864 | tf_op jit(solution)/shard_map/all_to_all | solution.py:33
  70.8 12.4 %collective-permute-start.7 = (bf16[64,768]{1,0:T(8,128)(2,1)S(1)}, bf16[64,768]{1,0:T(8,128)(2,1)S(1)}, u32[]{:S(2)}, u32[]{:S(2)}) collective-permute-start(bf16[64,768]{1,0:T(8,128)(2,1)S(1)} %copy-done.4), channel_id=1, source_target_pairs={{0,64},{32,96},{64,0},{96,32},{128,192},{160,224},{192,128},{224,1... | collective-permute-start | bytes 294920 | tf_op jit(solution)/shard_map/ppermute | solution.py:29
  83.8 11.7 %collective-permute-start.5 = (bf16[128,768]{1,0:T(8,128)(2,1)S(1)}, bf16[128,768]{1,0:T(8,128)(2,1)S(1)}, u32[]{:S(2)}, u32[]{:S(2)}) collective-permute-start(bf16[128,768]{1,0:T(8,128)(2,1)S(1)} %shard_map.60._), channel_id=1, source_target_pairs={{0,64},{32,96},{64,0},{96,32},{128,192},{160,224},{192,128},{224,1... | collective-permute-start | bytes 589832 | tf_op jit(solution)/shard_map/ppermute | solution.py:29
  96.1 1.9 %collective-permute-start.8 = (bf16[64,768]{1,0:T(8,128)(2,1)S(1)}, bf16[64,768]{1,0:T(8,128)(2,1)S(1)}, u32[]{:S(2)}, u32[]{:S(2)}) collective-permute-start(bf16[64,768]{1,0:T(8,128)(2,1)S(1)} %get-tuple-element.16), channel_id=1, source_target_pairs={{0,1},{1,0},{2,3},{3,2},{4,5},{5,4},{6,7},{7,6},{8,9},{9,8},{10,11... | collective-permute-start | bytes 294920 | tf_op jit(solution)/shard_map/ppermute | solution.py:29
  98.7 3.5 %collective-permute-start.9 = (bf16[512,768]{1,0:T(8,128)(2,1)S(1)}, bf16[512,768]{1,0:T(8,128)(2,1)S(1)}, u32[]{:S(2)}, u32[]{:S(2)}) collective-permute-start(bf16[512,768]{1,0:T(8,128)(2,1)S(1)} %shard_map.63), channel_id=1, source_target_pairs={{0,1},{1,0},{2,3},{3,2},{4,5},{5,4},{6,7},{7,6},{8,9},{9,8},{10,11... | collective-permute-start | bytes 2359304 | tf_op jit(solution)/shard_map/ppermute | solution.py:29
  102.8 0.9 fusion.15
  103.7 19.0 %all_gather.7.grad = bf16[512,768]{1,0:T(8,128)(2,1)S(1)} all-gather(bf16[128,768]{1,0:T(8,128)(2,1)S(1)} %get-tuple-element.21), channel_id=1, replica_groups={{0,128,256,384},{32,160,288,416},{64,192,320,448},{96,224,352,480},{1,1..., dimensions={0}, use_global_device_ids=true | all-gather | bytes 983040 | tf_op jit(solution)/shard_map/all_gather | solution.py:227
  122.7 6.8 %collective-permute-start.10 = (bf16[512,768]{1,0:T(8,128)(2,1)S(1)}, bf16[512,768]{1,0:T(8,128)(2,1)S(1)}, u32[]{:S(2)}, u32[]{:S(2)}) collective-permute-start(bf16[512,768]{1,0:T(8,128)(2,1)S(1)} %all_gather.7.grad), channel_id=1, source_target_pairs={{0,32},{32,0},{64,96},{96,64},{128,160},{160,128},{192,224},{224,1... | collective-permute-start | bytes 2359304 | tf_op jit(solution)/shard_map/ppermute | solution.py:29
  129.6 1.4 shard_map.64
  131.7 1.4 shard_map.65
  133.2 2.5 %collective-permute-start.11 = (bf16[256,768]{1,0:T(8,128)(2,1)S(1)}, bf16[256,768]{1,0:T(8,128)(2,1)S(1)}, u32[]{:S(2)}, u32[]{:S(2)}) collective-permute-start(bf16[256,768]{1,0:T(8,128)(2,1)S(1)} %get-tuple-element.19), channel_id=1, source_target_pairs={{0,2},{1,3},{2,0},{3,1},{4,6},{5,7},{6,4},{7,5},{8,10},{9,11},{10,... | collective-permute-start | bytes 1179656 | tf_op jit(solution)/shard_map/ppermute | solution.py:29
  135.7 11.7 %collective-permute-done.11 = bf16[256,768]{1,0:T(8,128)(2,1)S(1)} collective-permute-done((bf16[256,768]{1,0:T(8,128)(2,1)S(1)}, bf16[256,768]{1,0:T(8,128)(2,1)S(1)}, u32[]{:S(2)}, u32[]{:S(2)}) %collective-permute-start.11) | collective-permute-done | bytes 393248 | tf_op jit(solution)/shard_map/ppermute | solution.py:29
  148.2 5.7 %all-to-all-start.1 = ((bf16[4,64,768]{2,1,0:T(8,128)(2,1)}), bf16[4,64,768]{2,1,0:T(8,128)(2,1)}, u32[]{:S(2)}, u32[]{:S(2)}) async-start(bf16[4,64,768]{2,1,0:T(8,128)(2,1)} %bitcast.4), calls=%async_computation.1 | async-start | bytes 786432 | tf_op jit(solution)/shard_map/all_to_all | solution.py:33
  153.9 1.9 %collective-permute-start.13 = (bf16[256,768]{1,0:T(8,128)(2,1)S(1)}, bf16[256,768]{1,0:T(8,128)(2,1)}, u32[]{:S(2)}, u32[]{:S(2)}) collective-permute-start(bf16[256,768]{1,0:T(8,128)(2,1)S(1)} %copy-done.6), channel_id=1, source_target_pairs={{0,1},{1,0},{2,3},{3,2},{4,5},{5,4},{6,7},{7,6},{8,9},{9,8},{10,11... | collective-permute-start | bytes 1179656 | tf_op jit(solution)/shard_map/ppermute | solution.py:29
  155.8 1.1 multiply_convert_fusion.1
  158.2 3.4 %collective-permute-start.6 = (bf16[32,768]{1,0:T(8,128)(2,1)}, bf16[32,768]{1,0:T(8,128)(2,1)}, u32[]{:S(2)}, u32[]{:S(2)}) collective-permute-start(bf16[32,768]{1,0:T(8,128)(2,1)} %slice.63), channel_id=1, source_target_pairs={{0,1},{1,0},{2,3},{3,2},{4,5},{5,4},{6,7},{7,6},{8,9},{9,8},{10,11... | collective-permute-start | bytes 147464 | tf_op jit(solution)/shard_map/ppermute | solution.py:29
  162.4 4.0 %collective-permute-done.6 = bf16[32,768]{1,0:T(8,128)(2,1)} collective-permute-done((bf16[32,768]{1,0:T(8,128)(2,1)}, bf16[32,768]{1,0:T(8,128)(2,1)}, u32[]{:S(2)}, u32[]{:S(2)}) %collective-permute-start.6) | collective-permute-done | bytes 49184 | tf_op jit(solution)/shard_map/ppermute | solution.py:29
  167.9 4.0 %collective-permute-start.14 = (bf16[256,768]{1,0:T(8,128)(2,1)}, bf16[256,768]{1,0:T(8,128)(2,1)S(1)}, u32[]{:S(2)}, u32[]{:S(2)}) collective-permute-start(bf16[256,768]{1,0:T(8,128)(2,1)} %collective-permute-done.13), channel_id=1, source_target_pairs={{0,32},{32,0},{64,96},{96,64},{128,160},{160,128},{192,224},{224,1... | collective-permute-start | bytes 1179656 | tf_op jit(solution)/shard_map/ppermute | solution.py:29
  171.9 1.1 convert_add_fusion.1
  173.0 6.8 %collective-permute-start.12 = (bf16[32,768]{1,0:T(8,128)(2,1)S(1)}, bf16[32,768]{1,0:T(8,128)(2,1)S(1)}, u32[]{:S(2)}, u32[]{:S(2)}) collective-permute-start(bf16[32,768]{1,0:T(8,128)(2,1)S(1)} %fusion.18), channel_id=1, source_target_pairs={{0,16},{1,17},{2,18},{3,19},{4,20},{5,21},{6,22},{7,23},{8,24},{9,... | collective-permute-start | bytes 147464 | tf_op jit(solution)/shard_map/ppermute | solution.py:29
  179.9 3.5 %multiply_convert_fusion = bf16[768,768]{1,0:T(8,128)(2,1)} fusion(bf16[512,768]{1,0:T(8,128)(2,1)S(1)} %copy-done.3, bf16[512,768]{1,0:T(8,128)(2,1)S(1)} %shard_map.63, bf16[256,768]{1,0:T(8,128)(2,1)S(1)} %collective-permute-done.14, bf16[256,768]{1,0:T(8,128)(2,1)} %collective-permute-done.13, bf16[256,768]{1,0:T(8,128)(2,1)S(1)} %bitcast.21, ...), kind=kOutput, calls=%fused_computation | convolution fusion | flops 1218576384 | bytes 4325376 | tf_op jit(solution)/shard_map/dot_general | solution.py:257
  (44 shorter events, 9.1 us)
Async XLA Ops:
  0.6 51.1 %collective-permute-start.3 = (bf16[768,768]{1,0:T(8,128)(2,1)}, bf16[768,768]{1,0:T(8,128)(2,1)S(1)}, u32[]{:S(2)}, u32[]{:S(2)}) collective-permute-start(bf16[768,768]{1,0:T(8,128)(2,1)} %w0.5), channel_id=1, source_target_pairs={{0,1},{1,0},{2,3},{3,2},{4,5},{5,4},{6,7},{7,6},{8,9},{9,8},{10,11... | collective-permute-start | bytes 3538952 | tf_op jit(solution)/shard_map/ppermute | solution.py:29
  4.6 29.8 %collective-permute-start.1 = (bf16[32,768]{1,0:T(8,128)(2,1)}, bf16[32,768]{1,0:T(8,128)(2,1)S(1)}, u32[]{:S(2)}, u32[]{:S(2)}) collective-permute-start(bf16[32,768]{1,0:T(8,128)(2,1)} %param.3), channel_id=1, source_target_pairs={{0,2},{1,3},{2,0},{3,1},{4,6},{5,7},{6,4},{7,5},{8,10},{9,11},{10,... | collective-permute-start | bytes 147464 | tf_op jit(solution)/shard_map/ppermute | solution.py:29
  9.0 25.5 %collective-permute-start = (bf16[32,768]{1,0:T(8,128)(2,1)}, bf16[32,768]{1,0:T(8,128)(2,1)S(1)}, u32[]{:S(2)}, u32[]{:S(2)}) collective-permute-start(bf16[32,768]{1,0:T(8,128)(2,1)} %param.3), channel_id=1, source_target_pairs={{0,16},{1,17},{2,18},{3,19},{4,20},{5,21},{6,22},{7,23},{8,24},{9,... | collective-permute-start | bytes 147464 | tf_op jit(solution)/shard_map/ppermute | solution.py:29
  17.8 16.6 %collective-permute-start.2 = (bf16[32,768]{1,0:T(8,128)(2,1)}, bf16[32,768]{1,0:T(8,128)(2,1)S(1)}, u32[]{:S(2)}, u32[]{:S(2)}) collective-permute-start(bf16[32,768]{1,0:T(8,128)(2,1)} %param.3), channel_id=1, source_target_pairs={{0,18},{1,19},{2,16},{3,17},{4,22},{5,23},{6,20},{7,21},{8,26},{9,... | collective-permute-start | bytes 147464 | tf_op jit(solution)/shard_map/ppermute | solution.py:29
  51.7 1.3 copy-start
  55.0 9.8 %collective-permute-start.4 = (bf16[512,768]{1,0:T(8,128)(2,1)S(1)}, bf16[512,768]{1,0:T(8,128)(2,1)S(1)}, u32[]{:S(2)}, u32[]{:S(2)}) collective-permute-start(bf16[512,768]{1,0:T(8,128)(2,1)S(1)} %get-tuple-element.14), channel_id=1, source_target_pairs={{0,32},{32,0},{64,96},{96,64},{128,160},{160,128},{192,224},{224,1... | collective-permute-start | bytes 2359304 | tf_op jit(solution)/shard_map/ppermute | solution.py:29
  66.4 4.3 %copy-start.4 = (bf16[64,768]{1,0:T(8,128)(2,1)S(1)}, bf16[64,768]{1,0:T(8,128)(2,1)}, u32[]{:S(2)}) copy-start(bf16[64,768]{1,0:T(8,128)(2,1)} %own.1) | copy-start | bytes 294916
  66.4 16.7 %all-to-all-start = ((bf16[4,128,768]{2,1,0:T(8,128)(2,1)}), bf16[4,128,768]{2,1,0:T(8,128)(2,1)S(1)}, u32[]{:S(2)}, u32[]{:S(2)}) async-start(bf16[4,128,768]{2,1,0:T(8,128)(2,1)} %bitcast.2), calls=%async_computation | async-start | bytes 1572864 | tf_op jit(solution)/shard_map/all_to_all | solution.py:33
  70.8 24.8 %collective-permute-start.7 = (bf16[64,768]{1,0:T(8,128)(2,1)S(1)}, bf16[64,768]{1,0:T(8,128)(2,1)S(1)}, u32[]{:S(2)}, u32[]{:S(2)}) collective-permute-start(bf16[64,768]{1,0:T(8,128)(2,1)S(1)} %copy-done.4), channel_id=1, source_target_pairs={{0,64},{32,96},{64,0},{96,32},{128,192},{160,224},{192,128},{224,1... | collective-permute-start | bytes 294920 | tf_op jit(solution)/shard_map/ppermute | solution.py:29
  83.8 18.9 %collective-permute-start.5 = (bf16[128,768]{1,0:T(8,128)(2,1)S(1)}, bf16[128,768]{1,0:T(8,128)(2,1)S(1)}, u32[]{:S(2)}, u32[]{:S(2)}) collective-permute-start(bf16[128,768]{1,0:T(8,128)(2,1)S(1)} %shard_map.60._), channel_id=1, source_target_pairs={{0,64},{32,96},{64,0},{96,32},{128,192},{160,224},{192,128},{224,1... | collective-permute-start | bytes 589832 | tf_op jit(solution)/shard_map/ppermute | solution.py:29
  96.1 6.1 %collective-permute-start.8 = (bf16[64,768]{1,0:T(8,128)(2,1)S(1)}, bf16[64,768]{1,0:T(8,128)(2,1)S(1)}, u32[]{:S(2)}, u32[]{:S(2)}) collective-permute-start(bf16[64,768]{1,0:T(8,128)(2,1)S(1)} %get-tuple-element.16), channel_id=1, source_target_pairs={{0,1},{1,0},{2,3},{3,2},{4,5},{5,4},{6,7},{7,6},{8,9},{9,8},{10,11... | collective-permute-start | bytes 294920 | tf_op jit(solution)/shard_map/ppermute | solution.py:29
  98.7 30.9 %copy-start.1 = (bf16[768,768]{1,0:T(8,128)(2,1)S(1)}, bf16[768,768]{1,0:T(8,128)(2,1)}, u32[]{:S(2)}) copy-start(bf16[768,768]{1,0:T(8,128)(2,1)} %w0.5) | copy-start | bytes 3538948
  98.7 30.9 %collective-permute-start.9 = (bf16[512,768]{1,0:T(8,128)(2,1)S(1)}, bf16[512,768]{1,0:T(8,128)(2,1)S(1)}, u32[]{:S(2)}, u32[]{:S(2)}) collective-permute-start(bf16[512,768]{1,0:T(8,128)(2,1)S(1)} %shard_map.63), channel_id=1, source_target_pairs={{0,1},{1,0},{2,3},{3,2},{4,5},{5,4},{6,7},{7,6},{8,9},{9,8},{10,11... | collective-permute-start | bytes 2359304 | tf_op jit(solution)/shard_map/ppermute | solution.py:29
  122.7 9.0 %collective-permute-start.10 = (bf16[512,768]{1,0:T(8,128)(2,1)S(1)}, bf16[512,768]{1,0:T(8,128)(2,1)S(1)}, u32[]{:S(2)}, u32[]{:S(2)}) collective-permute-start(bf16[512,768]{1,0:T(8,128)(2,1)S(1)} %all_gather.7.grad), channel_id=1, source_target_pairs={{0,32},{32,0},{64,96},{96,64},{128,160},{160,128},{192,224},{224,1... | collective-permute-start | bytes 2359304 | tf_op jit(solution)/shard_map/ppermute | solution.py:29
  129.6 1.4 copy-start.2
  131.0 0.8 copy-start.5
  133.2 20.7 %copy-start.6 = (bf16[256,768]{1,0:T(8,128)(2,1)S(1)}, bf16[256,768]{1,0:T(8,128)(2,1)}, u32[]{:S(2)}) copy-start(bf16[256,768]{1,0:T(8,128)(2,1)} %copy-done.5) | copy-start | bytes 1179652
  133.2 14.2 %collective-permute-start.11 = (bf16[256,768]{1,0:T(8,128)(2,1)S(1)}, bf16[256,768]{1,0:T(8,128)(2,1)S(1)}, u32[]{:S(2)}, u32[]{:S(2)}) collective-permute-start(bf16[256,768]{1,0:T(8,128)(2,1)S(1)} %get-tuple-element.19), channel_id=1, source_target_pairs={{0,2},{1,3},{2,0},{3,1},{4,6},{5,7},{6,4},{7,5},{8,10},{9,11},{10,... | collective-permute-start | bytes 1179656 | tf_op jit(solution)/shard_map/ppermute | solution.py:29
  148.2 23.7 %all-to-all-start.1 = ((bf16[4,64,768]{2,1,0:T(8,128)(2,1)}), bf16[4,64,768]{2,1,0:T(8,128)(2,1)}, u32[]{:S(2)}, u32[]{:S(2)}) async-start(bf16[4,64,768]{2,1,0:T(8,128)(2,1)} %bitcast.4), calls=%async_computation.1 | async-start | bytes 786432 | tf_op jit(solution)/shard_map/all_to_all | solution.py:33
  153.9 14.0 %collective-permute-start.13 = (bf16[256,768]{1,0:T(8,128)(2,1)S(1)}, bf16[256,768]{1,0:T(8,128)(2,1)}, u32[]{:S(2)}, u32[]{:S(2)}) collective-permute-start(bf16[256,768]{1,0:T(8,128)(2,1)S(1)} %copy-done.6), channel_id=1, source_target_pairs={{0,1},{1,0},{2,3},{3,2},{4,5},{5,4},{6,7},{7,6},{8,9},{9,8},{10,11... | collective-permute-start | bytes 1179656 | tf_op jit(solution)/shard_map/ppermute | solution.py:29
  155.8 24.1 %copy-start.3 = (bf16[512,768]{1,0:T(8,128)(2,1)S(1)}, bf16[512,768]{1,0:T(8,128)(2,1)}, u32[]{:S(2)}) copy-start(bf16[512,768]{1,0:T(8,128)(2,1)} %copy-done.2) | copy-start | bytes 2359300
  157.0 0.6 copy-start.8
  158.2 8.2 %collective-permute-start.6 = (bf16[32,768]{1,0:T(8,128)(2,1)}, bf16[32,768]{1,0:T(8,128)(2,1)}, u32[]{:S(2)}, u32[]{:S(2)}) collective-permute-start(bf16[32,768]{1,0:T(8,128)(2,1)} %slice.63), channel_id=1, source_target_pairs={{0,1},{1,0},{2,3},{3,2},{4,5},{5,4},{6,7},{7,6},{8,9},{9,8},{10,11... | collective-permute-start | bytes 147464 | tf_op jit(solution)/shard_map/ppermute | solution.py:29
  162.4 17.5 %copy-start.7 = (bf16[8,1,32,768]{3,2,1,0:T(8,128)(2,1)S(1)}, bf16[8,1,32,768]{3,2,1,0:T(8,128)(2,1)}, u32[]{:S(2)}) copy-start(bf16[8,1,32,768]{3,2,1,0:T(8,128)(2,1)} %slice.71) | copy-start | bytes 1179652
  167.9 11.9 %collective-permute-start.14 = (bf16[256,768]{1,0:T(8,128)(2,1)}, bf16[256,768]{1,0:T(8,128)(2,1)S(1)}, u32[]{:S(2)}, u32[]{:S(2)}) collective-permute-start(bf16[256,768]{1,0:T(8,128)(2,1)} %collective-permute-done.13), channel_id=1, source_target_pairs={{0,32},{32,0},{64,96},{96,64},{128,160},{160,128},{192,224},{224,1... | collective-permute-start | bytes 1179656 | tf_op jit(solution)/shard_map/ppermute | solution.py:29
  173.0 10.3 %collective-permute-start.12 = (bf16[32,768]{1,0:T(8,128)(2,1)S(1)}, bf16[32,768]{1,0:T(8,128)(2,1)S(1)}, u32[]{:S(2)}, u32[]{:S(2)}) collective-permute-start(bf16[32,768]{1,0:T(8,128)(2,1)S(1)} %fusion.18), channel_id=1, source_target_pairs={{0,16},{1,17},{2,18},{3,19},{4,20},{5,21},{6,22},{7,23},{8,24},{9,... | collective-permute-start | bytes 147464 | tf_op jit(solution)/shard_map/ppermute | solution.py:29

commit v11 on v10

--- a/solution.py
+++ b/solution.py
@@ -84,6 +84,10 @@
     @pl.when(jnp.logical_not(own_first(me)))
     def _():
         out[...] = (late[...] + got[...].astype(F32)).astype(BF16)
+
+
+def after_kernel(me, value, _, __, out):
+    out[...] = value[...]
 
 
 def four_kernel(me, got, out):
@@ -187,8 +191,10 @@
     tokens = part * COLS
     flops = tokens * depth * width
 
-    pair = jnp.concatenate([acts] + [swap(acts, "col", mask) for mask in (16, 2, 18)])
-    partner = swap(weight, "col", 1)
+    blocks = [swap(acts, "col", mask) for mask in (16, 2, 18)]
+    pair = jnp.concatenate([acts] + blocks)
+    (ready,) = call(after_kernel, [shape(depth, width, BF16)], [], 0, me, weight, *blocks[1:])
+    partner = swap(ready, "col", 1)
     line = lax.all_gather(pair, "col", axis=0, tiled=True, axis_index_groups=Z_GROUPS)
 
     size = tokens // 2

time: 185 us -> 181 us (0.978)
  waiting for transfers between devices: 32 us -> 19.5 us
  starting transfers between devices: 92.1 us -> 96.3 us
  blocking collectives: 35.5 us -> 39.5 us
    ppermute x15, waiting for transfers between devices: 32 us -> 19.5 us  [swap(): return lax.ppermute(value, axis, [(i, i ^ mask) for i in range(size)])]
    ppermute x15, starting transfers between devices: 82.1 us -> 86.7 us  [swap(): return lax.ppermute(value, axis, [(i, i ^ mask) for i in range(size)])]
    all_gather x1, blocking collectives: 16.5 us -> 19.8 us  [shards(): lax.all_gather(pair, 'col', axis=0, tiled=True, axis_index_groups=Z_GROUPS)]
    pallas_call x8 -> x9, Pallas kernels: 8.75 us -> 9.38 us  [call(): pl.pallas_call(kernel, out_shape=outs, in_specs=[pl.BlockSpec(memory_spac...]
  transfers between devices with their start and end apart: 17 -> 17, of which waited for: 4 -> 6; matrix products, arithmetic and copies ran while one was open for 6% -> 6% of each run, Pallas kernels for 2% -> 2%
where the time goes in v11:
time: 181 us; the launch traced here: 180 us
  starting transfers between devices  96.3 us (53%)
  blocking collectives  39.5 us (22%)
  waiting for transfers between devices  19.5 us (11%)
  Pallas kernels  9.38 us (5%)
  other arithmetic  6.93 us (4%)
  local copies, waits for them, and re-layouts  3.56 us (2%)
  matrix products  3.45 us (2%)
    ppermute x15, starting transfers between devices, swap(): return lax.ppermute(value, axis, [(i, i ^ mask) for i in range(size)])  86.7 us
    all_gather x1, blocking collectives, shards(): lax.all_gather(pair, 'col', axis=0, tiled=True, axis_index_groups=Z_GROUPS)  19.8 us
    all_gather x1, blocking collectives, shards(): lax.all_gather(grad, 'row', axis=0, tiled=True, axis_index_groups=Y_GROUPS)  19.7 us
    ppermute x15, waiting for transfers between devices, swap(): return lax.ppermute(value, axis, [(i, i ^ mask) for i in range(size)])  19.5 us
    all_to_all x2, starting transfers between devices, spread(): lax.all_to_all(value, axis, split_axis=0, concat_axis=0, axis_index_group...  9.64 us
    pallas_call x9, Pallas kernels, call(): pl.pallas_call(kernel, out_shape=outs, in_specs=[pl.BlockSpec(memory_spac...  9.38 us
  transfers between devices with their start and end apart: 17, of which 6 were waited for; matrix products, arithmetic and copies ran while one was open for 6% of the time, Pallas kernels for 2%

profile of v11, /device:TPU:1, one launch (start us, length us, event | category | flops | bytes accessed | tf_op | source)
XLA Modules:
  0.0 179.6 jit_solution(4899396035713077656)
XLA Ops:
  0.6 5.5 %collective-permute-start.1 = (bf16[32,768]{1,0:T(8,128)(2,1)}, bf16[32,768]{1,0:T(8,128)(2,1)S(1)}, u32[]{:S(2)}, u32[]{:S(2)}) collective-permute-start(bf16[32,768]{1,0:T(8,128)(2,1)} %param.3), channel_id=1, source_target_pairs={{0,2},{1,3},{2,0},{3,1},{4,6},{5,7},{6,4},{7,5},{8,10},{9,11},{10,... | collective-permute-start | bytes 147464 | tf_op jit(solution)/shard_map/ppermute | solution.py:29
  6.1 8.8 %collective-permute-start.2 = (bf16[32,768]{1,0:T(8,128)(2,1)}, bf16[32,768]{1,0:T(8,128)(2,1)S(1)}, u32[]{:S(2)}, u32[]{:S(2)}) collective-permute-start(bf16[32,768]{1,0:T(8,128)(2,1)} %param.3), channel_id=1, source_target_pairs={{0,18},{1,19},{2,16},{3,17},{4,22},{5,23},{6,20},{7,21},{8,26},{9,... | collective-permute-start | bytes 147464 | tf_op jit(solution)/shard_map/ppermute | solution.py:29
  15.0 2.5 %collective-permute-done.2.__ = bf16[32,768]{1,0:T(8,128)(2,1)S(1)} collective-permute-done((bf16[32,768]{1,0:T(8,128)(2,1)}, bf16[32,768]{1,0:T(8,128)(2,1)S(1)}, u32[]{:S(2)}, u32[]{:S(2)}) %collective-permute-start.2) | collective-permute-done | bytes 49184 | tf_op jit(solution)/shard_map/ppermute | solution.py:29
  17.5 1.3 copy-done
  19.4 2.2 %collective-permute-start.3 = (bf16[768,768]{1,0:T(8,128)(2,1)S(1)}, bf16[768,768]{1,0:T(8,128)(2,1)S(1)}, u32[]{:S(2)}, u32[]{:S(2)}) collective-permute-start(bf16[768,768]{1,0:T(8,128)(2,1)S(1)} %shard_map.58), channel_id=1, source_target_pairs={{0,1},{1,0},{2,3},{3,2},{4,5},{5,4},{6,7},{7,6},{8,9},{9,8},{10,11... | collective-permute-start | bytes 3538952 | tf_op jit(solution)/shard_map/ppermute | solution.py:29
  21.6 8.8 %collective-permute-start = (bf16[32,768]{1,0:T(8,128)(2,1)S(1)}, bf16[32,768]{1,0:T(8,128)(2,1)S(1)}, u32[]{:S(2)}, u32[]{:S(2)}) collective-permute-start(bf16[32,768]{1,0:T(8,128)(2,1)S(1)} %copy-done.14), channel_id=1, source_target_pairs={{0,16},{1,17},{2,18},{3,19},{4,20},{5,21},{6,22},{7,23},{8,24},{9,... | collective-permute-start | bytes 147464 | tf_op jit(solution)/shard_map/ppermute | solution.py:29
  30.4 1.5 collective-permute-done
  31.9 19.8 %all_gather.6.line = bf16[512,768]{1,0:T(8,128)(2,1)S(1)} all-gather(bf16[128,768]{1,0:T(8,128)(2,1)S(1)} %pad_maximum_fusion), channel_id=1, replica_groups={{0,4,8,12},{1,5,9,13},{2,6,10,14},{3,7,11,15},{16,20,24,28},{17,21,25,2..., dimensions={0}, use_global_device_ids=true | all-gather | bytes 983040 | tf_op jit(solution)/shard_map/all_gather | solution.py:198
  51.7 2.0 %shard_map.59 = (f32[512,768]{1,0:T(8,128)S(1)}, f32[512,768]{1,0:T(8,128)S(1)}, bf16[512,768]{1,0:T(8,128)(2,1)S(1)}) custom-call(s32[2]{0:T(128)S(1)} %pad_add_fusion.me, bf16[512,768]{1,0:T(8,128)(2,1)S(1)} %all_gather.6.line, bf16[768,768]{1,0:T(8,128)(2,1)S(1)} %copy-done.1, bf16[768,768]{1,0:T(8,128)(2,1)S(1)} %collective-permute-done.3.w1), custom_call_target="tpu_custom_call" | custom-call | flops 1207959552 | bytes 3145728 | tf_op jit(solution)/shard_map/pallas_call | solution.py:167
  53.7 7.2 %collective-permute-start.4 = (bf16[512,768]{1,0:T(8,128)(2,1)S(1)}, bf16[512,768]{1,0:T(8,128)(2,1)S(1)}, u32[]{:S(2)}, u32[]{:S(2)}) collective-permute-start(bf16[512,768]{1,0:T(8,128)(2,1)S(1)} %get-tuple-element.14), channel_id=1, source_target_pairs={{0,32},{32,0},{64,96},{96,64},{128,160},{160,128},{192,224},{224,1... | collective-permute-start | bytes 2359304 | tf_op jit(solution)/shard_map/ppermute | solution.py:29
  60.9 1.9 %collective-permute-done.4.got = bf16[512,768]{1,0:T(8,128)(2,1)S(1)} collective-permute-done((bf16[512,768]{1,0:T(8,128)(2,1)S(1)}, bf16[512,768]{1,0:T(8,128)(2,1)S(1)}, u32[]{:S(2)}, u32[]{:S(2)}) %collective-permute-start.4) | collective-permute-done | bytes 786464 | tf_op jit(solution)/shard_map/ppermute | solution.py:29
  62.8 1.6 shard_map.60
  64.4 4.3 %all-to-all-start = ((bf16[4,128,768]{2,1,0:T(8,128)(2,1)}), bf16[4,128,768]{2,1,0:T(8,128)(2,1)S(1)}, u32[]{:S(2)}, u32[]{:S(2)}) async-start(bf16[4,128,768]{2,1,0:T(8,128)(2,1)} %bitcast.2), calls=%async_computation | async-start | bytes 1572864 | tf_op jit(solution)/shard_map/all_to_all | solution.py:33
  68.8 12.6 %collective-permute-start.7 = (bf16[64,768]{1,0:T(8,128)(2,1)S(1)}, bf16[64,768]{1,0:T(8,128)(2,1)S(1)}, u32[]{:S(2)}, u32[]{:S(2)}) collective-permute-start(bf16[64,768]{1,0:T(8,128)(2,1)S(1)} %copy-done.10), channel_id=1, source_target_pairs={{0,64},{32,96},{64,0},{96,32},{128,192},{160,224},{192,128},{224,1... | collective-permute-start | bytes 294920 | tf_op jit(solution)/shard_map/ppermute | solution.py:29
  82.0 11.7 %collective-permute-start.5 = (bf16[128,768]{1,0:T(8,128)(2,1)S(1)}, bf16[128,768]{1,0:T(8,128)(2,1)S(1)}, u32[]{:S(2)}, u32[]{:S(2)}) collective-permute-start(bf16[128,768]{1,0:T(8,128)(2,1)S(1)} %shard_map.61._), channel_id=1, source_target_pairs={{0,64},{32,96},{64,0},{96,32},{128,192},{160,224},{192,128},{224,1... | collective-permute-start | bytes 589832 | tf_op jit(solution)/shard_map/ppermute | solution.py:29
  94.3 3.1 %collective-permute-start.8 = (bf16[64,768]{1,0:T(8,128)(2,1)S(1)}, bf16[64,768]{1,0:T(8,128)(2,1)S(1)}, u32[]{:S(2)}, u32[]{:S(2)}) collective-permute-start(bf16[64,768]{1,0:T(8,128)(2,1)S(1)} %get-tuple-element.16), channel_id=1, source_target_pairs={{0,1},{1,0},{2,3},{3,2},{4,5},{5,4},{6,7},{7,6},{8,9},{9,8},{10,11... | collective-permute-start | bytes 294920 | tf_op jit(solution)/shard_map/ppermute | solution.py:29
  98.0 2.2 %collective-permute-start.9 = (bf16[512,768]{1,0:T(8,128)(2,1)S(1)}, bf16[512,768]{1,0:T(8,128)(2,1)S(1)}, u32[]{:S(2)}, u32[]{:S(2)}) collective-permute-start(bf16[512,768]{1,0:T(8,128)(2,1)S(1)} %shard_map.64), channel_id=1, source_target_pairs={{0,1},{1,0},{2,3},{3,2},{4,5},{5,4},{6,7},{7,6},{8,9},{9,8},{10,11... | collective-permute-start | bytes 2359304 | tf_op jit(solution)/shard_map/ppermute | solution.py:29
  101.8 19.7 %all_gather.7.grad = bf16[512,768]{1,0:T(8,128)(2,1)S(1)} all-gather(bf16[128,768]{1,0:T(8,128)(2,1)S(1)} %get-tuple-element.21), channel_id=1, replica_groups={{0,128,256,384},{32,160,288,416},{64,192,320,448},{96,224,352,480},{1,1..., dimensions={0}, use_global_device_ids=true | all-gather | bytes 983040 | tf_op jit(solution)/shard_map/all_gather | solution.py:233
  121.5 5.5 %collective-permute-start.10 = (bf16[512,768]{1,0:T(8,128)(2,1)S(1)}, bf16[512,768]{1,0:T(8,128)(2,1)S(1)}, u32[]{:S(2)}, u32[]{:S(2)}) collective-permute-start(bf16[512,768]{1,0:T(8,128)(2,1)S(1)} %all_gather.7.grad), channel_id=1, source_target_pairs={{0,32},{32,0},{64,96},{96,64},{128,160},{160,128},{192,224},{224,1... | collective-permute-start | bytes 2359304 | tf_op jit(solution)/shard_map/ppermute | solution.py:29
  127.0 1.4 shard_map.65
  128.9 1.4 shard_map.66
  130.4 3.8 %collective-permute-start.11 = (bf16[256,768]{1,0:T(8,128)(2,1)S(1)}, bf16[256,768]{1,0:T(8,128)(2,1)S(1)}, u32[]{:S(2)}, u32[]{:S(2)}) collective-permute-start(bf16[256,768]{1,0:T(8,128)(2,1)S(1)} %get-tuple-element.19), channel_id=1, source_target_pairs={{0,2},{1,3},{2,0},{3,1},{4,6},{5,7},{6,4},{7,5},{8,10},{9,11},{10,... | collective-permute-start | bytes 1179656 | tf_op jit(solution)/shard_map/ppermute | solution.py:29
  134.2 10.1 %collective-permute-done.11 = bf16[256,768]{1,0:T(8,128)(2,1)S(1)} collective-permute-done((bf16[256,768]{1,0:T(8,128)(2,1)S(1)}, bf16[256,768]{1,0:T(8,128)(2,1)S(1)}, u32[]{:S(2)}, u32[]{:S(2)}) %collective-permute-start.11) | collective-permute-done | bytes 393248 | tf_op jit(solution)/shard_map/ppermute | solution.py:29
  145.1 5.3 %all-to-all-start.1 = ((bf16[4,64,768]{2,1,0:T(8,128)(2,1)}), bf16[4,64,768]{2,1,0:T(8,128)(2,1)}, u32[]{:S(2)}, u32[]{:S(2)}) async-start(bf16[4,64,768]{2,1,0:T(8,128)(2,1)} %bitcast.4), calls=%async_computation.1 | async-start | bytes 786432 | tf_op jit(solution)/shard_map/all_to_all | solution.py:33
  150.4 3.1 %collective-permute-start.13 = (bf16[256,768]{1,0:T(8,128)(2,1)S(1)}, bf16[256,768]{1,0:T(8,128)(2,1)}, u32[]{:S(2)}, u32[]{:S(2)}) collective-permute-start(bf16[256,768]{1,0:T(8,128)(2,1)S(1)} %copy-done.12), channel_id=1, source_target_pairs={{0,1},{1,0},{2,3},{3,2},{4,5},{5,4},{6,7},{7,6},{8,9},{9,8},{10,11... | collective-permute-start | bytes 1179656 | tf_op jit(solution)/shard_map/ppermute | solution.py:29
  153.5 1.8 %multiply_convert_fusion.1 = bf16[64,768]{1,0:T(8,128)(2,1)} fusion(f32[128,768]{1,0:T(8,128)} %get-tuple-element.22, pred[]{:T(512)S(6)} %eq.7), kind=kLoop, calls=%fused_computation.23 | loop fusion | flops 294912 | bytes 491521 | tf_op jit(solution)/shard_map/convert_element_type | solution.py:228
  155.3 1.4 slice.63
  156.8 2.2 %collective-permute-start.6 = (bf16[32,768]{1,0:T(8,128)(2,1)}, bf16[32,768]{1,0:T(8,128)(2,1)}, u32[]{:S(2)}, u32[]{:S(2)}) collective-permute-start(bf16[32,768]{1,0:T(8,128)(2,1)} %slice.63), channel_id=1, source_target_pairs={{0,1},{1,0},{2,3},{3,2},{4,5},{5,4},{6,7},{7,6},{8,9},{9,8},{10,11... | collective-permute-start | bytes 147464 | tf_op jit(solution)/shard_map/ppermute | solution.py:29
  159.8 3.0 %collective-permute-done.6 = bf16[32,768]{1,0:T(8,128)(2,1)} collective-permute-done((bf16[32,768]{1,0:T(8,128)(2,1)}, bf16[32,768]{1,0:T(8,128)(2,1)}, u32[]{:S(2)}, u32[]{:S(2)}) %collective-permute-start.6) | collective-permute-done | bytes 49184 | tf_op jit(solution)/shard_map/ppermute | solution.py:29
  164.3 4.1 %collective-permute-start.14 = (bf16[256,768]{1,0:T(8,128)(2,1)}, bf16[256,768]{1,0:T(8,128)(2,1)S(1)}, u32[]{:S(2)}, u32[]{:S(2)}) collective-permute-start(bf16[256,768]{1,0:T(8,128)(2,1)} %collective-permute-done.13), channel_id=1, source_target_pairs={{0,32},{32,0},{64,96},{96,64},{128,160},{160,128},{192,224},{224,1... | collective-permute-start | bytes 1179656 | tf_op jit(solution)/shard_map/ppermute | solution.py:29
  169.6 5.9 %collective-permute-start.12 = (bf16[32,768]{1,0:T(8,128)(2,1)S(1)}, bf16[32,768]{1,0:T(8,128)(2,1)S(1)}, u32[]{:S(2)}, u32[]{:S(2)}) collective-permute-start(bf16[32,768]{1,0:T(8,128)(2,1)S(1)} %fusion.18), channel_id=1, source_target_pairs={{0,16},{1,17},{2,18},{3,19},{4,20},{5,21},{6,22},{7,23},{8,24},{9,... | collective-permute-start | bytes 147464 | tf_op jit(solution)/shard_map/ppermute | solution.py:29
  175.5 3.5 %multiply_convert_fusion = bf16[768,768]{1,0:T(8,128)(2,1)} fusion(bf16[512,768]{1,0:T(8,128)(2,1)S(1)} %copy-done.9, bf16[512,768]{1,0:T(8,128)(2,1)S(1)} %copy-done.7, bf16[256,768]{1,0:T(8,128)(2,1)S(1)} %collective-permute-done.14, bf16[256,768]{1,0:T(8,128)(2,1)} %collective-permute-done.13, bf16[256,768]{1,0:T(8,128)(2,1)S(1)} %bitcast.21, ...), kind=kOutput, calls=%fused_computation | convolution fusion | flops 1218576384 | bytes 4325376 | tf_op jit(solution)/shard_map/dot_general | solution.py:263
  (57 shorter events, 9.4 us)
Async XLA Ops:
  0.6 14.3 %collective-permute-start.1 = (bf16[32,768]{1,0:T(8,128)(2,1)}, bf16[32,768]{1,0:T(8,128)(2,1)S(1)}, u32[]{:S(2)}, u32[]{:S(2)}) collective-permute-start(bf16[32,768]{1,0:T(8,128)(2,1)} %param.3), channel_id=1, source_target_pairs={{0,2},{1,3},{2,0},{3,1},{4,6},{5,7},{6,4},{7,5},{8,10},{9,11},{10,... | collective-permute-start | bytes 147464 | tf_op jit(solution)/shard_map/ppermute | solution.py:29
  6.1 11.4 %collective-permute-start.2 = (bf16[32,768]{1,0:T(8,128)(2,1)}, bf16[32,768]{1,0:T(8,128)(2,1)S(1)}, u32[]{:S(2)}, u32[]{:S(2)}) collective-permute-start(bf16[32,768]{1,0:T(8,128)(2,1)} %param.3), channel_id=1, source_target_pairs={{0,18},{1,19},{2,16},{3,17},{4,22},{5,23},{6,20},{7,21},{8,26},{9,... | collective-permute-start | bytes 147464 | tf_op jit(solution)/shard_map/ppermute | solution.py:29
  17.5 1.3 copy-start
  18.8 2.9 %copy-start.14 = (bf16[32,768]{1,0:T(8,128)(2,1)S(1)}, bf16[32,768]{1,0:T(8,128)(2,1)}, u32[]{:S(2)}) copy-start(bf16[32,768]{1,0:T(8,128)(2,1)} %param.3) | copy-start | bytes 147460
  18.8 33.0 %copy-start.1 = (bf16[768,768]{1,0:T(8,128)(2,1)S(1)}, bf16[768,768]{1,0:T(8,128)(2,1)}, u32[]{:S(2)}) copy-start(bf16[768,768]{1,0:T(8,128)(2,1)} %w0.5) | copy-start | bytes 3538948
  19.4 32.3 %collective-permute-start.3 = (bf16[768,768]{1,0:T(8,128)(2,1)S(1)}, bf16[768,768]{1,0:T(8,128)(2,1)S(1)}, u32[]{:S(2)}, u32[]{:S(2)}) collective-permute-start(bf16[768,768]{1,0:T(8,128)(2,1)S(1)} %shard_map.58), channel_id=1, source_target_pairs={{0,1},{1,0},{2,3},{3,2},{4,5},{5,4},{6,7},{7,6},{8,9},{9,8},{10,11... | collective-permute-start | bytes 3538952 | tf_op jit(solution)/shard_map/ppermute | solution.py:29
  21.6 10.3 %collective-permute-start = (bf16[32,768]{1,0:T(8,128)(2,1)S(1)}, bf16[32,768]{1,0:T(8,128)(2,1)S(1)}, u32[]{:S(2)}, u32[]{:S(2)}) collective-permute-start(bf16[32,768]{1,0:T(8,128)(2,1)S(1)} %copy-done.14), channel_id=1, source_target_pairs={{0,16},{1,17},{2,18},{3,19},{4,20},{5,21},{6,22},{7,23},{8,24},{9,... | collective-permute-start | bytes 147464 | tf_op jit(solution)/shard_map/ppermute | solution.py:29
  51.7 2.0 %copy-start.2 = (bf16[512,768]{1,0:T(8,128)(2,1)}, bf16[512,768]{1,0:T(8,128)(2,1)S(1)}, u32[]{:S(2)}) copy-start(bf16[512,768]{1,0:T(8,128)(2,1)S(1)} %all_gather.6.line) | copy-start | bytes 2359300
  53.7 9.1 %collective-permute-start.4 = (bf16[512,768]{1,0:T(8,128)(2,1)S(1)}, bf16[512,768]{1,0:T(8,128)(2,1)S(1)}, u32[]{:S(2)}, u32[]{:S(2)}) collective-permute-start(bf16[512,768]{1,0:T(8,128)(2,1)S(1)} %get-tuple-element.14), channel_id=1, source_target_pairs={{0,32},{32,0},{64,96},{96,64},{128,160},{160,128},{192,224},{224,1... | collective-permute-start | bytes 2359304 | tf_op jit(solution)/shard_map/ppermute | solution.py:29
  64.4 4.3 %copy-start.10 = (bf16[64,768]{1,0:T(8,128)(2,1)S(1)}, bf16[64,768]{1,0:T(8,128)(2,1)}, u32[]{:S(2)}) copy-start(bf16[64,768]{1,0:T(8,128)(2,1)} %own.1) | copy-start | bytes 294916
  64.4 16.9 %all-to-all-start = ((bf16[4,128,768]{2,1,0:T(8,128)(2,1)}), bf16[4,128,768]{2,1,0:T(8,128)(2,1)S(1)}, u32[]{:S(2)}, u32[]{:S(2)}) async-start(bf16[4,128,768]{2,1,0:T(8,128)(2,1)} %bitcast.2), calls=%async_computation | async-start | bytes 1572864 | tf_op jit(solution)/shard_map/all_to_all | solution.py:33
  68.8 25.0 %collective-permute-start.7 = (bf16[64,768]{1,0:T(8,128)(2,1)S(1)}, bf16[64,768]{1,0:T(8,128)(2,1)S(1)}, u32[]{:S(2)}, u32[]{:S(2)}) collective-permute-start(bf16[64,768]{1,0:T(8,128)(2,1)S(1)} %copy-done.10), channel_id=1, source_target_pairs={{0,64},{32,96},{64,0},{96,32},{128,192},{160,224},{192,128},{224,1... | collective-permute-start | bytes 294920 | tf_op jit(solution)/shard_map/ppermute | solution.py:29
  81.4 16.0 %copy-start.3 = (bf16[512,768]{1,0:T(8,128)(2,1)S(1)}, bf16[512,768]{1,0:T(8,128)(2,1)}, u32[]{:S(2)}) copy-start(bf16[512,768]{1,0:T(8,128)(2,1)} %copy-done.2) | copy-start | bytes 2359300
  82.0 18.8 %collective-permute-start.5 = (bf16[128,768]{1,0:T(8,128)(2,1)S(1)}, bf16[128,768]{1,0:T(8,128)(2,1)S(1)}, u32[]{:S(2)}, u32[]{:S(2)}) collective-permute-start(bf16[128,768]{1,0:T(8,128)(2,1)S(1)} %shard_map.61._), channel_id=1, source_target_pairs={{0,64},{32,96},{64,0},{96,32},{128,192},{160,224},{192,128},{224,1... | collective-permute-start | bytes 589832 | tf_op jit(solution)/shard_map/ppermute | solution.py:29
  94.3 5.9 %collective-permute-start.8 = (bf16[64,768]{1,0:T(8,128)(2,1)S(1)}, bf16[64,768]{1,0:T(8,128)(2,1)S(1)}, u32[]{:S(2)}, u32[]{:S(2)}) collective-permute-start(bf16[64,768]{1,0:T(8,128)(2,1)S(1)} %get-tuple-element.16), channel_id=1, source_target_pairs={{0,1},{1,0},{2,3},{3,2},{4,5},{5,4},{6,7},{7,6},{8,9},{9,8},{10,11... | collective-permute-start | bytes 294920 | tf_op jit(solution)/shard_map/ppermute | solution.py:29
  98.0 30.4 %copy-start.6 = (bf16[512,768]{1,0:T(8,128)(2,1)}, bf16[512,768]{1,0:T(8,128)(2,1)S(1)}, u32[]{:S(2)}) copy-start(bf16[512,768]{1,0:T(8,128)(2,1)S(1)} %shard_map.64) | copy-start | bytes 2359300
  98.0 29.0 %collective-permute-start.9 = (bf16[512,768]{1,0:T(8,128)(2,1)S(1)}, bf16[512,768]{1,0:T(8,128)(2,1)S(1)}, u32[]{:S(2)}, u32[]{:S(2)}) collective-permute-start(bf16[512,768]{1,0:T(8,128)(2,1)S(1)} %shard_map.64), channel_id=1, source_target_pairs={{0,1},{1,0},{2,3},{3,2},{4,5},{5,4},{6,7},{7,6},{8,9},{9,8},{10,11... | collective-permute-start | bytes 2359304 | tf_op jit(solution)/shard_map/ppermute | solution.py:29
  121.5 7.4 %collective-permute-start.10 = (bf16[512,768]{1,0:T(8,128)(2,1)S(1)}, bf16[512,768]{1,0:T(8,128)(2,1)S(1)}, u32[]{:S(2)}, u32[]{:S(2)}) collective-permute-start(bf16[512,768]{1,0:T(8,128)(2,1)S(1)} %all_gather.7.grad), channel_id=1, source_target_pairs={{0,32},{32,0},{64,96},{96,64},{128,160},{160,128},{192,224},{224,1... | collective-permute-start | bytes 2359304 | tf_op jit(solution)/shard_map/ppermute | solution.py:29
  127.0 1.4 copy-start.8
  128.4 1.9 %copy-start.11 = (bf16[256,768]{1,0:T(8,128)(2,1)}, bf16[256,768]{1,0:T(8,128)(2,1)S(1)}, u32[]{:S(2)}) copy-start(bf16[256,768]{1,0:T(8,128)(2,1)S(1)} %get-tuple-element.20) | copy-start | bytes 1179652
  128.9 1.5 copy-start.4
  130.4 20.0 %copy-start.12 = (bf16[256,768]{1,0:T(8,128)(2,1)S(1)}, bf16[256,768]{1,0:T(8,128)(2,1)}, u32[]{:S(2)}) copy-start(bf16[256,768]{1,0:T(8,128)(2,1)} %copy-done.11) | copy-start | bytes 1179652
  130.4 13.8 %collective-permute-start.11 = (bf16[256,768]{1,0:T(8,128)(2,1)S(1)}, bf16[256,768]{1,0:T(8,128)(2,1)S(1)}, u32[]{:S(2)}, u32[]{:S(2)}) collective-permute-start(bf16[256,768]{1,0:T(8,128)(2,1)S(1)} %get-tuple-element.19), channel_id=1, source_target_pairs={{0,2},{1,3},{2,0},{3,1},{4,6},{5,7},{6,4},{7,5},{8,10},{9,11},{10,... | collective-permute-start | bytes 1179656 | tf_op jit(solution)/shard_map/ppermute | solution.py:29
  145.1 19.2 %copy-start.5 = (bf16[512,768]{1,0:T(8,128)(2,1)S(1)}, bf16[512,768]{1,0:T(8,128)(2,1)}, u32[]{:S(2)}) copy-start(bf16[512,768]{1,0:T(8,128)(2,1)} %copy-done.4) | copy-start | bytes 2359300
  145.1 23.3 %all-to-all-start.1 = ((bf16[4,64,768]{2,1,0:T(8,128)(2,1)}), bf16[4,64,768]{2,1,0:T(8,128)(2,1)}, u32[]{:S(2)}, u32[]{:S(2)}) async-start(bf16[4,64,768]{2,1,0:T(8,128)(2,1)} %bitcast.4), calls=%async_computation.1 | async-start | bytes 786432 | tf_op jit(solution)/shard_map/all_to_all | solution.py:33
  150.4 13.9 %collective-permute-start.13 = (bf16[256,768]{1,0:T(8,128)(2,1)S(1)}, bf16[256,768]{1,0:T(8,128)(2,1)}, u32[]{:S(2)}, u32[]{:S(2)}) collective-permute-start(bf16[256,768]{1,0:T(8,128)(2,1)S(1)} %copy-done.12), channel_id=1, source_target_pairs={{0,1},{1,0},{2,3},{3,2},{4,5},{5,4},{6,7},{7,6},{8,9},{9,8},{10,11... | collective-permute-start | bytes 1179656 | tf_op jit(solution)/shard_map/ppermute | solution.py:29
  153.5 22.0 %copy-start.7 = (bf16[512,768]{1,0:T(8,128)(2,1)S(1)}, bf16[512,768]{1,0:T(8,128)(2,1)}, u32[]{:S(2)}) copy-start(bf16[512,768]{1,0:T(8,128)(2,1)} %copy-done.6) | copy-start | bytes 2359300
  153.5 22.0 %copy-start.9 = (bf16[512,768]{1,0:T(8,128)(2,1)S(1)}, bf16[512,768]{1,0:T(8,128)(2,1)}, u32[]{:S(2)}) copy-start(bf16[512,768]{1,0:T(8,128)(2,1)} %copy-done.8) | copy-start | bytes 2359300
  156.8 6.0 %collective-permute-start.6 = (bf16[32,768]{1,0:T(8,128)(2,1)}, bf16[32,768]{1,0:T(8,128)(2,1)}, u32[]{:S(2)}, u32[]{:S(2)}) collective-permute-start(bf16[32,768]{1,0:T(8,128)(2,1)} %slice.63), channel_id=1, source_target_pairs={{0,1},{1,0},{2,3},{3,2},{4,5},{5,4},{6,7},{7,6},{8,9},{9,8},{10,11... | collective-permute-start | bytes 147464 | tf_op jit(solution)/shard_map/ppermute | solution.py:29
  159.7 15.8 %copy-start.13 = (bf16[8,1,32,768]{3,2,1,0:T(8,128)(2,1)S(1)}, bf16[8,1,32,768]{3,2,1,0:T(8,128)(2,1)}, u32[]{:S(2)}) copy-start(bf16[8,1,32,768]{3,2,1,0:T(8,128)(2,1)} %slice.71) | copy-start | bytes 1179652
  164.3 11.2 %collective-permute-start.14 = (bf16[256,768]{1,0:T(8,128)(2,1)}, bf16[256,768]{1,0:T(8,128)(2,1)S(1)}, u32[]{:S(2)}, u32[]{:S(2)}) collective-permute-start(bf16[256,768]{1,0:T(8,128)(2,1)} %collective-permute-done.13), channel_id=1, source_target_pairs={{0,32},{32,0},{64,96},{96,64},{128,160},{160,128},{192,224},{224,1... | collective-permute-start | bytes 1179656 | tf_op jit(solution)/shard_map/ppermute | solution.py:29
  169.6 9.4 %collective-permute-start.12 = (bf16[32,768]{1,0:T(8,128)(2,1)S(1)}, bf16[32,768]{1,0:T(8,128)(2,1)S(1)}, u32[]{:S(2)}, u32[]{:S(2)}) collective-permute-start(bf16[32,768]{1,0:T(8,128)(2,1)S(1)} %fusion.18), channel_id=1, source_target_pairs={{0,16},{1,17},{2,18},{3,19},{4,20},{5,21},{6,22},{7,23},{8,24},{9,... | collective-permute-start | bytes 147464 | tf_op jit(solution)/shard_map/ppermute | solution.py:29
